TPU v7x, 32 devices: a whole 2x2x4 slice. The times are simulated.
32 devices in a mesh: row: 8 (over y, x, core), col: 4 (over z).
Axes of the slice: x: 2, y: 2, z: 4, core: 2. Of those that a mesh axis runs over, the one named last changes fastest.
Arguments:
- hidden: bfloat16 [1792, 8192], P('col', 'row'), may hold values from -6 to 6
- down_weight: bfloat16 [8192, 4096], P('row', 'col'), may hold values from -0.0625 to 0.0625
- tokens: bfloat16 [1792, 4096], P(None, 'col'), may hold values from -6 to 6
- layer_scale: bfloat16 [4096], P('col'), may hold values from 0.25 to 1
- merge_weight: bfloat16 [4, 4096, 4096], P(None, 'col', 'row'), may hold values from -0.046875 to 0.046875
- text_embeds: bfloat16 [2048, 4096], P('col', 'row'), may hold values from -6 to 6
- positions: int32 [448], replicated, may hold values from 0 to 2047, as said below
Outputs:
- prompt_states: bfloat16 [2048, 4096], P('col', 'row')
Inputs may be any that keep to these rules, and one draw needn't show every extreme that they name: All distinct; the merged rows of each of 28 pictures occupy consecutive positions in their own order, the pictures appear in the prompt in any order, and position 0 holds an image row.
All inputs are finite; a program needn't handle non-finite values.
Results may differ from a plain program's by a relative error of at most 0.0034.
Values may be sent and summed in bfloat16 or wider, within the bound.
No kernel may reach another device: no remote copies, remote signals or barrier semaphores. Data moves between devices by JAX's collectives and lax.ppermute only.
A program may use at most 64 MiB of HBM per device.

v0:
```python
import jax
import jax.numpy as jnp
from jax import lax
from jax.sharding import PartitionSpec as P


def per_device(hidden, down_weight, tokens, layer_scale, merge_weight, text_embeds, positions):
    gathered = lax.all_gather(hidden, "col", axis=0, tiled=True)
    all_rows = gathered.shape[0]
    scale_row = layer_scale.astype(jnp.float32)[None, :]
    partial_term = jnp.dot(gathered, down_weight, preferred_element_type=jnp.float32)
    row_total = lax.psum(partial_term, "row")
    vision = (tokens.astype(jnp.float32) + scale_row * row_total).astype(jnp.bfloat16)
    width_local = vision.shape[1]
    merged = vision.reshape(all_rows // 4, 4 * width_local)
    merge_flat = merge_weight.reshape(4 * width_local, merge_weight.shape[2])
    prompt_count = text_embeds.shape[0]
    prompt_first = lax.axis_index("col") * prompt_count
    prompt_index = prompt_first + jnp.arange(prompt_count, dtype=jnp.int32)
    landed = jnp.any(positions[None, :] == prompt_index[:, None], axis=1)
    portion_proj = lax.psum_scatter(
        jnp.dot(merged, merge_flat, preferred_element_type=jnp.float32),
        "col",
        scatter_dimension=0,
        tiled=True,
    )
    projected = portion_proj.astype(jnp.bfloat16)
    every_proj = lax.all_gather(projected, "col", axis=0, tiled=True)
    chooser = (positions[None, :] == prompt_index[:, None]).astype(jnp.bfloat16)
    image_rows = jnp.dot(chooser, every_proj, preferred_element_type=jnp.float32).astype(
        jnp.bfloat16
    )
    return jnp.where(landed[:, None], image_rows, text_embeds)


def solution(mesh):
    in_specs = (
        P("col", "row"),
        P("row", "col"),
        P(None, "col"),
        P("col"),
        P(None, "col", "row"),
        P("col", "row"),
        P(),
    )
    out_specs = P("col", "row")
    return jax.shard_map(
        per_device, mesh=mesh, in_specs=in_specs, out_specs=out_specs, check_vma=False
    )
```

profile of v0, /device:TPU:0, one launch (start us, length us, event | category | flops | bytes accessed | tf_op | source)
XLA Modules:
  0.0 276.8 jit_solution(16689612369844608021)
XLA Ops:
  6.5 0.0 copy-start
  6.5 0.0 all-gather.2.cloned.1.call-start
  6.5 0.7 all-gather.2.cloned.1.call-update
  7.3 0.0 all-reduce.2.cloned.1.call-start
  7.3 76.5 %all-gather.2.cloned.1.call-done = bf16[1792,1024]{1,0:T(8,128)(2,1)} async-done(((bf16[448,1024]{1,0:T(8,128)(2,1)}), bf16[1792,1024]{1,0:T(8,128)(2,1)}) %all-gather.2.cloned.1.call-update) | async-done | bytes 3670032 | tf_op jit(solution)/shard_map/all_gather | solution.py:8
  83.8 0.0 copy-done
  83.8 8.1 %fusion.4 = f32[1792,1024]{1,0:T(8,128)} fusion(bf16[1792,1024]{1,0:T(8,128)(2,1)} %all-gather.2.cloned.1.call-done, bf16[1024,1024]{1,0:T(8,128)(2,1)S(1)} %copy-done), kind=kOutput, calls=%fused_computation.8 | convolution fusion | flops 3758096384 | bytes 13107200 | tf_op jit(solution)/shard_map/dot_general | solution.py:11
  91.9 0.0 copy-start.1
  91.9 0.0 all-reduce.2.cloned.1.call-update
  91.9 0.0 reduce-scatter.2.cloned.1.call-start
  92.0 0.6 copy-done.1
  92.6 113.9 %all-reduce.2.cloned.1.call-done = f32[1792,1024]{1,0:T(8,128)} async-done(((f32[1792,1024]{1,0:T(8,128)}), f32[1792,1024]{1,0:T(8,128)}) %all-reduce.2.cloned.1.call-update) | async-done | bytes 7340048 | tf_op jit(solution)/shard_map/psum | solution.py:12
  206.4 7.4 %add_convert_fusion = bf16[1792,1024]{1,0:T(8,128)(2,1)} fusion(f32[1792,1024]{1,0:T(8,128)} %all-reduce.2.cloned.1.call-done, bf16[1792,1024]{1,0:T(8,128)(2,1)} %param.9, f32[1024]{0:T(1024)S(1)} %convert_element_type.17), kind=kLoop, calls=%fused_computation | loop fusion | flops 7340032 | bytes 14684160 | tf_op jit(solution)/shard_map/convert_element_type | solution.py:13
  213.9 6.9 %reshape.13 = bf16[448,4096]{1,0:T(8,128)(2,1)} reshape(bf16[1792,1024]{1,0:T(8,128)(2,1)} %add_convert_fusion) | data formatting | bytes 7340032 | tf_op jit(solution)/shard_map/reshape | solution.py:15
  220.8 0.0 copy-start.2
  220.8 0.0 copy-start.3
  220.8 6.3 %fusion.5 = f32[448,512]{1,0:T(8,128)} fusion(bf16[448,4096]{1,0:T(8,128)(2,1)} %reshape.13, bf16[4096,512]{1,0:T(8,128)(2,1)} %bitcast.6), kind=kOutput, calls=%fused_computation.9 | convolution fusion | flops 1879048192 | bytes 8781824 | tf_op jit(solution)/shard_map/dot_general | solution.py:22
  227.1 0.0 reduce-scatter.2.cloned.1.call-update
  227.1 0.0 copy-done.2
  227.1 0.2 compare_reduce_fusion
  227.3 25.1 %reduce-scatter.2.cloned.1.call-done = f32[112,512]{1,0:T(8,128)} async-done(((f32[448,512]{1,0:T(8,128)}), f32[112,512]{1,0:T(8,128)}) %reduce-scatter.2.cloned.1.call-update) | async-done | bytes 229392 | tf_op jit(solution)/shard_map/reduce_scatter | solution.py:21
  252.5 1.0 convert_element_type.19
  253.4 15.5 %all_gather.7 = bf16[448,512]{1,0:T(8,128)(2,1)S(1)} all-gather(bf16[112,512]{1,0:T(8,128)(2,1)S(1)} %convert_element_type.19), channel_id=1, replica_groups=mesh['row'=8,'col'=4] {'col'}, dimensions={0}, use_global_device_ids=true | all-gather | bytes 573440 | tf_op jit(solution)/shard_map/all_gather | solution.py:28
  268.9 0.0 copy-done.3
  268.9 1.4 fusion
  (2 shorter events, 0.0 us)
Async XLA Ops:
  6.5 77.2 %copy-start = (bf16[1024,1024]{1,0:T(8,128)(2,1)S(1)}, bf16[1024,1024]{1,0:T(8,128)(2,1)}, u32[]{:S(2)}) copy-start(bf16[1024,1024]{1,0:T(8,128)(2,1)} %param.8) | copy-start | bytes 6291460
  6.5 77.2 %all-gather.2.cloned.1.call-start = ((), (), s32[]{:S(2)}) async-start(), calls=%async_computation.1 | async-start | bytes 4587520 | tf_op jit(solution)/shard_map/all_gather | solution.py:8
  7.3 199.2 %all-reduce.2.cloned.1.call-start = ((), (), s32[]{:S(2)}) async-start(), calls=%async_computation.2 | async-start | bytes 14680064 | tf_op jit(solution)/shard_map/psum | solution.py:12
  91.9 0.7 copy-start.1
  91.9 160.6 %reduce-scatter.2.cloned.1.call-start = ((), (), s32[]{:S(2)}) async-start(), calls=%async_computation.3 | async-start | bytes 1146880 | tf_op jit(solution)/shard_map/reduce_scatter | solution.py:21
  220.8 6.4 %copy-start.2 = (s32[448]{0:T(512)S(1)}, s32[448]{0:T(512)}, u32[]{:S(2)}) copy-start(s32[448]{0:T(512)} %param.13) | copy-start | bytes 5380
  220.8 48.2 %copy-start.3 = (bf16[512,512]{1,0:T(8,128)(2,1)S(1)}, bf16[512,512]{1,0:T(8,128)(2,1)}, u32[]{:S(2)}) copy-start(bf16[512,512]{1,0:T(8,128)(2,1)} %param.12) | copy-start | bytes 1572868
Sparse Core Ops, SparseCore 0:
  8.9 74.7 all-gather.1
  92.0 114.3 all-reduce.1
  227.2 25.2 reduce-scatter.1
where the time goes:
time: 277 us
  waiting for transfers between devices  216 us (78%)
  matrix products  15.8 us (6%)
  blocking collectives  15.5 us (6%)
  between operations  13.1 us (5%)
  other arithmetic  8.59 us (3%)
  local copies, waits for them, and re-layouts  7.51 us (3%)
    psum x1, waiting for transfers between devices, per_device(): row_total = lax.psum(partial_term, 'row')  114 us
    all_gather x1, waiting for transfers between devices, per_device(): gathered = lax.all_gather(hidden, 'col', axis=0, tiled=True)  76.5 us
    reduce_scatter x1, waiting for transfers between devices, per_device(): lax.psum_scatter(jnp.dot(merged, merge_flat, preferred_element_type=jnp.f...  25.1 us
    all_gather x1, blocking collectives, per_device(): every_proj = lax.all_gather(projected, 'col', axis=0, tiled=True)  15.5 us
    dot_general x1, matrix products, per_device(): jnp.dot(gathered, down_weight, preferred_element_type=jnp.float32)  8.11 us
    convert_element_type x1, other arithmetic, per_device(): (tokens.astype(jnp.float32) + scale_row * row_total).astype(jnp.bfloat16)  7.43 us
    reshape x1, local copies, waits for them, and re-layouts, per_device(): merged = vision.reshape(all_rows // 4, 4 * width_local)  6.89 us
    dot_general x1, matrix products, per_device(): jnp.dot(merged, merge_flat, preferred_element_type=jnp.float32)  6.32 us
  transfers between devices with their start and end apart: 3, of which 3 were waited for; matrix products, arithmetic and copies ran while one was open for 0% of the time, Pallas kernels for 0%

commit v1 on v0

v1 whole, which is shorter than its diff:
```python
import functools

import jax
import jax.numpy as jnp
from jax import lax
from jax.experimental import pallas as pl
from jax.experimental.pallas import tpu as pltpu
from jax.sharding import PartitionSpec as P

BF = jnp.bfloat16
F32 = jnp.float32
ANY = pl.BlockSpec(memory_space=pl.ANY)
LITTLE = pl.CostEstimate(flops=1, bytes_accessed=1, transcendentals=0)
ROOM = 8 * 1024 * 1024


def _dot(a, b):
    return jnp.dot(a, b, preferred_element_type=F32)


def _down_kernel(half, blocks, info, *refs):
    w, give, keep = refs[blocks], refs[-2], refs[-1]
    mine = info[0]
    block = refs[0][...] if blocks == 1 else jnp.where(info[1] > 0, refs[0][...], refs[1][...])
    give[...] = _dot(block, w[:, pl.ds(pl.multiple_of((1 - mine) * half, half), half)]).astype(BF)
    keep[...] = _dot(block, w[:, pl.ds(pl.multiple_of(mine * half, half), half)])


def _add_kernel(mine, came, *refs):
    refs[-1][...] = (mine[...].astype(F32) + came[...].astype(F32)).astype(refs[-1].dtype)


def _sum_kernel(mine, came, *refs):
    total = mine[...] + came[...].astype(F32)
    refs[-2][...] = total.astype(BF)
    refs[-1][...] = total


def _vision_kernel(mine, came, tokens, scale, *refs):
    out, spread = refs[-2], refs[-1]
    for j in range(spread.shape[0]):
        lanes = pl.ds(j * 128, 128)
        total = mine[:, lanes].astype(F32) + came[:, lanes].astype(F32)
        vision = tokens[:, lanes].astype(F32) + scale[:, lanes].astype(F32) * total
        spread[j] = vision.astype(BF).astype(F32)
        for k in range(4):
            out[k, :, lanes] = spread[j, pl.ds(k, out.shape[1], stride=4), :].astype(BF)


def _merge_kernel(half, info, own, other, weight, *refs):
    give, total, held, sems = refs[-4:]
    mine = info[0]
    copies = [pltpu.make_async_copy(weight.at[k], held.at[k], sems.at[k]) for k in range(4)]
    for copy in copies:
        copy.start()
    here = pl.ds(pl.multiple_of(mine * half, half), half)
    there = pl.ds(pl.multiple_of((1 - mine) * half, half), half)
    part = None
    for k in range(4):
        copies[k].wait()
        more = _dot(own[k], held[k, here, :]) + _dot(other[k], held[k, there, :])
        part = more if part is None else part + more
    total[...] = part
    give[...] = part.astype(BF)


HBM = pl.BlockSpec(memory_space=pltpu.HBM)
VMEM = pl.BlockSpec(memory_space=pltpu.VMEM)
SMEM = pl.BlockSpec(memory_space=pltpu.SMEM)


def build(rows, cols):
    def swap(x, axis, bit):
        size = rows if axis == "row" else cols
        return lax.ppermute(x, axis, [(i, i ^ bit) for i in range(size)])

    def per_device(hidden, down_weight, tokens, layer_scale, merge_weight, text_embeds, positions):
        patches, depth = hidden.shape
        width = down_weight.shape[1]
        half = width // 2
        merged_rows = patches // 4
        dec = merge_weight.shape[2]
        row, col = lax.axis_index("row"), lax.axis_index("col")
        mine = row % 2
        inner = (col == 1) | (col == 2)
        info = jnp.stack([mine, inner.astype(jnp.int32)])
        scale = lax.dynamic_slice(layer_scale, (mine * half,), (half,))[None, :]
        row_bits = [1 << i for i in range(1, rows.bit_length() - 1)]
        after = []

        def down(*blocks):
            count = blocks[0].shape[0]
            give, keep = pl.pallas_call(
                functools.partial(_down_kernel, half, len(blocks)),
                out_shape=(
                    jax.ShapeDtypeStruct((count, half), BF),
                    jax.ShapeDtypeStruct((count, half), F32),
                ),
                in_specs=[SMEM] + [VMEM] * (len(blocks) + 1) + [ANY] * len(after),
                out_specs=(VMEM, VMEM),
                cost_estimate=LITTLE,
                compiler_params=pltpu.CompilerParams(vmem_limit_bytes=ROOM),
                name="down",
            )(info, *blocks, down_weight, *after)
            after[:] = [give]
            return give, keep

        def add(total, came):
            give = pl.pallas_call(
                _add_kernel,
                out_shape=jax.ShapeDtypeStruct(total.shape, BF),
                in_specs=[VMEM, VMEM] + [ANY] * len(after),
                out_specs=VMEM,
                cost_estimate=LITTLE,
                compiler_params=pltpu.CompilerParams(vmem_limit_bytes=ROOM),
                name="add",
            )(total, came, *after)
            after[:] = [give]
            return give

        def add_both(total, came):
            give, total = pl.pallas_call(
                _sum_kernel,
                out_shape=(
                    jax.ShapeDtypeStruct(total.shape, BF),
                    jax.ShapeDtypeStruct(total.shape, F32),
                ),
                in_specs=[VMEM, VMEM] + [ANY] * len(after),
                out_specs=(VMEM, VMEM),
                cost_estimate=LITTLE,
                compiler_params=pltpu.CompilerParams(vmem_limit_bytes=ROOM),
                name="add_both",
            )(total, came, *after)
            after[:] = [give]
            return give, total

        def see(total, came, first):
            count = total.shape[0]
            residual = lax.dynamic_slice(tokens, (first, mine * half), (count, half))
            out = pl.pallas_call(
                _vision_kernel,
                out_shape=jax.ShapeDtypeStruct((4, count // 4, half), BF),
                in_specs=[VMEM] * 4 + [ANY] * len(after),
                out_specs=VMEM,
                scratch_shapes=[pltpu.VMEM((half // 128, count, 128), F32)],
                cost_estimate=LITTLE,
                compiler_params=pltpu.CompilerParams(vmem_limit_bytes=ROOM),
                name="vision",
            )(total, came, residual, scale, *after)
            after[:] = [out]
            return out

        def merge(own, other):
            count = own.shape[1]
            give, total = pl.pallas_call(
                functools.partial(_merge_kernel, half),
                out_shape=(
                    jax.ShapeDtypeStruct((count, dec), BF),
                    jax.ShapeDtypeStruct((count, dec), F32),
                ),
                in_specs=[SMEM, VMEM, VMEM, HBM] + [ANY] * len(after),
                out_specs=(VMEM, VMEM),
                scratch_shapes=[pltpu.VMEM(merge_weight.shape, BF), pltpu.SemaphoreType.DMA((4,))],
                cost_estimate=LITTLE,
                compiler_params=pltpu.CompilerParams(vmem_limit_bytes=ROOM),
                name="merge",
            )(info, own, other, merge_weight, *after)
            after[:] = [give]
            return give, total

        def place(projected, where_to):
            prompt_count = text_embeds.shape[0]
            prompt_index = col * prompt_count + jnp.arange(prompt_count, dtype=jnp.int32)
            hit = where_to[None, :] == prompt_index[:, None]
            image_rows = _dot(hit.astype(BF), projected).astype(BF)
            return jnp.where(jnp.any(hit, axis=1)[:, None], image_rows, text_embeds)

        if cols != 4:
            parts = jnp.zeros((cols * merged_rows, dec), F32)
            for step in range(cols):
                block = hidden if step == 0 else swap(hidden, "col", step)
                owner = jnp.bitwise_xor(col, step)
                give, total = down(block)
                came = swap(give, "row", 1)
                for bit in row_bits:
                    total = add(total, came)
                    came = swap(total, "row", bit)
                own = see(total, came, owner * patches)
                _, part = merge(own, swap(own, "row", 1))
                parts = lax.dynamic_update_slice(parts, part, (owner * merged_rows, 0))
            return place(lax.psum(parts, "col").astype(BF), positions)

        low = col < 2
        between, outward = [(1, 2), (2, 1)], [(1, 0), (2, 3)]
        near, far = jnp.where(low, 2, 1), jnp.where(low, 3, 0)
        bit_x, bit_y = (row_bits + row_bits)[:2] if row_bits else (1, 1)

        hop_a = swap(hidden, "col", 1)
        hop_b = lax.ppermute(hidden, "col", between)
        hop_c = lax.ppermute(hop_b, "col", outward)
        hop_d = lax.ppermute(hop_a, "col", between)
        rest = patches - patches // 4 // 64 * 64 - 64
        hop_e = [lax.ppermute(hop_d[:rest], "col", outward), lax.ppermute(hop_d[rest:], "col", outward)]

        def x(give):
            return swap(give, "row", bit_x)

        def y(give):
            return swap(give, "row", bit_y)

        def core(give):
            return swap(give, "row", 1)

        def pairs(give):
            return swap(give, "col", 1)

        def halves(give):
            return swap(give, "col", 2)

        even = col % 2 == 0

        def ordered(a, b):
            return jnp.concatenate([jnp.where(even, a, b), jnp.where(even, b, a)], axis=0)

        g0, k0 = down(hidden)
        c0 = core(g0)
        a0 = add(k0, c0)
        x0 = x(a0)
        g1, k1 = down(hop_a)
        c1 = core(g1)
        b0 = add(a0, x0)
        y0 = y(b0)
        a1 = add(k1, c1)
        x1 = x(a1)
        g2, k2 = down(hop_b, hop_c)
        c2 = core(g2)
        b1 = add(a1, x1)
        y1 = y(b1)
        v0 = see(b0, y0, col * patches)
        o0 = core(v0)
        a2 = add(k2, c2)
        x2 = x(a2)
        s0, p0 = merge(v0, o0)
        v1 = see(b1, y1, (col ^ 1) * patches)
        o1 = core(v1)
        g3, k3 = down(hop_d[:rest], hop_e[0])
        c3 = core(g3)
        b2 = add(a2, x2)
        y2 = y(b2)
        a3 = add(k3, c3)
        x3 = x(a3)
        s1, p1 = merge(v1, o1)
        z01 = pairs(ordered(s0, s1))
        g4, k4 = down(hop_d[rest:], hop_e[1])
        c4 = core(g4)
        v2 = see(b2, y2, near * patches)
        o2 = core(v2)
        b3 = add(a3, x3)
        y3 = y(b3)
        a4 = add(k4, c4)
        x4 = x(a4)
        s2, p2 = merge(v2, o2)
        z2 = pairs(s2)
        b4 = add(a4, x4)
        y4 = y(b4)
        give, p01 = add_both(ordered(p0, p1), z01)
        far01 = halves(give)
        v3 = see(b3, y3, far * patches)
        o3 = core(v3)
        give, p2 = add_both(p2, z2)
        far2 = halves(give)
        v4 = see(b4, y4, far * patches + rest)
        o4 = core(v4)
        s3, p3 = merge(v3, o3)
        z3 = pairs(s3)
        s4, p4 = merge(v4, o4)
        z4 = pairs(s4)
        give, p3 = add_both(p3, z3)
        far3 = halves(give)
        give, p4 = add_both(p4, z4)
        far4 = halves(give)
        pair, far_pair, far_p2 = p01, far01, far2
        p3 = jnp.concatenate([p3, p4], axis=0)
        far_p3 = jnp.concatenate([far3, far4], axis=0)

        far_pair, far_p2, far_p3 = far_pair.astype(F32), far_p2.astype(F32), far_p3.astype(F32)
        first, second = pair[:merged_rows], pair[merged_rows:]
        f_first, f_second = far_pair[:merged_rows], far_pair[merged_rows:]
        own_inner = jnp.where(low, second, first) + far_p2
        own_outer = jnp.where(low, first, second) + far_p3
        away_inner = p2 + jnp.where(low, f_first, f_second)
        away_outer = p3 + jnp.where(low, f_second, f_first)
        projected = jnp.concatenate([own_inner, own_outer, away_inner, away_outer], axis=0).astype(BF)
        at = [positions[i * merged_rows : (i + 1) * merged_rows] for i in range(4)]
        where_to = jnp.concatenate(
            [
                jnp.where(low, at[1], at[2]),
                jnp.where(low, at[0], at[3]),
                jnp.where(low, at[2], at[1]),
                jnp.where(low, at[3], at[0]),
            ]
        )
        return place(projected, where_to)

    return per_device


def solution(mesh):
    in_specs = (
        P("col", "row"),
        P("row", "col"),
        P(None, "col"),
        P("col"),
        P(None, "col", "row"),
        P("col", "row"),
        P(),
    )
    out_specs = P("col", "row")
    return jax.shard_map(
        build(mesh.shape["row"], mesh.shape["col"]),
        mesh=mesh,
        in_specs=in_specs,
        out_specs=out_specs,
        check_vma=False,
    )
```

time: 277 us -> 134 us (0.48)
  waiting for transfers between devices: 216 us -> 48.2 us
  starting transfers between devices: 0.08 us -> 39.8 us
  Pallas kernels: 0 us -> 27.3 us
  blocking collectives: 15.5 us -> 0 us
  matrix products: 15.8 us -> 1.39 us
  between operations: 13.1 us -> 0.53 us
  local copies, waits for them, and re-layouts: 7.51 us -> 15.4 us
  other arithmetic: 8.59 us -> 0.72 us
    psum x1 -> x0, waiting for transfers between devices: 114 us -> none  [per_device(): row_total = lax.psum(partial_term, 'row')]
    all_gather x1 -> x0, waiting for transfers between devices: 76.5 us -> none  [per_device(): gathered = lax.all_gather(hidden, 'col', axis=0, tiled=True)]
    ppermute x0 -> x34, waiting for transfers between devices: none -> 48.2 us  [the longest x29 43.3 us: swap(): return lax.ppermute(x, axis, [(i, i ^ bit) for i in range(size)])]
    ppermute x0 -> x34, starting transfers between devices: none -> 39.8 us  [the longest x29 32.4 us: swap(): return lax.ppermute(x, axis, [(i, i ^ bit) for i in range(size)])]
    pallas_call x0 -> x29, Pallas kernels: none -> 27.3 us  [the longest x5 9.95 us: down(): pl.pallas_call(functools.partial(_down_kernel, half, len(blocks)), out_sh...]
    reduce_scatter x1 -> x0, waiting for transfers between devices: 25.1 us -> none  [per_device(): lax.psum_scatter(jnp.dot(merged, merge_flat, preferred_element_type=jnp.f...]
    all_gather x1 -> x0, blocking collectives: 15.5 us -> none  [per_device(): every_proj = lax.all_gather(projected, 'col', axis=0, tiled=True)]
    dot_general x3 -> x1, matrix products: 15.8 us -> 1.39 us  [_dot(): return jnp.dot(a, b, preferred_element_type=F32)]
  transfers between devices with their start and end apart: 3 -> 34, of which waited for: 3 -> 13; matrix products, arithmetic and copies ran while one was open for 0% -> 5% of each run, Pallas kernels for 0% -> 20%
where the time goes in v1:
time: 134 us; the launch traced here: 133 us
  waiting for transfers between devices  48.2 us (36%)
  starting transfers between devices  39.8 us (30%)
  Pallas kernels  27.3 us (20%)
  local copies, waits for them, and re-layouts  15.4 us (11%)
  matrix products  1.39 us (1%)
    ppermute x29, waiting for transfers between devices, swap(): return lax.ppermute(x, axis, [(i, i ^ bit) for i in range(size)])  43.3 us
    ppermute x29, starting transfers between devices, swap(): return lax.ppermute(x, axis, [(i, i ^ bit) for i in range(size)])  32.4 us
    pallas_call x5, Pallas kernels, down(): pl.pallas_call(functools.partial(_down_kernel, half, len(blocks)), out_sh...  9.95 us
    pallas_call x5, Pallas kernels, merge(): pl.pallas_call(functools.partial(_merge_kernel, half), out_shape=(jax.Sha...  9.23 us
    unnamed x36, local copies, waits for them, and re-layouts  9.22 us
    ppermute x1, waiting for transfers between devices, per_device(): hop_c = lax.ppermute(hop_b, 'col', outward)  4.82 us
    pallas_call x5, Pallas kernels, see(): pl.pallas_call(_vision_kernel, out_shape=jax.ShapeDtypeStruct((4, count /...  4.08 us
    pallas_call x10, Pallas kernels, add(): pl.pallas_call(_add_kernel, out_shape=jax.ShapeDtypeStruct(total.shape, B...  3.97 us
  transfers between devices with their start and end apart: 34, of which 13 were waited for; matrix products, arithmetic and copies ran while one was open for 5% of the time, Pallas kernels for 20%

profile of v1, /device:TPU:0, one launch (start us, length us, event | category | flops | bytes accessed | tf_op | source)
XLA Modules:
  0.0 133.4 jit_solution(15258584394613692746)
XLA Ops:
  0.0 1.6 %collective-permute-start.6 = (bf16[448,1024]{1,0:T(8,128)(2,1)}, bf16[448,1024]{1,0:T(8,128)(2,1)}, u32[]{:S(2)}, u32[]{:S(2)}) collective-permute-start(bf16[448,1024]{1,0:T(8,128)(2,1)} %refs_0_.1), channel_id=1, source_target_pairs={{1,2},{2,1},{5,6},{6,5},{9,10},{10,9},{13,14},{14,13},{17,18},{18,... | collective-permute-start | bytes 2752520 | tf_op jit(solution)/shard_map/ppermute | solution.py:199
  1.6 5.0 %collective-permute-start.2 = (bf16[448,1024]{1,0:T(8,128)(2,1)}, bf16[448,1024]{1,0:T(8,128)(2,1)}, u32[]{:S(2)}, u32[]{:S(2)}) collective-permute-start(bf16[448,1024]{1,0:T(8,128)(2,1)} %refs_0_.1), channel_id=1, source_target_pairs={{0,1},{1,0},{2,3},{3,2},{4,5},{5,4},{6,7},{7,6},{8,9},{9,8},{10,11... | collective-permute-start | bytes 2752520 | tf_op jit(solution)/shard_map/ppermute | solution.py:75
  6.7 1.6 %copy-done.4 = bf16[1024,1024]{1,0:T(8,128)(2,1)S(1)} copy-done((bf16[1024,1024]{1,0:T(8,128)(2,1)S(1)}, bf16[1024,1024]{1,0:T(8,128)(2,1)}, u32[]{:S(2)}) %copy-start.4) | copy-done | bytes 2097176
  8.2 1.2 copy-done.8
  9.4 1.7 %down.5 = (bf16[448,512]{1,0:T(8,128)(2,1)S(1)}, f32[448,512]{1,0:T(8,128)S(1)}) custom-call(s32[2]{0:T(128)S(1)} %pad_add_fusion.1.info, bf16[448,1024]{1,0:T(8,128)(2,1)S(1)} %copy-done.8, bf16[1024,1024]{1,0:T(8,128)(2,1)S(1)} %copy-done.4), custom_call_target="tpu_custom_call" | custom-call | flops 1 | bytes 1 | tf_op jit(solution)/shard_map/down/pallas_call | solution.py:93
  11.2 1.3 collective-permute-start.7
  12.5 14.5 %collective-permute-done.2.refs_0_ = bf16[448,1024]{1,0:T(8,128)(2,1)} collective-permute-done((bf16[448,1024]{1,0:T(8,128)(2,1)}, bf16[448,1024]{1,0:T(8,128)(2,1)}, u32[]{:S(2)}, u32[]{:S(2)}) %collective-permute-start.2) | collective-permute-done | bytes 917536 | tf_op jit(solution)/shard_map/ppermute | solution.py:75
  27.0 1.6 %collective-permute-start.12 = (bf16[448,1024]{1,0:T(8,128)(2,1)}, bf16[448,1024]{1,0:T(8,128)(2,1)}, u32[]{:S(2)}, u32[]{:S(2)}) collective-permute-start(bf16[448,1024]{1,0:T(8,128)(2,1)} %collective-permute-done.2.refs_0_), channel_id=1, source_target_pairs={{1,2},{2,1},{5,6},{6,5},{9,10},{10,9},{13,14},{14,13},{17,18},{18,... | collective-permute-start | bytes 2752520 | tf_op jit(solution)/shard_map/ppermute | solution.py:201
  28.7 1.6 %collective-permute-start.1 = (bf16[448,512]{1,0:T(8,128)(2,1)S(1)}, bf16[448,512]{1,0:T(8,128)(2,1)S(1)}, u32[]{:S(2)}, u32[]{:S(2)}) collective-permute-start(bf16[448,512]{1,0:T(8,128)(2,1)S(1)} %add.98.refs_2_.mine), channel_id=1, source_target_pairs={{0,8},{4,12},{8,0},{12,4},{16,24},{20,28},{24,16},{28,20},{1,9},{5... | collective-permute-start | bytes 1376264 | tf_op jit(solution)/shard_map/ppermute | solution.py:75
  30.3 2.3 %down.6 = (bf16[448,512]{1,0:T(8,128)(2,1)S(1)}, f32[448,512]{1,0:T(8,128)S(1)}) custom-call(s32[2]{0:T(128)S(1)} %pad_add_fusion.1.info, bf16[448,1024]{1,0:T(8,128)(2,1)} %collective-permute-done.2.refs_0_, bf16[1024,1024]{1,0:T(8,128)(2,1)S(1)} %copy-done.5, bf16[448,512]{1,0:T(8,128)(2,1)S(1)} %add.98.refs_2_.mine), custom_call_target="tpu_custom_call" | custom-call | flops 1 | bytes 1 | tf_op jit(solution)/shard_map/down/pallas_call | solution.py:93
  32.6 7.5 %collective-permute-done.1.came = bf16[448,512]{1,0:T(8,128)(2,1)S(1)} collective-permute-done((bf16[448,512]{1,0:T(8,128)(2,1)S(1)}, bf16[448,512]{1,0:T(8,128)(2,1)S(1)}, u32[]{:S(2)}, u32[]{:S(2)}) %collective-permute-start.1) | collective-permute-done | bytes 458784 | tf_op jit(solution)/shard_map/ppermute | solution.py:75
  40.4 1.6 %collective-permute-start.5 = (bf16[448,512]{1,0:T(8,128)(2,1)S(1)}, bf16[448,512]{1,0:T(8,128)(2,1)}, u32[]{:S(2)}, u32[]{:S(2)}) collective-permute-start(bf16[448,512]{1,0:T(8,128)(2,1)S(1)} %add.100.refs_3_.mine), channel_id=1, source_target_pairs={{0,8},{4,12},{8,0},{12,4},{16,24},{20,28},{24,16},{28,20},{1,9},{5... | collective-permute-start | bytes 1376264 | tf_op jit(solution)/shard_map/ppermute | solution.py:75
  41.9 1.5 %collective-permute-start.3 = (bf16[448,512]{1,0:T(8,128)(2,1)S(1)}, bf16[448,512]{1,0:T(8,128)(2,1)}, u32[]{:S(2)}, u32[]{:S(2)}) collective-permute-start(bf16[448,512]{1,0:T(8,128)(2,1)S(1)} %add.99.refs_0_.mine), channel_id=1, source_target_pairs={{0,16},{4,20},{8,24},{12,28},{16,0},{20,4},{24,8},{28,12},{1,17},{... | collective-permute-start | bytes 1376264 | tf_op jit(solution)/shard_map/ppermute | solution.py:75
  43.4 4.8 %collective-permute-done.7.refs_1_ = bf16[448,1024]{1,0:T(8,128)(2,1)S(1)} collective-permute-done((bf16[448,1024]{1,0:T(8,128)(2,1)}, bf16[448,1024]{1,0:T(8,128)(2,1)S(1)}, u32[]{:S(2)}, u32[]{:S(2)}) %collective-permute-start.7) | collective-permute-done | bytes 917536 | tf_op jit(solution)/shard_map/ppermute | solution.py:200
  48.3 2.6 %down.7 = (bf16[448,512]{1,0:T(8,128)(2,1)}, f32[448,512]{1,0:T(8,128)S(1)}) custom-call(s32[2]{0:T(128)S(1)} %pad_add_fusion.1.info, bf16[448,1024]{1,0:T(8,128)(2,1)} %collective-permute-done.6.refs_0_, bf16[448,1024]{1,0:T(8,128)(2,1)S(1)} %collective-permute-done.7.refs_1_, bf16[1024,1024]{1,0:T(8,128)(2,1)S(1)} %copy-done.5, ...), custom_call_target="tpu_custom_call" | custom-call | flops 1 | bytes 1 | tf_op jit(solution)/shard_map/down/pallas_call | solution.py:93
  53.0 1.4 %collective-permute-start.13 = (bf16[320,1024]{1,0:T(8,128)(2,1)S(1)}, bf16[320,1024]{1,0:T(8,128)(2,1)S(1)}, u32[]{:S(2)}, u32[]{:S(2)}) collective-permute-start(bf16[320,1024]{1,0:T(8,128)(2,1)S(1)} %slice.42.refs_0_), channel_id=1, source_target_pairs={{1,0},{2,3},{5,4},{6,7},{9,8},{10,11},{13,12},{14,15},{17,16},{18,... | collective-permute-start | bytes 1966088 | tf_op jit(solution)/shard_map/ppermute | solution.py:203
  54.4 1.4 %fusion.13 = (bf16[448,512]{1,0:T(8,128)(2,1)S(1)}, bf16[448,512]{1,0:T(8,128)(2,1)S(1)}, bf16[448,512]{1,0:T(8,128)(2,1)S(1)}) fusion(bf16[1792,1024]{1,0:T(8,128)(2,1)} %param.9, s32[]{:T(128)S(6)} %select_n.122, s32[]{:T(128)S(6)} %select_n.115, s32[]{:T(128)S(6)} %select_n.116, s32[]{:T(128)S(6)} %select_n.114), kind=kLoop, calls=%fused_computation.32 | loop fusion | bytes 2752528 | tf_op jit(solution)/shard_map/dynamic_slice | solution.py:139
  55.9 1.3 add.101.refs_0_.mine
  57.2 1.5 %vision.5.refs_0_.own = bf16[4,112,512]{2,1,0:T(8,128)(2,1)S(1)} custom-call(bf16[448,512]{1,0:T(8,128)(2,1)S(1)} %add.99.refs_0_.mine, bf16[448,512]{1,0:T(8,128)(2,1)} %collective-permute-done.3.came, bf16[448,512]{1,0:T(8,128)(2,1)S(1)} %get-tuple-element.63.tokens, bf16[1,512]{1,0:T(2,128)(2,1)S(1)} %broadcast_in_dim.15.scale, ...), custom_call_target="tpu_custom_call" | custom-call | flops 1 | bytes 1 | tf_op jit(solution)/shard_map/vision/pallas_call | solution.py:140
  59.3 1.5 %collective-permute-start.10 = (bf16[448,512]{1,0:T(8,128)(2,1)S(1)}, bf16[448,512]{1,0:T(8,128)(2,1)S(1)}, u32[]{:S(2)}, u32[]{:S(2)}) collective-permute-start(bf16[448,512]{1,0:T(8,128)(2,1)S(1)} %add.101.refs_0_.mine), channel_id=1, source_target_pairs={{0,16},{4,20},{8,24},{12,28},{16,0},{20,4},{24,8},{28,12},{1,17},{... | collective-permute-start | bytes 1376264 | tf_op jit(solution)/shard_map/ppermute | solution.py:75
  61.9 1.6 %collective-permute-start.15 = (bf16[448,512]{1,0:T(8,128)(2,1)S(1)}, bf16[448,512]{1,0:T(8,128)(2,1)S(1)}, u32[]{:S(2)}, u32[]{:S(2)}) collective-permute-start(bf16[448,512]{1,0:T(8,128)(2,1)S(1)} %add.102.refs_0_.mine), channel_id=1, source_target_pairs={{0,8},{4,12},{8,0},{12,4},{16,24},{20,28},{24,16},{28,20},{1,9},{5... | collective-permute-start | bytes 1376264 | tf_op jit(solution)/shard_map/ppermute | solution.py:75
  63.5 1.8 %merge.5 = (bf16[112,512]{1,0:T(8,128)(2,1)S(1)}, f32[112,512]{1,0:T(8,128)S(1)}) custom-call(s32[2]{0:T(128)S(1)} %pad_add_fusion.1.info, bf16[4,112,512]{2,1,0:T(8,128)(2,1)S(1)} %vision.5.refs_0_.own, bf16[4,112,512]{2,1,0:T(8,128)(2,1)S(1)} %collective-permute-done.8.other, bf16[4,1024,512]{2,1,0:T(8,128)(2,1)S(1)} %copy-done, ...), custom_call_target="tpu_custom_call" | custom-call | flops 1 | bytes 1 | tf_op jit(solution)/shard_map/merge/pallas_call | solution.py:155
  65.2 6.5 %collective-permute-done.10.came = bf16[448,512]{1,0:T(8,128)(2,1)S(1)} collective-permute-done((bf16[448,512]{1,0:T(8,128)(2,1)S(1)}, bf16[448,512]{1,0:T(8,128)(2,1)S(1)}, u32[]{:S(2)}, u32[]{:S(2)}) %collective-permute-start.10) | collective-permute-done | bytes 458784 | tf_op jit(solution)/shard_map/ppermute | solution.py:75
  72.4 1.8 %down.8 = (bf16[320,512]{1,0:T(8,128)(2,1)}, f32[320,512]{1,0:T(8,128)S(1)}) custom-call(s32[2]{0:T(128)S(1)} %pad_add_fusion.1.info, bf16[320,1024]{1,0:T(8,128)(2,1)S(1)} %slice.42.refs_0_, bf16[320,1024]{1,0:T(8,128)(2,1)S(1)} %collective-permute-done.13.refs_1_, bf16[1024,1024]{1,0:T(8,128)(2,1)S(1)} %copy-done.5, bf16[4,112,512]{2,1,0:T(8,128)(2,1)S(1)} %vision.6.refs_3_.own), custom_call_target="tpu_custom_call" | custom-call | flops 1 | bytes 1 | tf_op jit(solution)/shard_map/down/pallas_call | solution.py:93
  74.7 1.7 %slice.43.refs_0_ = bf16[128,1024]{1,0:T(8,128)(2,1)} slice(bf16[448,1024]{1,0:T(8,128)(2,1)} %collective-permute-done.12), slice={[320:448], [0:1024]} | slice | bytes 524288 | tf_op jit(solution)/shard_map/slice | solution.py:254
  76.3 1.5 %collective-permute-start.17 = (bf16[128,1024]{1,0:T(8,128)(2,1)}, bf16[128,1024]{1,0:T(8,128)(2,1)}, u32[]{:S(2)}, u32[]{:S(2)}) collective-permute-start(bf16[128,1024]{1,0:T(8,128)(2,1)} %slice.43.refs_0_), channel_id=1, source_target_pairs={{1,0},{2,3},{5,4},{6,7},{9,8},{10,11},{13,12},{14,15},{17,16},{18,... | collective-permute-start | bytes 786440 | tf_op jit(solution)/shard_map/ppermute | solution.py:203
  77.9 1.6 %collective-permute-start.20 = (bf16[448,512]{1,0:T(8,128)(2,1)S(1)}, bf16[448,512]{1,0:T(8,128)(2,1)}, u32[]{:S(2)}, u32[]{:S(2)}) collective-permute-start(bf16[448,512]{1,0:T(8,128)(2,1)S(1)} %add.103.refs_0_.mine), channel_id=1, source_target_pairs={{0,16},{4,20},{8,24},{12,28},{16,0},{20,4},{24,8},{28,12},{1,17},{... | collective-permute-start | bytes 1376264 | tf_op jit(solution)/shard_map/ppermute | solution.py:75
  82.7 1.6 %collective-permute-start.19 = (bf16[320,512]{1,0:T(8,128)(2,1)S(1)}, bf16[320,512]{1,0:T(8,128)(2,1)S(1)}, u32[]{:S(2)}, u32[]{:S(2)}) collective-permute-start(bf16[320,512]{1,0:T(8,128)(2,1)S(1)} %add.104.refs_0_.mine), channel_id=1, source_target_pairs={{0,8},{4,12},{8,0},{12,4},{16,24},{20,28},{24,16},{28,20},{1,9},{5... | collective-permute-start | bytes 983048 | tf_op jit(solution)/shard_map/ppermute | solution.py:75
  84.3 2.2 %copy-done.1 = bf16[4,1024,512]{2,1,0:T(8,128)(2,1)S(1)} copy-done((bf16[4,1024,512]{2,1,0:T(8,128)(2,1)S(1)}, bf16[4,1024,512]{2,1,0:T(8,128)(2,1)}, u32[]{:S(2)}) %copy-start.1) | copy-done | bytes 4194328
  86.4 2.2 %merge.6 = (bf16[112,512]{1,0:T(8,128)(2,1)S(1)}, f32[112,512]{1,0:T(8,128)S(1)}) custom-call(s32[2]{0:T(128)S(1)} %pad_add_fusion.1.info, bf16[4,112,512]{2,1,0:T(8,128)(2,1)S(1)} %vision.6.refs_3_.own, bf16[4,112,512]{2,1,0:T(8,128)(2,1)} %collective-permute-done.11.other, bf16[4,1024,512]{2,1,0:T(8,128)(2,1)S(1)} %copy-done.1, ...), custom_call_target="tpu_custom_call" | custom-call | flops 1 | bytes 1 | tf_op jit(solution)/shard_map/merge/pallas_call | solution.py:155
  88.7 1.5 %down.9 = (bf16[128,512]{1,0:T(8,128)(2,1)S(1)}, f32[128,512]{1,0:T(8,128)S(1)}) custom-call(s32[2]{0:T(128)S(1)} %pad_add_fusion.1.info, bf16[128,1024]{1,0:T(8,128)(2,1)} %slice.43.refs_0_, bf16[128,1024]{1,0:T(8,128)(2,1)} %collective-permute-done.17.refs_1_, bf16[1024,1024]{1,0:T(8,128)(2,1)S(1)} %copy-done.5, bf16[112,512]{1,0:T(8,128)(2,1)S(1)} %get-tuple-element.44.refs_3_), custom_call_target="tpu_custom_call" | custom-call | flops 1 | bytes 1 | tf_op jit(solution)/shard_map/down/pallas_call | solution.py:93
  90.8 1.7 %vision.7.refs_0_.own = bf16[4,112,512]{2,1,0:T(8,128)(2,1)S(1)} custom-call(bf16[448,512]{1,0:T(8,128)(2,1)S(1)} %add.103.refs_0_.mine, bf16[448,512]{1,0:T(8,128)(2,1)} %collective-permute-done.20.came, bf16[448,512]{1,0:T(8,128)(2,1)S(1)} %get-tuple-element.61.tokens, bf16[1,512]{1,0:T(2,128)(2,1)S(1)} %broadcast_in_dim.15.scale, ...), custom_call_target="tpu_custom_call" | custom-call | flops 1 | bytes 1 | tf_op jit(solution)/shard_map/vision/pallas_call | solution.py:140
  92.8 3.2 %collective-permute-start.16 = (bf16[224,512]{1,0:T(8,128)(2,1)S(1)}, bf16[224,512]{1,0:T(8,128)(2,1)S(1)}, u32[]{:S(2)}, u32[]{:S(2)}) collective-permute-start(bf16[224,512]{1,0:T(8,128)(2,1)S(1)} %pad_maximum_fusion.1), channel_id=1, source_target_pairs={{0,1},{1,0},{2,3},{3,2},{4,5},{5,4},{6,7},{7,6},{8,9},{9,8},{10,11... | collective-permute-start | bytes 688136 | tf_op jit(solution)/shard_map/ppermute | solution.py:75
  97.2 1.6 %collective-permute-start.21 = (bf16[128,512]{1,0:T(8,128)(2,1)S(1)}, bf16[128,512]{1,0:T(8,128)(2,1)S(1)}, u32[]{:S(2)}, u32[]{:S(2)}) collective-permute-start(bf16[128,512]{1,0:T(8,128)(2,1)S(1)} %add.106.refs_0_.mine), channel_id=1, source_target_pairs={{0,8},{4,12},{8,0},{12,4},{16,24},{20,28},{24,16},{28,20},{1,9},{5... | collective-permute-start | bytes 393224 | tf_op jit(solution)/shard_map/ppermute | solution.py:75
  98.9 1.8 %merge.7 = (bf16[112,512]{1,0:T(8,128)(2,1)S(1)}, f32[112,512]{1,0:T(8,128)S(1)}) custom-call(s32[2]{0:T(128)S(1)} %pad_add_fusion.1.info, bf16[4,112,512]{2,1,0:T(8,128)(2,1)S(1)} %vision.7.refs_0_.own, bf16[4,112,512]{2,1,0:T(8,128)(2,1)S(1)} %collective-permute-done.22.other, bf16[4,1024,512]{2,1,0:T(8,128)(2,1)S(1)} %copy-done.2, ...), custom_call_target="tpu_custom_call" | custom-call | flops 1 | bytes 1 | tf_op jit(solution)/shard_map/merge/pallas_call | solution.py:155
  100.7 1.9 %collective-permute-done.21.came = bf16[128,512]{1,0:T(8,128)(2,1)S(1)} collective-permute-done((bf16[128,512]{1,0:T(8,128)(2,1)S(1)}, bf16[128,512]{1,0:T(8,128)(2,1)S(1)}, u32[]{:S(2)}, u32[]{:S(2)}) %collective-permute-start.21) | collective-permute-done | bytes 131104 | tf_op jit(solution)/shard_map/ppermute | solution.py:75
  103.5 3.2 %collective-permute-done.24.came = bf16[320,512]{1,0:T(8,128)(2,1)S(1)} collective-permute-done((bf16[320,512]{1,0:T(8,128)(2,1)S(1)}, bf16[320,512]{1,0:T(8,128)(2,1)S(1)}, u32[]{:S(2)}, u32[]{:S(2)}) %collective-permute-start.24) | collective-permute-done | bytes 327712 | tf_op jit(solution)/shard_map/ppermute | solution.py:75
  108.8 1.3 collective-permute-start.33
  110.2 2.2 %copy-done.3 = bf16[4,1024,512]{2,1,0:T(8,128)(2,1)S(1)} copy-done((bf16[4,1024,512]{2,1,0:T(8,128)(2,1)S(1)}, bf16[4,1024,512]{2,1,0:T(8,128)(2,1)}, u32[]{:S(2)}) %copy-start.3) | copy-done | bytes 4194328
  112.4 1.8 %merge.8 = (bf16[80,512]{1,0:T(8,128)(2,1)S(1)}, f32[80,512]{1,0:T(8,128)S(1)}) custom-call(s32[2]{0:T(128)S(1)} %pad_add_fusion.1.info, bf16[4,80,512]{2,1,0:T(8,128)(2,1)S(1)} %vision.8.refs_0_.own, bf16[4,80,512]{2,1,0:T(8,128)(2,1)S(1)} %collective-permute-done.26.other, bf16[4,1024,512]{2,1,0:T(8,128)(2,1)S(1)} %copy-done.3, ...), custom_call_target="tpu_custom_call" | custom-call | flops 1 | bytes 1 | tf_op jit(solution)/shard_map/merge/pallas_call | solution.py:155
  114.1 1.8 %collective-permute-start.28 = (bf16[80,512]{1,0:T(8,128)(2,1)S(1)}, bf16[80,512]{1,0:T(8,128)(2,1)S(1)}, u32[]{:S(2)}, u32[]{:S(2)}) collective-permute-start(bf16[80,512]{1,0:T(8,128)(2,1)S(1)} %get-tuple-element.53.refs_0_), channel_id=1, source_target_pairs={{0,1},{1,0},{2,3},{3,2},{4,5},{5,4},{6,7},{7,6},{8,9},{9,8},{10,11... | collective-permute-start | bytes 245768 | tf_op jit(solution)/shard_map/ppermute | solution.py:75
  115.9 1.7 %merge.9 = (bf16[32,512]{1,0:T(8,128)(2,1)S(1)}, f32[32,512]{1,0:T(8,128)S(1)}) custom-call(s32[2]{0:T(128)S(1)} %pad_add_fusion.1.info, bf16[4,32,512]{2,1,0:T(8,128)(2,1)S(1)} %vision.9.refs_0_.own, bf16[4,32,512]{2,1,0:T(8,128)(2,1)S(1)} %collective-permute-done.29.other, bf16[4,1024,512]{2,1,0:T(8,128)(2,1)S(1)} %copy-done.3, ...), custom_call_target="tpu_custom_call" | custom-call | flops 1 | bytes 1 | tf_op jit(solution)/shard_map/merge/pallas_call | solution.py:155
  118.2 1.7 %collective-permute-start.25 = (bf16[112,512]{1,0:T(8,128)(2,1)S(1)}, bf16[112,512]{1,0:T(8,128)(2,1)S(1)}, u32[]{:S(2)}, u32[]{:S(2)}) collective-permute-start(bf16[112,512]{1,0:T(8,128)(2,1)S(1)} %get-tuple-element.51.refs_0_), channel_id=1, source_target_pairs={{0,2},{1,3},{2,0},{3,1},{4,6},{5,7},{6,4},{7,5},{8,10},{9,11},{10,... | collective-permute-start | bytes 344072 | tf_op jit(solution)/shard_map/ppermute | solution.py:75
  119.9 2.6 %collective-permute-done.33 = bf16[224,512]{1,0:T(8,128)(2,1)S(1)} collective-permute-done((bf16[224,512]{1,0:T(8,128)(2,1)S(1)}, bf16[224,512]{1,0:T(8,128)(2,1)S(1)}, u32[]{:S(2)}, u32[]{:S(2)}) %collective-permute-start.33) | collective-permute-done | bytes 229408 | tf_op jit(solution)/shard_map/ppermute | solution.py:75
  122.6 1.6 %collective-permute-done.28.came = bf16[80,512]{1,0:T(8,128)(2,1)S(1)} collective-permute-done((bf16[80,512]{1,0:T(8,128)(2,1)S(1)}, bf16[80,512]{1,0:T(8,128)(2,1)S(1)}, u32[]{:S(2)}, u32[]{:S(2)}) %collective-permute-start.28) | collective-permute-done | bytes 81952 | tf_op jit(solution)/shard_map/ppermute | solution.py:75
  124.5 2.7 %collective-permute-start.32 = (bf16[32,512]{1,0:T(8,128)(2,1)S(1)}, bf16[32,512]{1,0:T(8,128)(2,1)S(1)}, u32[]{:S(2)}, u32[]{:S(2)}) collective-permute-start(bf16[32,512]{1,0:T(8,128)(2,1)S(1)} %get-tuple-element.57), channel_id=1, source_target_pairs={{0,2},{1,3},{2,0},{3,1},{4,6},{5,7},{6,4},{7,5},{8,10},{9,11},{10,... | collective-permute-start | bytes 98312 | tf_op jit(solution)/shard_map/ppermute | solution.py:75
  127.6 4.3 %collective-permute-done.32 = bf16[32,512]{1,0:T(8,128)(2,1)S(1)} collective-permute-done((bf16[32,512]{1,0:T(8,128)(2,1)S(1)}, bf16[32,512]{1,0:T(8,128)(2,1)S(1)}, u32[]{:S(2)}, u32[]{:S(2)}) %collective-permute-start.32) | collective-permute-done | bytes 32800 | tf_op jit(solution)/shard_map/ppermute | solution.py:75
  132.0 1.4 %fusion = bf16[512,512]{1,0:T(8,128)(2,1)} fusion(bf16[512,512]{1,0:T(8,128)(2,1)S(1)} %copy-done.17, pred[512]{0:T(512)(128)(4,1)S(1)} %compare_reduce_fusion, bf16[112,512]{1,0:T(8,128)(2,1)S(1)} %get-tuple-element.67, bf16[112,512]{1,0:T(8,128)(2,1)S(1)} %get-tuple-element.66, bf16[112,512]{1,0:T(8,128)(2,1)S(1)} %get-tuple-element.65, ...), kind=kOutput, calls=%fused_computation.1 | convolution fusion | flops 237469696 | bytes 1511680 | tf_op jit(solution)/shard_map/dot_general | solution.py:18
  (105 shorter events, 15.3 us)
Async XLA Ops:
  0.0 11.2 %collective-permute-start.6 = (bf16[448,1024]{1,0:T(8,128)(2,1)}, bf16[448,1024]{1,0:T(8,128)(2,1)}, u32[]{:S(2)}, u32[]{:S(2)}) collective-permute-start(bf16[448,1024]{1,0:T(8,128)(2,1)} %refs_0_.1), channel_id=1, source_target_pairs={{1,2},{2,1},{5,6},{6,5},{9,10},{10,9},{13,14},{14,13},{17,18},{18,... | collective-permute-start | bytes 2752520 | tf_op jit(solution)/shard_map/ppermute | solution.py:199
  1.6 25.4 %collective-permute-start.2 = (bf16[448,1024]{1,0:T(8,128)(2,1)}, bf16[448,1024]{1,0:T(8,128)(2,1)}, u32[]{:S(2)}, u32[]{:S(2)}) collective-permute-start(bf16[448,1024]{1,0:T(8,128)(2,1)} %refs_0_.1), channel_id=1, source_target_pairs={{0,1},{1,0},{2,3},{3,2},{4,5},{5,4},{6,7},{7,6},{8,9},{9,8},{10,11... | collective-permute-start | bytes 2752520 | tf_op jit(solution)/shard_map/ppermute | solution.py:75
  9.4 20.8 %copy-start.5 = (bf16[1024,1024]{1,0:T(8,128)(2,1)S(1)}, bf16[1024,1024]{1,0:T(8,128)(2,1)}, u32[]{:S(2)}) copy-start(bf16[1024,1024]{1,0:T(8,128)(2,1)} %refs_2_.5) | copy-start | bytes 6291460
  11.1 17.5 %collective-permute-start = (bf16[448,512]{1,0:T(8,128)(2,1)S(1)}, bf16[448,512]{1,0:T(8,128)(2,1)S(1)}, u32[]{:S(2)}, u32[]{:S(2)}) collective-permute-start(bf16[448,512]{1,0:T(8,128)(2,1)S(1)} %get-tuple-element.34.refs_0_), channel_id=1, source_target_pairs={{0,4},{4,0},{8,12},{12,8},{16,20},{20,16},{24,28},{28,24},{1,5},{5... | collective-permute-start | bytes 1376264 | tf_op jit(solution)/shard_map/ppermute | solution.py:75
  11.2 37.1 %collective-permute-start.7 = (bf16[448,1024]{1,0:T(8,128)(2,1)}, bf16[448,1024]{1,0:T(8,128)(2,1)S(1)}, u32[]{:S(2)}, u32[]{:S(2)}) collective-permute-start(bf16[448,1024]{1,0:T(8,128)(2,1)} %collective-permute-done.6.refs_0_), channel_id=1, source_target_pairs={{1,0},{2,3},{5,4},{6,7},{9,8},{10,11},{13,12},{14,15},{17,16},{18,... | collective-permute-start | bytes 2752520 | tf_op jit(solution)/shard_map/ppermute | solution.py:200
  27.0 24.9 %collective-permute-start.12 = (bf16[448,1024]{1,0:T(8,128)(2,1)}, bf16[448,1024]{1,0:T(8,128)(2,1)}, u32[]{:S(2)}, u32[]{:S(2)}) collective-permute-start(bf16[448,1024]{1,0:T(8,128)(2,1)} %collective-permute-done.2.refs_0_), channel_id=1, source_target_pairs={{1,2},{2,1},{5,6},{6,5},{9,10},{10,9},{13,14},{14,13},{17,18},{18,... | collective-permute-start | bytes 2752520 | tf_op jit(solution)/shard_map/ppermute | solution.py:201
  28.7 11.5 %collective-permute-start.1 = (bf16[448,512]{1,0:T(8,128)(2,1)S(1)}, bf16[448,512]{1,0:T(8,128)(2,1)S(1)}, u32[]{:S(2)}, u32[]{:S(2)}) collective-permute-start(bf16[448,512]{1,0:T(8,128)(2,1)S(1)} %add.98.refs_2_.mine), channel_id=1, source_target_pairs={{0,8},{4,12},{8,0},{12,4},{16,24},{20,28},{24,16},{28,20},{1,9},{5... | collective-permute-start | bytes 1376264 | tf_op jit(solution)/shard_map/ppermute | solution.py:75
  32.6 7.7 %collective-permute-start.4 = (bf16[448,512]{1,0:T(8,128)(2,1)S(1)}, bf16[448,512]{1,0:T(8,128)(2,1)S(1)}, u32[]{:S(2)}, u32[]{:S(2)}) collective-permute-start(bf16[448,512]{1,0:T(8,128)(2,1)S(1)} %get-tuple-element.35.refs_0_), channel_id=1, source_target_pairs={{0,4},{4,0},{8,12},{12,8},{16,20},{20,16},{24,28},{28,24},{1,5},{5... | collective-permute-start | bytes 1376264 | tf_op jit(solution)/shard_map/ppermute | solution.py:75
  40.4 15.5 %copy-start.16 = (bf16[1024]{0:T(1024)(128)(2,1)S(1)}, bf16[1024]{0:T(1024)(128)(2,1)}, u32[]{:S(2)}) copy-start(bf16[1024]{0:T(1024)(128)(2,1)} %param.10) | copy-start | bytes 6148
  40.4 15.6 %collective-permute-start.5 = (bf16[448,512]{1,0:T(8,128)(2,1)S(1)}, bf16[448,512]{1,0:T(8,128)(2,1)}, u32[]{:S(2)}, u32[]{:S(2)}) collective-permute-start(bf16[448,512]{1,0:T(8,128)(2,1)S(1)} %add.100.refs_3_.mine), channel_id=1, source_target_pairs={{0,8},{4,12},{8,0},{12,4},{16,24},{20,28},{24,16},{28,20},{1,9},{5... | collective-permute-start | bytes 1376264 | tf_op jit(solution)/shard_map/ppermute | solution.py:75
  41.9 15.3 %collective-permute-start.3 = (bf16[448,512]{1,0:T(8,128)(2,1)S(1)}, bf16[448,512]{1,0:T(8,128)(2,1)}, u32[]{:S(2)}, u32[]{:S(2)}) collective-permute-start(bf16[448,512]{1,0:T(8,128)(2,1)S(1)} %add.99.refs_0_.mine), channel_id=1, source_target_pairs={{0,16},{4,20},{8,24},{12,28},{16,0},{20,4},{24,8},{28,12},{1,17},{... | collective-permute-start | bytes 1376264 | tf_op jit(solution)/shard_map/ppermute | solution.py:75
  51.8 9.0 %collective-permute-start.9 = (bf16[448,512]{1,0:T(8,128)(2,1)}, bf16[448,512]{1,0:T(8,128)(2,1)}, u32[]{:S(2)}, u32[]{:S(2)}) collective-permute-start(bf16[448,512]{1,0:T(8,128)(2,1)} %get-tuple-element.37.refs_0_), channel_id=1, source_target_pairs={{0,4},{4,0},{8,12},{12,8},{16,20},{20,16},{24,28},{28,24},{1,5},{5... | collective-permute-start | bytes 1376264 | tf_op jit(solution)/shard_map/ppermute | solution.py:75
  53.0 7.8 %copy-start.7 = (f32[448,512]{1,0:T(8,128)S(1)}, f32[448,512]{1,0:T(8,128)}, u32[]{:S(2)}) copy-start(f32[448,512]{1,0:T(8,128)} %copy-done.6) | copy-start | bytes 2752516
  53.0 19.4 %collective-permute-start.13 = (bf16[320,1024]{1,0:T(8,128)(2,1)S(1)}, bf16[320,1024]{1,0:T(8,128)(2,1)S(1)}, u32[]{:S(2)}, u32[]{:S(2)}) collective-permute-start(bf16[320,1024]{1,0:T(8,128)(2,1)S(1)} %slice.42.refs_0_), channel_id=1, source_target_pairs={{1,0},{2,3},{5,4},{6,7},{9,8},{10,11},{13,12},{14,15},{17,16},{18,... | collective-permute-start | bytes 1966088 | tf_op jit(solution)/shard_map/ppermute | solution.py:203
  55.8 7.6 %copy-start = (bf16[4,1024,512]{2,1,0:T(8,128)(2,1)S(1)}, bf16[4,1024,512]{2,1,0:T(8,128)(2,1)}, u32[]{:S(2)}) copy-start(bf16[4,1024,512]{2,1,0:T(8,128)(2,1)} %weight.9) | copy-start | bytes 12582916
  58.7 4.8 %collective-permute-start.8 = (bf16[4,112,512]{2,1,0:T(8,128)(2,1)S(1)}, bf16[4,112,512]{2,1,0:T(8,128)(2,1)S(1)}, u32[]{:S(2)}, u32[]{:S(2)}) collective-permute-start(bf16[4,112,512]{2,1,0:T(8,128)(2,1)S(1)} %vision.5.refs_0_.own), channel_id=1, source_target_pairs={{0,4},{4,0},{8,12},{12,8},{16,20},{20,16},{24,28},{28,24},{1,5},{5... | collective-permute-start | bytes 1376264 | tf_op jit(solution)/shard_map/ppermute | solution.py:75
  59.3 12.5 %collective-permute-start.10 = (bf16[448,512]{1,0:T(8,128)(2,1)S(1)}, bf16[448,512]{1,0:T(8,128)(2,1)S(1)}, u32[]{:S(2)}, u32[]{:S(2)}) collective-permute-start(bf16[448,512]{1,0:T(8,128)(2,1)S(1)} %add.101.refs_0_.mine), channel_id=1, source_target_pairs={{0,16},{4,20},{8,24},{12,28},{16,0},{20,4},{24,8},{28,12},{1,17},{... | collective-permute-start | bytes 1376264 | tf_op jit(solution)/shard_map/ppermute | solution.py:75
  61.9 15.9 %collective-permute-start.15 = (bf16[448,512]{1,0:T(8,128)(2,1)S(1)}, bf16[448,512]{1,0:T(8,128)(2,1)S(1)}, u32[]{:S(2)}, u32[]{:S(2)}) collective-permute-start(bf16[448,512]{1,0:T(8,128)(2,1)S(1)} %add.102.refs_0_.mine), channel_id=1, source_target_pairs={{0,8},{4,12},{8,0},{12,4},{16,24},{20,28},{24,16},{28,20},{1,9},{5... | collective-permute-start | bytes 1376264 | tf_op jit(solution)/shard_map/ppermute | solution.py:75
  65.2 12.7 %copy-start.11 = (bf16[112,512]{1,0:T(8,128)(2,1)}, bf16[112,512]{1,0:T(8,128)(2,1)S(1)}, u32[]{:S(2)}) copy-start(bf16[112,512]{1,0:T(8,128)(2,1)S(1)} %get-tuple-element.40.refs_0_) | copy-start | bytes 344068
  65.2 12.7 %copy-start.13 = (f32[112,512]{1,0:T(8,128)}, f32[112,512]{1,0:T(8,128)S(1)}, u32[]{:S(2)}) copy-start(f32[112,512]{1,0:T(8,128)S(1)} %get-tuple-element.39) | copy-start | bytes 688132
  72.3 12.0 %collective-permute-start.11 = (bf16[4,112,512]{2,1,0:T(8,128)(2,1)S(1)}, bf16[4,112,512]{2,1,0:T(8,128)(2,1)}, u32[]{:S(2)}, u32[]{:S(2)}) collective-permute-start(bf16[4,112,512]{2,1,0:T(8,128)(2,1)S(1)} %vision.6.refs_3_.own), channel_id=1, source_target_pairs={{0,4},{4,0},{8,12},{12,8},{16,20},{20,16},{24,28},{28,24},{1,5},{5... | collective-permute-start | bytes 1376264 | tf_op jit(solution)/shard_map/ppermute | solution.py:75
  74.2 3.8 %copy-start.9 = (f32[320,512]{1,0:T(8,128)}, f32[320,512]{1,0:T(8,128)S(1)}, u32[]{:S(2)}) copy-start(f32[320,512]{1,0:T(8,128)S(1)} %get-tuple-element.41.mine) | copy-start | bytes 1966084
  74.2 6.3 %collective-permute-start.14 = (bf16[320,512]{1,0:T(8,128)(2,1)}, bf16[320,512]{1,0:T(8,128)(2,1)}, u32[]{:S(2)}, u32[]{:S(2)}) collective-permute-start(bf16[320,512]{1,0:T(8,128)(2,1)} %get-tuple-element.42.refs_0_), channel_id=1, source_target_pairs={{0,4},{4,0},{8,12},{12,8},{16,20},{20,16},{24,28},{28,24},{1,5},{5... | collective-permute-start | bytes 983048 | tf_op jit(solution)/shard_map/ppermute | solution.py:75
  76.3 12.4 %collective-permute-start.17 = (bf16[128,1024]{1,0:T(8,128)(2,1)}, bf16[128,1024]{1,0:T(8,128)(2,1)}, u32[]{:S(2)}, u32[]{:S(2)}) collective-permute-start(bf16[128,1024]{1,0:T(8,128)(2,1)} %slice.43.refs_0_), channel_id=1, source_target_pairs={{1,0},{2,3},{5,4},{6,7},{9,8},{10,11},{13,12},{14,15},{17,16},{18,... | collective-permute-start | bytes 786440 | tf_op jit(solution)/shard_map/ppermute | solution.py:203
  77.9 12.8 %collective-permute-start.20 = (bf16[448,512]{1,0:T(8,128)(2,1)S(1)}, bf16[448,512]{1,0:T(8,128)(2,1)}, u32[]{:S(2)}, u32[]{:S(2)}) collective-permute-start(bf16[448,512]{1,0:T(8,128)(2,1)S(1)} %add.103.refs_0_.mine), channel_id=1, source_target_pairs={{0,16},{4,20},{8,24},{12,28},{16,0},{20,4},{24,8},{28,12},{1,17},{... | collective-permute-start | bytes 1376264 | tf_op jit(solution)/shard_map/ppermute | solution.py:75
  81.6 8.8 %copy-start.12 = (bf16[112,512]{1,0:T(8,128)(2,1)S(1)}, bf16[112,512]{1,0:T(8,128)(2,1)}, u32[]{:S(2)}) copy-start(bf16[112,512]{1,0:T(8,128)(2,1)} %copy-done.11) | copy-start | bytes 344068
  82.7 13.2 %collective-permute-start.19 = (bf16[320,512]{1,0:T(8,128)(2,1)S(1)}, bf16[320,512]{1,0:T(8,128)(2,1)S(1)}, u32[]{:S(2)}, u32[]{:S(2)}) collective-permute-start(bf16[320,512]{1,0:T(8,128)(2,1)S(1)} %add.104.refs_0_.mine), channel_id=1, source_target_pairs={{0,8},{4,12},{8,0},{12,4},{16,24},{20,28},{24,16},{28,20},{1,9},{5... | collective-permute-start | bytes 983048 | tf_op jit(solution)/shard_map/ppermute | solution.py:75
  84.3 2.2 %copy-start.1 = (bf16[4,1024,512]{2,1,0:T(8,128)(2,1)S(1)}, bf16[4,1024,512]{2,1,0:T(8,128)(2,1)}, u32[]{:S(2)}) copy-start(bf16[4,1024,512]{2,1,0:T(8,128)(2,1)} %weight.9) | copy-start | bytes 12582916
  88.7 10.1 %copy-start.14 = (f32[112,512]{1,0:T(8,128)S(1)}, f32[112,512]{1,0:T(8,128)}, u32[]{:S(2)}) copy-start(f32[112,512]{1,0:T(8,128)} %copy-done.13) | copy-start | bytes 688132
  90.3 8.6 %copy-start.2 = (bf16[4,1024,512]{2,1,0:T(8,128)(2,1)S(1)}, bf16[4,1024,512]{2,1,0:T(8,128)(2,1)}, u32[]{:S(2)}) copy-start(bf16[4,1024,512]{2,1,0:T(8,128)(2,1)} %weight.9) | copy-start | bytes 12582916
  90.3 6.9 %collective-permute-start.18 = (bf16[128,512]{1,0:T(8,128)(2,1)S(1)}, bf16[128,512]{1,0:T(8,128)(2,1)S(1)}, u32[]{:S(2)}, u32[]{:S(2)}) collective-permute-start(bf16[128,512]{1,0:T(8,128)(2,1)S(1)} %get-tuple-element.46.refs_0_), channel_id=1, source_target_pairs={{0,4},{4,0},{8,12},{12,8},{16,20},{20,16},{24,28},{28,24},{1,5},{5... | collective-permute-start | bytes 393224 | tf_op jit(solution)/shard_map/ppermute | solution.py:75
  92.5 6.4 %collective-permute-start.22 = (bf16[4,112,512]{2,1,0:T(8,128)(2,1)S(1)}, bf16[4,112,512]{2,1,0:T(8,128)(2,1)S(1)}, u32[]{:S(2)}, u32[]{:S(2)}) collective-permute-start(bf16[4,112,512]{2,1,0:T(8,128)(2,1)S(1)} %vision.7.refs_0_.own), channel_id=1, source_target_pairs={{0,4},{4,0},{8,12},{12,8},{16,20},{20,16},{24,28},{28,24},{1,5},{5... | collective-permute-start | bytes 1376264 | tf_op jit(solution)/shard_map/ppermute | solution.py:75
  92.8 10.7 %collective-permute-start.16 = (bf16[224,512]{1,0:T(8,128)(2,1)S(1)}, bf16[224,512]{1,0:T(8,128)(2,1)S(1)}, u32[]{:S(2)}, u32[]{:S(2)}) collective-permute-start(bf16[224,512]{1,0:T(8,128)(2,1)S(1)} %pad_maximum_fusion.1), channel_id=1, source_target_pairs={{0,1},{1,0},{2,3},{3,2},{4,5},{5,4},{6,7},{7,6},{8,9},{9,8},{10,11... | collective-permute-start | bytes 688136 | tf_op jit(solution)/shard_map/ppermute | solution.py:75
  96.0 10.6 %collective-permute-start.24 = (bf16[320,512]{1,0:T(8,128)(2,1)S(1)}, bf16[320,512]{1,0:T(8,128)(2,1)S(1)}, u32[]{:S(2)}, u32[]{:S(2)}) collective-permute-start(bf16[320,512]{1,0:T(8,128)(2,1)S(1)} %add.105.refs_0_.mine), channel_id=1, source_target_pairs={{0,16},{4,20},{8,24},{12,28},{16,0},{20,4},{24,8},{28,12},{1,17},{... | collective-permute-start | bytes 983048 | tf_op jit(solution)/shard_map/ppermute | solution.py:75
  97.2 5.4 %collective-permute-start.21 = (bf16[128,512]{1,0:T(8,128)(2,1)S(1)}, bf16[128,512]{1,0:T(8,128)(2,1)S(1)}, u32[]{:S(2)}, u32[]{:S(2)}) collective-permute-start(bf16[128,512]{1,0:T(8,128)(2,1)S(1)} %add.106.refs_0_.mine), channel_id=1, source_target_pairs={{0,8},{4,12},{8,0},{12,4},{16,24},{20,28},{24,16},{28,20},{1,9},{5... | collective-permute-start | bytes 393224 | tf_op jit(solution)/shard_map/ppermute | solution.py:75
  98.8 8.2 %copy-start.15 = (s32[448]{0:T(512)S(1)}, s32[448]{0:T(512)}, u32[]{:S(2)}) copy-start(s32[448]{0:T(512)} %param.13) | copy-start | bytes 5380
  100.6 7.4 %collective-permute-start.23 = (bf16[112,512]{1,0:T(8,128)(2,1)S(1)}, bf16[112,512]{1,0:T(8,128)(2,1)S(1)}, u32[]{:S(2)}, u32[]{:S(2)}) collective-permute-start(bf16[112,512]{1,0:T(8,128)(2,1)S(1)} %get-tuple-element.47.refs_0_), channel_id=1, source_target_pairs={{0,1},{1,0},{2,3},{3,2},{4,5},{5,4},{6,7},{7,6},{8,9},{9,8},{10,11... | collective-permute-start | bytes 344072 | tf_op jit(solution)/shard_map/ppermute | solution.py:75
  102.6 5.9 %collective-permute-start.27 = (bf16[128,512]{1,0:T(8,128)(2,1)S(1)}, bf16[128,512]{1,0:T(8,128)(2,1)S(1)}, u32[]{:S(2)}, u32[]{:S(2)}) collective-permute-start(bf16[128,512]{1,0:T(8,128)(2,1)S(1)} %add.107.refs_0_.mine), channel_id=1, source_target_pairs={{0,16},{4,20},{8,24},{12,28},{16,0},{20,4},{24,8},{28,12},{1,17},{... | collective-permute-start | bytes 393224 | tf_op jit(solution)/shard_map/ppermute | solution.py:75
  107.0 3.2 %collective-permute-start.26 = (bf16[4,80,512]{2,1,0:T(8,128)(2,1)S(1)}, bf16[4,80,512]{2,1,0:T(8,128)(2,1)S(1)}, u32[]{:S(2)}, u32[]{:S(2)}) collective-permute-start(bf16[4,80,512]{2,1,0:T(8,128)(2,1)S(1)} %vision.8.refs_0_.own), channel_id=1, source_target_pairs={{0,4},{4,0},{8,12},{12,8},{16,20},{20,16},{24,28},{28,24},{1,5},{5... | collective-permute-start | bytes 983048 | tf_op jit(solution)/shard_map/ppermute | solution.py:75
  108.6 7.3 %collective-permute-start.29 = (bf16[4,32,512]{2,1,0:T(8,128)(2,1)S(1)}, bf16[4,32,512]{2,1,0:T(8,128)(2,1)S(1)}, u32[]{:S(2)}, u32[]{:S(2)}) collective-permute-start(bf16[4,32,512]{2,1,0:T(8,128)(2,1)S(1)} %vision.9.refs_0_.own), channel_id=1, source_target_pairs={{0,4},{4,0},{8,12},{12,8},{16,20},{20,16},{24,28},{28,24},{1,5},{5... | collective-permute-start | bytes 393224 | tf_op jit(solution)/shard_map/ppermute | solution.py:75
  108.8 13.7 %collective-permute-start.33 = (bf16[224,512]{1,0:T(8,128)(2,1)S(1)}, bf16[224,512]{1,0:T(8,128)(2,1)S(1)}, u32[]{:S(2)}, u32[]{:S(2)}) collective-permute-start(bf16[224,512]{1,0:T(8,128)(2,1)S(1)} %get-tuple-element.50.refs_0_), channel_id=1, source_target_pairs={{0,2},{1,3},{2,0},{3,1},{4,6},{5,7},{6,4},{7,5},{8,10},{9,11},{10,... | collective-permute-start | bytes 688136 | tf_op jit(solution)/shard_map/ppermute | solution.py:75
  110.2 2.2 %copy-start.3 = (bf16[4,1024,512]{2,1,0:T(8,128)(2,1)S(1)}, bf16[4,1024,512]{2,1,0:T(8,128)(2,1)}, u32[]{:S(2)}) copy-start(bf16[4,1024,512]{2,1,0:T(8,128)(2,1)} %weight.9) | copy-start | bytes 12582916
  114.1 17.8 %copy-start.17 = (bf16[512,512]{1,0:T(8,128)(2,1)S(1)}, bf16[512,512]{1,0:T(8,128)(2,1)}, u32[]{:S(2)}) copy-start(bf16[512,512]{1,0:T(8,128)(2,1)} %param.12) | copy-start | bytes 1572868
  114.1 10.0 %collective-permute-start.28 = (bf16[80,512]{1,0:T(8,128)(2,1)S(1)}, bf16[80,512]{1,0:T(8,128)(2,1)S(1)}, u32[]{:S(2)}, u32[]{:S(2)}) collective-permute-start(bf16[80,512]{1,0:T(8,128)(2,1)S(1)} %get-tuple-element.53.refs_0_), channel_id=1, source_target_pairs={{0,1},{1,0},{2,3},{3,2},{4,5},{5,4},{6,7},{7,6},{8,9},{9,8},{10,11... | collective-permute-start | bytes 245768 | tf_op jit(solution)/shard_map/ppermute | solution.py:75
  117.7 6.9 %collective-permute-start.31 = (bf16[32,512]{1,0:T(8,128)(2,1)S(1)}, bf16[32,512]{1,0:T(8,128)(2,1)S(1)}, u32[]{:S(2)}, u32[]{:S(2)}) collective-permute-start(bf16[32,512]{1,0:T(8,128)(2,1)S(1)} %get-tuple-element.54.refs_0_), channel_id=1, source_target_pairs={{0,1},{1,0},{2,3},{3,2},{4,5},{5,4},{6,7},{7,6},{8,9},{9,8},{10,11... | collective-permute-start | bytes 98312 | tf_op jit(solution)/shard_map/ppermute | solution.py:75
  118.2 9.4 %collective-permute-start.25 = (bf16[112,512]{1,0:T(8,128)(2,1)S(1)}, bf16[112,512]{1,0:T(8,128)(2,1)S(1)}, u32[]{:S(2)}, u32[]{:S(2)}) collective-permute-start(bf16[112,512]{1,0:T(8,128)(2,1)S(1)} %get-tuple-element.51.refs_0_), channel_id=1, source_target_pairs={{0,2},{1,3},{2,0},{3,1},{4,6},{5,7},{6,4},{7,5},{8,10},{9,11},{10,... | collective-permute-start | bytes 344072 | tf_op jit(solution)/shard_map/ppermute | solution.py:75
  124.2 7.7 %collective-permute-start.30 = (bf16[80,512]{1,0:T(8,128)(2,1)S(1)}, bf16[80,512]{1,0:T(8,128)(2,1)S(1)}, u32[]{:S(2)}, u32[]{:S(2)}) collective-permute-start(bf16[80,512]{1,0:T(8,128)(2,1)S(1)} %get-tuple-element.55.refs_0_), channel_id=1, source_target_pairs={{0,2},{1,3},{2,0},{3,1},{4,6},{5,7},{6,4},{7,5},{8,10},{9,11},{10,... | collective-permute-start | bytes 245768 | tf_op jit(solution)/shard_map/ppermute | solution.py:75
  124.5 7.3 %collective-permute-start.32 = (bf16[32,512]{1,0:T(8,128)(2,1)S(1)}, bf16[32,512]{1,0:T(8,128)(2,1)S(1)}, u32[]{:S(2)}, u32[]{:S(2)}) collective-permute-start(bf16[32,512]{1,0:T(8,128)(2,1)S(1)} %get-tuple-element.57), channel_id=1, source_target_pairs={{0,2},{1,3},{2,0},{3,1},{4,6},{5,7},{6,4},{7,5},{8,10},{9,11},{10,... | collective-permute-start | bytes 98312 | tf_op jit(solution)/shard_map/ppermute | solution.py:75
  (4 other events, 4.8 us)

commit v2 on v0

v2 whole, which is shorter than its diff:
```python
import functools

import jax
import jax.numpy as jnp
from jax import lax
from jax.experimental import pallas as pl
from jax.experimental.pallas import tpu as pltpu
from jax.sharding import PartitionSpec as P

BF = jnp.bfloat16
F32 = jnp.float32
ANY = pl.BlockSpec(memory_space=pl.ANY)
LITTLE = pl.CostEstimate(flops=1, bytes_accessed=1, transcendentals=0)
ROOM = 8 * 1024 * 1024
PARTS = (2, 2, 2, 2, 2)
SPLIT = (2, 3)
CUT = 0
ORDER = (
    "down0", "sum0", "turn0", "down1:hop_b", "sum1", "residual", "hold", "see0",
    "merge0", "hop3", "down2:hop_d", "turn1", "sum2", "see1:far0", "turn2", "turn2",
    "merge1", "down3", "see2", "sum3", "turn3", "turn3", "merge2", "see3",
    "merge3", "done2", "done3", "early",
)


def _near(shape, kind):
    return pltpu.VMEM(shape, kind)


def _dot(a, b):
    return jnp.dot(a, b, preferred_element_type=F32)


def _down_kernel(half, blocks, waits, info, *refs):
    w, gives, keep = refs[blocks], refs[blocks + 1 + waits : -1], refs[-1]
    mine = info[0]
    block = refs[0][...] if blocks == 1 else jnp.where(info[1] > 0, refs[0][...], refs[1][...])
    give = _dot(block, w[:, pl.ds(pl.multiple_of((1 - mine) * half, half), half)]).astype(BF)
    count = gives[0].shape[0]
    for i, out in enumerate(gives):
        out[...] = give[i * count : (i + 1) * count]
    keep[...] = _dot(block, w[:, pl.ds(pl.multiple_of(mine * half, half), half)])


def _add_kernel(ins, outs, mine, *refs):
    came = refs[0][...] if ins == 1 else jnp.concatenate([ref[...] for ref in refs[:ins]], axis=0)
    total = (mine[...].astype(F32) + came.astype(F32)).astype(BF)
    first = 0
    for out in refs[-outs:]:
        out[...] = total[first : first + out.shape[0]]
        first += out.shape[0]


def _vision_kernel(parts, *refs):
    tokens, scale, info = refs[2 * parts], refs[2 * parts + 1], refs[2 * parts + 2]
    offset = info[0] * tokens.shape[1]
    outs, spread = refs[-3:-1], refs[-1]
    first = 0
    for mine, came in zip(refs[:parts], refs[parts : 2 * parts]):
        rows = pl.ds(first, mine.shape[0])
        for j in range(spread.shape[0]):
            lanes = pl.ds(j * 128, 128)
            scales = scale[:, pl.ds(pl.multiple_of(offset + j * 128, 128), 128)].astype(F32)
            total = mine[:, lanes].astype(F32) + came[:, lanes].astype(F32)
            vision = tokens[rows, lanes].astype(F32) + scales * total
            spread[j, rows, :] = vision.astype(BF).astype(F32)
        first += mine.shape[0]
    for j in range(spread.shape[0]):
        for k in range(4):
            out = outs[k // 2]
            out[k % 2, :, pl.ds(j * 128, 128)] = spread[j, pl.ds(k, out.shape[1], stride=4), :].astype(BF)


def _residual_kernel(half, pieces, info, tokens, *refs):
    sems, outs = refs[-1], refs[-1 - len(pieces) : -1]
    lanes = pl.ds(pl.multiple_of(info[0] * half, half), half)
    patches = tokens.shape[0] // 4
    copies = []
    for i, (block, first, count) in enumerate(pieces):
        rows = pl.ds(pl.multiple_of(info[3 + block] * patches + first, 32), count)
        copies.append(pltpu.make_async_copy(tokens.at[rows, lanes], outs[i], sems.at[i]))
        copies[-1].start()
    for copy in copies:
        copy.wait()


def _relay_kernel(first, block, *refs):
    refs[-1][...] = block[pl.ds(first, refs[-1].shape[0]), :]


def _hold_kernel(weight, *refs):
    held, sem = refs[-2:]
    copy = pltpu.make_async_copy(weight, held, sem)
    copy.start()
    copy.wait()


def _merge_kernel(half, blocks, late, first, info, *refs):
    own, other, weight = refs[: 2 * blocks], refs[2 * blocks : 4 * blocks], refs[4 * blocks]
    mine = info[0]
    here = pl.ds(pl.multiple_of(mine * half, half), half)
    there = pl.ds(pl.multiple_of((1 - mine) * half, half), half)

    def rows(these, k):
        found = [these[2 * i + k // 2][k % 2] for i in range(blocks)]
        return found[0] if blocks == 1 else jnp.concatenate(found, axis=0)

    part = None
    for k in range(4):
        more = _dot(rows(own, k), weight[k, here, :]) + _dot(rows(other, k), weight[k, there, :])
        part = more if part is None else part + more
    if late is None:
        refs[-1][...] = part.astype(BF)
        return
    near, next_to = refs[4 * blocks + 1], refs[4 * blocks + 2]
    second = info[1] > 0 if late == 0 else info[1] == 0
    found = pl.ds(first, part.shape[0])
    part = part + jnp.where(second, next_to[found, :], near[found, :]).astype(F32)
    refs[-1][...] = part
    refs[-2][...] = part.astype(BF)


def _hits(info, where_to, first, count, rows):
    index = lax.broadcasted_iota(jnp.int32, (rows, count), 0) + info[3] * rows
    return (index == where_to[:, first : first + count]).astype(F32)


def _early_kernel(parts, late, info, where_to, *refs):
    text, out, spots = refs[parts], refs[-2], refs[-1]
    projected = jnp.concatenate([ref[...] for ref in refs[:parts]], axis=0)
    rows = out.shape[0]
    to_come = _hits(info, where_to, 0, late, rows)
    hit = _hits(info, where_to, late, projected.shape[0], rows)
    image = _dot(hit.astype(BF), projected).astype(BF)
    taken = jnp.max(hit, axis=1, keepdims=True) + jnp.max(to_come, axis=1, keepdims=True)
    out[...] = jnp.where(taken > 0, image, text[...])
    spots[...] = to_come.astype(BF)


def _late_kernel(parts, base, spots, *refs):
    projected = jnp.concatenate([ref[...] for ref in refs[:parts]], axis=0)
    refs[-1][...] = (_dot(spots[...], projected) + base[...].astype(F32)).astype(BF)


def _place_kernel(parts, info, where_to, *refs):
    text, out = refs[parts], refs[-1]
    projected = jnp.concatenate([ref[...] for ref in refs[:parts]], axis=0)
    hit = _hits(info, where_to, 0, projected.shape[0], out.shape[0])
    image = _dot(hit.astype(BF), projected).astype(BF)
    out[...] = jnp.where(jnp.max(hit, axis=1, keepdims=True) > 0, image, text[...])


HBM = pl.BlockSpec(memory_space=pltpu.HBM)
VMEM = pl.BlockSpec(memory_space=pltpu.VMEM)
SMEM = pl.BlockSpec(memory_space=pltpu.SMEM)


def build(rows, cols):
    def swap(x, axis, bit):
        size = rows if axis == "row" else cols
        return lax.ppermute(x, axis, [(i, i ^ bit) for i in range(size)])

    def per_device(hidden, down_weight, tokens, layer_scale, merge_weight, text_embeds, positions):
        patches, depth = hidden.shape
        width = down_weight.shape[1]
        half = width // 2
        merged_rows = patches // 4
        dec = merge_weight.shape[2]
        row, col = lax.axis_index("row"), lax.axis_index("col")
        mine = row % 2
        inner = (col == 1) | (col == 2)
        low = col < 2
        near, far = jnp.where(low, 2, 1), jnp.where(low, 3, 0)
        info = jnp.stack([mine, inner.astype(jnp.int32), 1 - col % 2, col, col ^ 1, near, far])
        scale = layer_scale[None, :]
        row_bits = [1 << i for i in range(1, rows.bit_length() - 1)]
        after = []

        def stay(x):
            return pltpu.with_memory_space_constraint(x, pltpu.VMEM)

        def hold():
            held = pl.pallas_call(
                _hold_kernel,
                out_shape=_near(merge_weight.shape, BF),
                in_specs=[HBM] + [ANY] * len(after),
                out_specs=VMEM,
                scratch_shapes=[pltpu.SemaphoreType.DMA],
                cost_estimate=LITTLE,
                compiler_params=pltpu.CompilerParams(vmem_limit_bytes=ROOM),
                name="hold",
            )(pltpu.with_memory_space_constraint(merge_weight, pltpu.HBM), *after)
            after[:] = [held]
            return held

        def residuals(pieces):
            copies = pl.pallas_call(
                functools.partial(_residual_kernel, half, pieces),
                out_shape=tuple(_near((count, half), BF) for _, _, count in pieces),
                in_specs=[SMEM, HBM] + [ANY] * len(after),
                out_specs=(VMEM,) * len(pieces),
                scratch_shapes=[pltpu.SemaphoreType.DMA((len(pieces),))],
                cost_estimate=LITTLE,
                compiler_params=pltpu.CompilerParams(vmem_limit_bytes=ROOM),
                name="residuals",
            )(info, pltpu.with_memory_space_constraint(tokens, pltpu.HBM), *after)
            after[:] = [copies[0]]
            return copies

        def relay(block, first, count):
            same = pl.pallas_call(
                functools.partial(_relay_kernel, first),
                out_shape=_near((count, depth), BF),
                in_specs=[VMEM] + [ANY] * len(after),
                out_specs=VMEM,
                cost_estimate=LITTLE,
                compiler_params=pltpu.CompilerParams(vmem_limit_bytes=ROOM),
                name="relay",
            )(block, *after)
            after[:] = [same]
            return same

        def down(*blocks, parts=2):
            count = blocks[0].shape[0]
            *gives, keep = pl.pallas_call(
                functools.partial(_down_kernel, half, len(blocks), len(after)),
                out_shape=(_near((count // parts, half), BF),) * parts + (_near((count, half), F32),),
                in_specs=[SMEM] + [VMEM] * (len(blocks) + 1) + [ANY] * len(after),
                out_specs=(VMEM,) * (parts + 1),
                cost_estimate=LITTLE,
                compiler_params=pltpu.CompilerParams(vmem_limit_bytes=ROOM),
                name="down",
            )(info, *blocks, down_weight, *after)
            after[:] = [gives[0]]
            return tuple(gives), keep

        def add(total, came, *rows):
            counts = rows or (total.shape[0],)
            came = came if isinstance(came, tuple) else (came,)
            give = pl.pallas_call(
                functools.partial(_add_kernel, len(came), len(counts)),
                out_shape=tuple(_near((n, total.shape[1]), BF) for n in counts),
                in_specs=[VMEM] * (1 + len(came)) + [ANY] * len(after),
                out_specs=tuple(VMEM for _ in counts),
                cost_estimate=LITTLE,
                compiler_params=pltpu.CompilerParams(vmem_limit_bytes=ROOM),
                name="add",
            )(stay(total), *came, *after)
            after[:] = [give[0]]
            return give if rows else give[0]

        def see(mine_parts, came_parts, residual):
            count = residual.shape[0]
            out = pl.pallas_call(
                functools.partial(_vision_kernel, len(mine_parts)),
                out_shape=(_near((2, count // 4, half), BF),) * 2,
                in_specs=[VMEM] * (2 * len(mine_parts) + 2) + [SMEM] + [ANY] * len(after),
                out_specs=(VMEM, VMEM),
                scratch_shapes=[pltpu.VMEM((half // 128, count, 128), F32)],
                cost_estimate=LITTLE,
                compiler_params=pltpu.CompilerParams(vmem_limit_bytes=ROOM),
                name="vision",
            )(*mine_parts, *came_parts, stay(residual), scale, info, *after)
            after[:] = [out[0]]
            return tuple(out)

        def merge(own, other, weight, came=None, late=None, first=0):
            count = own[0].shape[1] * (len(own) // 2)
            extra = [] if came is None else list(came)
            outs = [_near((count, dec), BF)] + [_near((count, dec), F32)] * (len(extra) // 2)
            given = pl.pallas_call(
                functools.partial(_merge_kernel, half, len(own) // 2, late, first),
                out_shape=tuple(outs),
                in_specs=[SMEM] + [VMEM] * (2 * len(own) + 1 + len(extra)) + [ANY] * len(after),
                out_specs=(VMEM,) * len(outs),
                cost_estimate=LITTLE,
                compiler_params=pltpu.CompilerParams(vmem_limit_bytes=ROOM),
                name="merge",
            )(info, *own, *other, stay(weight), *extra, *after)
            after[:] = [given[0]]
            return given[0] if came is None else given

        def place(parts, where_to):
            return pl.pallas_call(
                functools.partial(_place_kernel, len(parts)),
                out_shape=jax.ShapeDtypeStruct(text_embeds.shape, BF),
                in_specs=[SMEM, VMEM] + [VMEM] * (len(parts) + 1) + [ANY] * len(after),
                out_specs=VMEM,
                cost_estimate=LITTLE,
                compiler_params=pltpu.CompilerParams(vmem_limit_bytes=ROOM),
                name="place",
            )(info, where_to, *parts, text_embeds, *after)

        def place_early(parts, late, where_to):
            base, spots = pl.pallas_call(
                functools.partial(_early_kernel, len(parts), late),
                out_shape=(_near(text_embeds.shape, BF), _near((text_embeds.shape[0], late), BF)),
                in_specs=[SMEM, VMEM] + [VMEM] * (len(parts) + 1) + [ANY] * len(after),
                out_specs=(VMEM, VMEM),
                cost_estimate=LITTLE,
                compiler_params=pltpu.CompilerParams(vmem_limit_bytes=ROOM),
                name="place_early",
            )(info, where_to, *parts, text_embeds, *after)
            after[:] = [spots]
            return base, spots

        def place_late(base, spots, parts):
            return pl.pallas_call(
                functools.partial(_late_kernel, len(parts)),
                out_shape=jax.ShapeDtypeStruct(text_embeds.shape, BF),
                in_specs=[VMEM] * (len(parts) + 2) + [ANY] * len(after),
                out_specs=VMEM,
                cost_estimate=LITTLE,
                compiler_params=pltpu.CompilerParams(vmem_limit_bytes=ROOM),
                name="place_late",
            )(stay(base), stay(spots), *parts, *after)

        if cols != 4:
            held = hold()
            parts = jnp.zeros((cols * merged_rows, dec), F32)
            for step in range(cols):
                block = hidden if step == 0 else swap(hidden, "col", step)
                owner = jnp.bitwise_xor(col, step)
                give, total = down(block)
                came = tuple(swap(part, "row", 1) for part in give)
                for bit in row_bits:
                    total = add(total, came)
                    came = swap(total, "row", bit)
                residual = lax.dynamic_slice(tokens, (owner * patches, mine * half), (patches, half))
                own = see([total], [came], residual)
                part = merge(own, tuple(swap(v, "row", 1) for v in own), held).astype(F32)
                parts = lax.dynamic_update_slice(parts, part, (owner * merged_rows, 0))
            return place([lax.psum(parts, "col").astype(BF)], positions[None, :])

        between, outward = [(1, 2), (2, 1)], [(1, 0), (2, 3)]
        bit_x, bit_y = (row_bits + row_bits)[:2] if row_bits else (1, 1)

        def x(give):
            return swap(give, "row", bit_x)

        def y(give):
            return swap(give, "row", bit_y)

        def core(parts):
            return tuple(swap(part, "row", 1) for part in parts)

        def pairs(give):
            return swap(give, "col", 1)

        def halves(give):
            return swap(give, "col", 2)

        at = [positions[i * merged_rows : (i + 1) * merged_rows] for i in range(4)]
        where_to = jnp.concatenate(
            [
                jnp.where(low, at[1], at[2]),
                jnp.where(low, at[0], at[3]),
                jnp.where(low, at[2], at[1]),
                jnp.where(low, at[3], at[0]),
            ]
        )[None, :]
        after.extend([scale, where_to])
        cut = CUT * patches // 7 if CUT else patches
        pieces = [(i, 0, patches) for i in range(3)] + [(3, 0, cut)]
        pieces += [(3, cut, patches - cut)] if CUT else []
        last = len(pieces)
        v = {}
        v["hop_a"] = swap(hidden, "col", 1)
        v["hop_b"] = lax.ppermute(hidden, "col", between)
        v["hop_c"] = lax.ppermute(v["hop_b"], "col", outward)
        v["hop_d"] = lax.ppermute(v["hop_a"], "col", between)

        def send_on(i):
            v["mid", i] = relay(v["hop_d"], *pieces[i][1:])
            v["hop", i] = lax.ppermute(v["mid", i], "col", outward)

        def send_down(i):
            if i < 3:
                blocks = [[hidden], [v["hop_a"]], [v["hop_b"], v["hop_c"]]][i]
            else:
                blocks = [v["mid", i], v["hop", i]]
            give, v["keep", i] = down(*blocks, parts=PARTS[i])
            v["core", i] = core(give)

        def first_sum(i):
            if i in SPLIT:
                count = pieces[i][2]
                v["sum", i] = add(v["keep", i], v["core", i], count // 2, count // 2)
                v["in", i] = [x(v["sum", i][0]), y(v["sum", i][1])]
            else:
                v["sum", i] = [add(v["keep", i], v["core", i])]
                v["in", i] = [x(v["sum", i][0])]
            v["turn", i], v["back", i] = [], []

        def second_sum(i):
            j = len(v["turn", i])
            v["turn", i].append(add(v["sum", i][j], v["in", i][j]))
            v["back", i].append((x if j else y)(v["turn", i][j]))

        def look(i):
            seen = see(v["turn", i], v["back", i], v["residual"][i])
            v["seen", i], v["other", i] = seen, core(seen)

        def project(i):
            if i < 2:
                v["far", i] = halves(merge(v["seen", i], v["other", i], v["held"]))
            else:
                block, first, _ = pieces[i]
                late = block - 2, first // 4
                give, v["part", i] = merge(v["seen", i], v["other", i], v["held"], (v["far", 0], v["far", 1]), *late)
                v["pair", i] = pairs(give)

        def complete(i):
            v["away", i] = add(v["part", i], v["pair", i])
            v["own", i] = halves(v["away", i])

        def others(name):
            if name == "hold":
                v["held"] = hold()
            elif name == "residual":
                v["residual"] = residuals(pieces)
            elif name == "early":
                v["base"] = place_early([v["away", i] for i in range(2, last)], 2 * merged_rows, where_to)

        calls = {
            "hop": send_on,
            "down": send_down,
            "sum": first_sum,
            "turn": second_sum,
            "see": look,
            "merge": project,
            "done": complete,
        }
        for step in ORDER:
            name, _, waits = step.partition(":")
            for wait in waits.split(",") if waits else ():
                after.append(v[wait if wait.startswith("hop_") else (wait[:-1], int(wait[-1]))])
            if name[:-1] in calls:
                calls[name[:-1]](int(name[-1]))
            else:
                others(name)
        return place_late(*v["base"], [v["own", i] for i in range(2, last)])

    return per_device


def solution(mesh):
    in_specs = (
        P("col", "row"),
        P("row", "col"),
        P(None, "col"),
        P("col"),
        P(None, "col", "row"),
        P("col", "row"),
        P(),
    )
    out_specs = P("col", "row")
    return jax.shard_map(
        build(mesh.shape["row"], mesh.shape["col"]),
        mesh=mesh,
        in_specs=in_specs,
        out_specs=out_specs,
        check_vma=False,
    )
```

time: 277 us -> 115 us (0.42)
  waiting for transfers between devices: 216 us -> 55.7 us
  starting transfers between devices: 0.08 us -> 31 us
  Pallas kernels: 0 us -> 22.8 us
  matrix products: 15.8 us -> 0 us
  blocking collectives: 15.5 us -> 0 us
  between operations: 13.1 us -> 0.36 us
  other arithmetic: 8.59 us -> 0.98 us
  local copies, waits for them, and re-layouts: 7.51 us -> 3.55 us
    psum x1 -> x0, waiting for transfers between devices: 114 us -> none  [per_device(): row_total = lax.psum(partial_term, 'row')]
    all_gather x1 -> x0, waiting for transfers between devices: 76.5 us -> none  [per_device(): gathered = lax.all_gather(hidden, 'col', axis=0, tiled=True)]
    ppermute x0 -> x39, waiting for transfers between devices: none -> 55.7 us  [the longest x35 47.8 us: swap(): return lax.ppermute(x, axis, [(i, i ^ bit) for i in range(size)])]
    ppermute x0 -> x39, starting transfers between devices: none -> 31 us  [the longest x35 27 us: swap(): return lax.ppermute(x, axis, [(i, i ^ bit) for i in range(size)])]
    reduce_scatter x1 -> x0, waiting for transfers between devices: 25.1 us -> none  [per_device(): lax.psum_scatter(jnp.dot(merged, merge_flat, preferred_element_type=jnp.f...]
    pallas_call x0 -> x29, Pallas kernels: none -> 22.8 us  [the longest x4 6.65 us: down(): pl.pallas_call(functools.partial(_down_kernel, half, len(blocks), len(aft...]
    dot_general x3 -> x0, matrix products: 15.8 us -> none  [the longest x1 8.11 us: per_device(): jnp.dot(gathered, down_weight, preferred_element_type=jnp.float32)]
    all_gather x1 -> x0, blocking collectives: 15.5 us -> none  [per_device(): every_proj = lax.all_gather(projected, 'col', axis=0, tiled=True)]
  transfers between devices with their start and end apart: 3 -> 39, of which waited for: 3 -> 23; matrix products, arithmetic and copies ran while one was open for 0% -> 2% of each run, Pallas kernels for 0% -> 18%
where the time goes in v2:
time: 115 us; the launch traced here: 114 us
  waiting for transfers between devices  55.7 us (48%)
  starting transfers between devices  31 us (27%)
  Pallas kernels  22.8 us (20%)
  local copies, waits for them, and re-layouts  3.55 us (3%)
    ppermute x35, waiting for transfers between devices, swap(): return lax.ppermute(x, axis, [(i, i ^ bit) for i in range(size)])  47.8 us
    ppermute x35, starting transfers between devices, swap(): return lax.ppermute(x, axis, [(i, i ^ bit) for i in range(size)])  27 us
    ppermute x1, waiting for transfers between devices, per_device(): v['hop_c'] = lax.ppermute(v['hop_b'], 'col', outward)  6.77 us
    pallas_call x4, Pallas kernels, down(): pl.pallas_call(functools.partial(_down_kernel, half, len(blocks), len(aft...  6.65 us
    pallas_call x4, Pallas kernels, merge(): pl.pallas_call(functools.partial(_merge_kernel, half, len(own) // 2, late...  5.2 us
    pallas_call x4, Pallas kernels, see(): pl.pallas_call(functools.partial(_vision_kernel, len(mine_parts)), out_sh...  3.73 us
    unnamed x8, local copies, waits for them, and re-layouts  2.78 us
  transfers between devices with their start and end apart: 39, of which 23 were waited for; matrix products, arithmetic and copies ran while one was open for 2% of the time, Pallas kernels for 18%

profile of v2, /device:TPU:0, one launch (start us, length us, event | category | flops | bytes accessed | tf_op | source)
XLA Modules:
  0.0 114.4 jit_solution(859658680176490105)
XLA Ops:
  0.0 3.0 %collective-permute-start.2 = (bf16[448,1024]{1,0:T(8,128)(2,1)}, bf16[448,1024]{1,0:T(8,128)(2,1)S(1)}, u32[]{:S(2)}, u32[]{:S(2)}) collective-permute-start(bf16[448,1024]{1,0:T(8,128)(2,1)} %refs_0_.1), channel_id=1, source_target_pairs={{0,1},{1,0},{2,3},{3,2},{4,5},{5,4},{6,7},{7,6},{8,9},{9,8},{10,11... | collective-permute-start | bytes 2752520 | tf_op jit(solution)/shard_map/ppermute | solution.py:161
  4.5 0.9 broadcast_select_fusion.3
  5.5 1.6 %copy-done = bf16[1024,1024]{1,0:T(8,128)(2,1)S(1)} copy-done((bf16[1024,1024]{1,0:T(8,128)(2,1)S(1)}, bf16[1024,1024]{1,0:T(8,128)(2,1)}, u32[]{:S(2)}) %copy-start) | copy-done | bytes 2097176
  7.1 1.2 %copy-done.2 = bf16[448,1024]{1,0:T(8,128)(2,1)S(1)} copy-done((bf16[448,1024]{1,0:T(8,128)(2,1)S(1)}, bf16[448,1024]{1,0:T(8,128)(2,1)}, u32[]{:S(2)}) %copy-start.2) | copy-done | bytes 917528
  8.3 1.7 %down.4 = (bf16[224,512]{1,0:T(8,128)(2,1)S(1)}, bf16[224,512]{1,0:T(8,128)(2,1)S(1)}, f32[448,512]{1,0:T(8,128)S(1)}) custom-call(s32[7]{0:T(128)S(1)} %stack.35.info.refs_4_.refs_6_, bf16[448,1024]{1,0:T(8,128)(2,1)S(1)} %copy-done.2, bf16[1024,1024]{1,0:T(8,128)(2,1)S(1)} %copy-done, bf16[1,1024]{1,0:T(2,128)(2,1)S(1)} %broadcast_in_dim.7.refs_2_.refs_3_.refs_5_, ...), custom_call_target="tpu_custom_call" | custom-call | flops 1 | bytes 1 | tf_op jit(solution)/shard_map/down/pallas_call | solution.py:225
  10.5 1.0 collective-permute-done.4.refs_0_
  11.9 1.6 %collective-permute-start.6 = (bf16[448,512]{1,0:T(8,128)(2,1)S(1)}, bf16[448,512]{1,0:T(8,128)(2,1)S(1)}, u32[]{:S(2)}, u32[]{:S(2)}) collective-permute-start(bf16[448,512]{1,0:T(8,128)(2,1)S(1)} %add.27.mine.refs_1_), channel_id=1, source_target_pairs={{0,8},{4,12},{8,0},{12,4},{16,24},{20,28},{24,16},{28,20},{1,9},{5... | collective-permute-start | bytes 1376264 | tf_op jit(solution)/shard_map/ppermute | solution.py:161
  13.5 10.1 %collective-permute-done.2.refs_0_ = bf16[448,1024]{1,0:T(8,128)(2,1)S(1)} collective-permute-done((bf16[448,1024]{1,0:T(8,128)(2,1)}, bf16[448,1024]{1,0:T(8,128)(2,1)S(1)}, u32[]{:S(2)}, u32[]{:S(2)}) %collective-permute-start.2) | collective-permute-done | bytes 917536 | tf_op jit(solution)/shard_map/ppermute | solution.py:161
  24.3 1.3 %collective-permute-start.1 = (bf16[448,1024]{1,0:T(8,128)(2,1)S(1)}, bf16[448,1024]{1,0:T(8,128)(2,1)S(1)}, u32[]{:S(2)}, u32[]{:S(2)}) collective-permute-start(bf16[448,1024]{1,0:T(8,128)(2,1)S(1)} %collective-permute-done.refs_3_.refs_0_), channel_id=1, source_target_pairs={{1,0},{2,3},{5,4},{6,7},{9,8},{10,11},{13,12},{14,15},{17,16},{18,... | collective-permute-start | bytes 2752520 | tf_op jit(solution)/shard_map/ppermute | solution.py:370
  25.7 1.8 %collective-permute-start.7 = (bf16[448,512]{1,0:T(8,128)(2,1)S(1)}, bf16[448,512]{1,0:T(8,128)(2,1)S(1)}, u32[]{:S(2)}, u32[]{:S(2)}) collective-permute-start(bf16[448,512]{1,0:T(8,128)(2,1)S(1)} %add.28.refs_2_.refs_0_), channel_id=1, source_target_pairs={{0,16},{4,20},{8,24},{12,28},{16,0},{20,4},{24,8},{28,12},{1,17},{... | collective-permute-start | bytes 1376264 | tf_op jit(solution)/shard_map/ppermute | solution.py:161
  27.5 1.7 %down.5 = (bf16[224,512]{1,0:T(8,128)(2,1)S(1)}, bf16[224,512]{1,0:T(8,128)(2,1)S(1)}, f32[448,512]{1,0:T(8,128)S(1)}) custom-call(s32[7]{0:T(128)S(1)} %stack.35.info.refs_4_.refs_6_, bf16[448,1024]{1,0:T(8,128)(2,1)S(1)} %collective-permute-done.2.refs_0_, bf16[1024,1024]{1,0:T(8,128)(2,1)S(1)} %copy-done.1, bf16[448,512]{1,0:T(8,128)(2,1)S(1)} %add.28.refs_2_.refs_0_, ...), custom_call_target="tpu_custom_call" | custom-call | flops 1 | bytes 1 | tf_op jit(solution)/shard_map/down/pallas_call | solution.py:225
  29.7 1.0 collective-permute-done.8.refs_0_
  31.1 1.6 %collective-permute-start.14 = (bf16[448,512]{1,0:T(8,128)(2,1)S(1)}, bf16[448,512]{1,0:T(8,128)(2,1)S(1)}, u32[]{:S(2)}, u32[]{:S(2)}) collective-permute-start(bf16[448,512]{1,0:T(8,128)(2,1)S(1)} %add.29.refs_0_.mine), channel_id=1, source_target_pairs={{0,8},{4,12},{8,0},{12,4},{16,24},{20,28},{24,16},{28,20},{1,9},{5... | collective-permute-start | bytes 1376264 | tf_op jit(solution)/shard_map/ppermute | solution.py:161
  32.7 2.0 %residuals.1 = (bf16[448,512]{1,0:T(8,128)(2,1)S(1)}, bf16[448,512]{1,0:T(8,128)(2,1)S(1)}, bf16[448,512]{1,0:T(8,128)(2,1)S(1)}, bf16[448,512]{1,0:T(8,128)(2,1)S(1)}) custom-call(s32[7]{0:T(128)S(1)} %stack.35.info.refs_4_.refs_6_, bf16[1792,1024]{1,0:T(8,128)(2,1)} %tokens.1, bf16[448,512]{1,0:T(8,128)(2,1)S(1)} %add.29.refs_0_.mine), custom_call_target="tpu_custom_call" | custom-call | flops 1 | bytes 1 | tf_op jit(solution)/shard_map/residuals/pallas_call | solution.py:197
  34.7 2.2 %hold.1.refs_5_.refs_4_ = bf16[4,1024,512]{2,1,0:T(8,128)(2,1)S(1)} custom-call(bf16[4,1024,512]{2,1,0:T(8,128)(2,1)} %weight.1, bf16[448,512]{1,0:T(8,128)(2,1)S(1)} %get-tuple-element.45.refs_0_.refs_2_), custom_call_target="tpu_custom_call" | custom-call | flops 1 | bytes 1 | tf_op jit(solution)/shard_map/hold/pallas_call | solution.py:183
  37.5 1.0 vision.4
  39.1 1.0 collective-permute-done.10.refs_2_
  40.4 1.3 %merge.4.refs_0_ = bf16[112,512]{1,0:T(8,128)(2,1)S(1)} custom-call(s32[7]{0:T(128)S(1)} %stack.35.info.refs_4_.refs_6_, bf16[2,112,512]{2,1,0:T(8,128)(2,1)S(1)} %get-tuple-element.46.refs_0_.refs_5_, bf16[2,112,512]{2,1,0:T(8,128)(2,1)S(1)} %get-tuple-element.47.refs_1_, bf16[2,112,512]{2,1,0:T(8,128)(2,1)S(1)} %collective-permute-done.10.refs_2_, ...), custom_call_target="tpu_custom_call" | custom-call | flops 1 | bytes 1 | tf_op jit(solution)/shard_map/merge/pallas_call | solution.py:271
  41.8 1.3 %collective-permute-start.21 = (bf16[448,1024]{1,0:T(8,128)(2,1)S(1)}, bf16[448,1024]{1,0:T(8,128)(2,1)S(1)}, u32[]{:S(2)}, u32[]{:S(2)}) collective-permute-start(bf16[448,1024]{1,0:T(8,128)(2,1)S(1)} %relay.1.refs_3_.refs_0_), channel_id=1, source_target_pairs={{1,0},{2,3},{5,4},{6,7},{9,8},{10,11},{13,12},{14,15},{17,16},{18,... | collective-permute-start | bytes 2752520 | tf_op jit(solution)/shard_map/ppermute | solution.py:375
  43.1 6.8 %collective-permute-done.1.refs_1_ = bf16[448,1024]{1,0:T(8,128)(2,1)S(1)} collective-permute-done((bf16[448,1024]{1,0:T(8,128)(2,1)S(1)}, bf16[448,1024]{1,0:T(8,128)(2,1)S(1)}, u32[]{:S(2)}, u32[]{:S(2)}) %collective-permute-start.1) | collective-permute-done | bytes 917536 | tf_op jit(solution)/shard_map/ppermute | solution.py:370
  49.8 1.7 %down.6 = (bf16[224,512]{1,0:T(8,128)(2,1)S(1)}, bf16[224,512]{1,0:T(8,128)(2,1)S(1)}, f32[448,512]{1,0:T(8,128)S(1)}) custom-call(s32[7]{0:T(128)S(1)} %stack.35.info.refs_4_.refs_6_, bf16[448,1024]{1,0:T(8,128)(2,1)S(1)} %collective-permute-done.refs_3_.refs_0_, bf16[448,1024]{1,0:T(8,128)(2,1)S(1)} %collective-permute-done.1.refs_1_, ...), custom_call_target="tpu_custom_call" | custom-call | flops 1 | bytes 1 | tf_op jit(solution)/shard_map/down/pallas_call | solution.py:225
  51.6 1.6 %collective-permute-start.16 = (bf16[448,512]{1,0:T(8,128)(2,1)S(1)}, bf16[448,512]{1,0:T(8,128)(2,1)S(1)}, u32[]{:S(2)}, u32[]{:S(2)}) collective-permute-start(bf16[448,512]{1,0:T(8,128)(2,1)S(1)} %add.30.refs_2_.refs_0_), channel_id=1, source_target_pairs={{0,16},{4,20},{8,24},{12,28},{16,0},{20,4},{24,8},{28,12},{1,17},{... | collective-permute-start | bytes 1376264 | tf_op jit(solution)/shard_map/ppermute | solution.py:161
  53.7 1.0 collective-permute-start.17
  55.2 1.6 %collective-permute-start.15 = (bf16[224,512]{1,0:T(8,128)(2,1)S(1)}, bf16[224,512]{1,0:T(8,128)(2,1)S(1)}, u32[]{:S(2)}, u32[]{:S(2)}) collective-permute-start(bf16[224,512]{1,0:T(8,128)(2,1)S(1)} %get-tuple-element.51.refs_5_.mine), channel_id=1, source_target_pairs={{0,8},{4,12},{8,0},{12,4},{16,24},{20,28},{24,16},{28,20},{1,9},{5... | collective-permute-start | bytes 688136 | tf_op jit(solution)/shard_map/ppermute | solution.py:161
  57.2 4.5 %collective-permute-done.17.refs_6_.refs_5_ = bf16[112,512]{1,0:T(8,128)(2,1)S(1)} collective-permute-done((bf16[112,512]{1,0:T(8,128)(2,1)S(1)}, bf16[112,512]{1,0:T(8,128)(2,1)S(1)}, u32[]{:S(2)}, u32[]{:S(2)}) %collective-permute-start.17) | collective-permute-done | bytes 114720 | tf_op jit(solution)/shard_map/ppermute | solution.py:161
  61.7 2.2 %collective-permute-done.16.refs_1_ = bf16[448,512]{1,0:T(8,128)(2,1)S(1)} collective-permute-done((bf16[448,512]{1,0:T(8,128)(2,1)S(1)}, bf16[448,512]{1,0:T(8,128)(2,1)S(1)}, u32[]{:S(2)}, u32[]{:S(2)}) %collective-permute-start.16) | collective-permute-done | bytes 458784 | tf_op jit(solution)/shard_map/ppermute | solution.py:161
  64.0 1.0 vision.5
  65.6 1.7 %collective-permute-start.19 = (bf16[224,512]{1,0:T(8,128)(2,1)S(1)}, bf16[224,512]{1,0:T(8,128)(2,1)S(1)}, u32[]{:S(2)}, u32[]{:S(2)}) collective-permute-start(bf16[224,512]{1,0:T(8,128)(2,1)S(1)} %add.32.refs_1_.refs_0_), channel_id=1, source_target_pairs={{0,16},{4,20},{8,24},{12,28},{16,0},{20,4},{24,8},{28,12},{1,17},{... | collective-permute-start | bytes 688136 | tf_op jit(solution)/shard_map/ppermute | solution.py:161
  67.4 1.6 %collective-permute-start.20 = (bf16[224,512]{1,0:T(8,128)(2,1)S(1)}, bf16[224,512]{1,0:T(8,128)(2,1)S(1)}, u32[]{:S(2)}, u32[]{:S(2)}) collective-permute-start(bf16[224,512]{1,0:T(8,128)(2,1)S(1)} %add.33.refs_5_.refs_1_), channel_id=1, source_target_pairs={{0,8},{4,12},{8,0},{12,4},{16,24},{20,28},{24,16},{28,20},{1,9},{5... | collective-permute-start | bytes 688136 | tf_op jit(solution)/shard_map/ppermute | solution.py:161
  68.9 1.3 %merge.5.refs_3_ = bf16[112,512]{1,0:T(8,128)(2,1)S(1)} custom-call(s32[7]{0:T(128)S(1)} %stack.35.info.refs_4_.refs_6_, bf16[2,112,512]{2,1,0:T(8,128)(2,1)S(1)} %get-tuple-element.53.refs_1_.refs_0_, bf16[2,112,512]{2,1,0:T(8,128)(2,1)S(1)} %get-tuple-element.56.refs_1_, bf16[2,112,512]{2,1,0:T(8,128)(2,1)S(1)} %collective-permute-done.22.refs_2_, ...), custom_call_target="tpu_custom_call" | custom-call | flops 1 | bytes 1 | tf_op jit(solution)/shard_map/merge/pallas_call | solution.py:271
  70.2 1.2 %collective-permute-done.21.refs_1_ = bf16[448,1024]{1,0:T(8,128)(2,1)S(1)} collective-permute-done((bf16[448,1024]{1,0:T(8,128)(2,1)S(1)}, bf16[448,1024]{1,0:T(8,128)(2,1)S(1)}, u32[]{:S(2)}, u32[]{:S(2)}) %collective-permute-start.21) | collective-permute-done | bytes 917536 | tf_op jit(solution)/shard_map/ppermute | solution.py:375
  71.4 1.7 %down.7 = (bf16[224,512]{1,0:T(8,128)(2,1)S(1)}, bf16[224,512]{1,0:T(8,128)(2,1)S(1)}, f32[448,512]{1,0:T(8,128)S(1)}) custom-call(s32[7]{0:T(128)S(1)} %stack.35.info.refs_4_.refs_6_, bf16[448,1024]{1,0:T(8,128)(2,1)S(1)} %relay.1.refs_3_.refs_0_, bf16[448,1024]{1,0:T(8,128)(2,1)S(1)} %collective-permute-done.21.refs_1_, bf16[1024,1024]{1,0:T(8,128)(2,1)S(1)} %copy-done.1, ...), custom_call_target="tpu_custom_call" | custom-call | flops 1 | bytes 1 | tf_op jit(solution)/shard_map/down/pallas_call | solution.py:225
  73.7 1.1 collective-permute-done.20.refs_3_
  75.7 1.6 %collective-permute-start.30 = (bf16[224,512]{1,0:T(8,128)(2,1)S(1)}, bf16[224,512]{1,0:T(8,128)(2,1)S(1)}, u32[]{:S(2)}, u32[]{:S(2)}) collective-permute-start(bf16[224,512]{1,0:T(8,128)(2,1)S(1)} %get-tuple-element.63.mine.refs_1_), channel_id=1, source_target_pairs={{0,8},{4,12},{8,0},{12,4},{16,24},{20,28},{24,16},{28,20},{1,9},{5... | collective-permute-start | bytes 688136 | tf_op jit(solution)/shard_map/ppermute | solution.py:161
  78.7 4.2 %collective-permute-done.30.refs_0_ = bf16[224,512]{1,0:T(8,128)(2,1)S(1)} collective-permute-done((bf16[224,512]{1,0:T(8,128)(2,1)S(1)}, bf16[224,512]{1,0:T(8,128)(2,1)S(1)}, u32[]{:S(2)}, u32[]{:S(2)}) %collective-permute-start.30) | collective-permute-done | bytes 229408 | tf_op jit(solution)/shard_map/ppermute | solution.py:161
  82.9 1.2 %collective-permute-done.29.refs_0_ = bf16[224,512]{1,0:T(8,128)(2,1)S(1)} collective-permute-done((bf16[224,512]{1,0:T(8,128)(2,1)S(1)}, bf16[224,512]{1,0:T(8,128)(2,1)S(1)}, u32[]{:S(2)}, u32[]{:S(2)}) %collective-permute-start.29) | collective-permute-done | bytes 229408 | tf_op jit(solution)/shard_map/ppermute | solution.py:161
  84.7 1.5 %collective-permute-start.32 = (bf16[224,512]{1,0:T(8,128)(2,1)S(1)}, bf16[224,512]{1,0:T(8,128)(2,1)S(1)}, u32[]{:S(2)}, u32[]{:S(2)}) collective-permute-start(bf16[224,512]{1,0:T(8,128)(2,1)S(1)} %add.35.refs_1_.refs_0_), channel_id=1, source_target_pairs={{0,16},{4,20},{8,24},{12,28},{16,0},{20,4},{24,8},{28,12},{1,17},{... | collective-permute-start | bytes 688136 | tf_op jit(solution)/shard_map/ppermute | solution.py:161
  86.4 6.3 %collective-permute-done.26.refs_6_ = bf16[112,512]{1,0:T(8,128)(2,1)S(1)} collective-permute-done((bf16[112,512]{1,0:T(8,128)(2,1)S(1)}, bf16[112,512]{1,0:T(8,128)(2,1)S(1)}, u32[]{:S(2)}, u32[]{:S(2)}) %collective-permute-start.26) | collective-permute-done | bytes 114720 | tf_op jit(solution)/shard_map/ppermute | solution.py:161
  92.7 1.3 %merge.6 = (bf16[112,512]{1,0:T(8,128)(2,1)S(1)}, f32[112,512]{1,0:T(8,128)S(1)}) custom-call(s32[7]{0:T(128)S(1)} %stack.35.info.refs_4_.refs_6_, bf16[2,112,512]{2,1,0:T(8,128)(2,1)S(1)} %get-tuple-element.58.refs_2_.refs_0_, bf16[2,112,512]{2,1,0:T(8,128)(2,1)S(1)} %get-tuple-element.59.refs_1_, bf16[2,112,512]{2,1,0:T(8,128)(2,1)S(1)} %collective-permute-done.24.refs_2_, ...), custom_call_target="tpu_custom_call" | custom-call | flops 1 | bytes 1 | tf_op jit(solution)/shard_map/merge/pallas_call | solution.py:271
  94.1 0.9 vision.7
  95.5 1.0 collective-permute-done.34.refs_2_
  96.8 1.3 %merge.7 = (bf16[112,512]{1,0:T(8,128)(2,1)S(1)}, f32[112,512]{1,0:T(8,128)S(1)}) custom-call(s32[7]{0:T(128)S(1)} %stack.35.info.refs_4_.refs_6_, bf16[2,112,512]{2,1,0:T(8,128)(2,1)S(1)} %get-tuple-element.67.refs_0_.refs_7_, bf16[2,112,512]{2,1,0:T(8,128)(2,1)S(1)} %get-tuple-element.68.refs_1_, bf16[2,112,512]{2,1,0:T(8,128)(2,1)S(1)} %collective-permute-done.34.refs_2_, ...), custom_call_target="tpu_custom_call" | custom-call | flops 1 | bytes 1 | tf_op jit(solution)/shard_map/merge/pallas_call | solution.py:271
  98.9 1.7 %collective-permute-done.31.refs_0_ = bf16[112,512]{1,0:T(8,128)(2,1)S(1)} collective-permute-done((bf16[112,512]{1,0:T(8,128)(2,1)S(1)}, bf16[112,512]{1,0:T(8,128)(2,1)S(1)}, u32[]{:S(2)}, u32[]{:S(2)}) %collective-permute-start.31) | collective-permute-done | bytes 114720 | tf_op jit(solution)/shard_map/ppermute | solution.py:161
  101.3 2.2 %collective-permute-done.36.refs_0_ = bf16[112,512]{1,0:T(8,128)(2,1)S(1)} collective-permute-done((bf16[112,512]{1,0:T(8,128)(2,1)S(1)}, bf16[112,512]{1,0:T(8,128)(2,1)S(1)}, u32[]{:S(2)}, u32[]{:S(2)}) %collective-permute-start.36) | collective-permute-done | bytes 114720 | tf_op jit(solution)/shard_map/ppermute | solution.py:161
  104.1 1.0 place_early.1
  105.1 6.0 %collective-permute-done.37.refs_0_ = bf16[112,512]{1,0:T(8,128)(2,1)S(1)} collective-permute-done((bf16[112,512]{1,0:T(8,128)(2,1)S(1)}, bf16[112,512]{1,0:T(8,128)(2,1)S(1)}, u32[]{:S(2)}, u32[]{:S(2)}) %collective-permute-start.37) | collective-permute-done | bytes 114720 | tf_op jit(solution)/shard_map/ppermute | solution.py:161
  111.0 2.2 %collective-permute-done.38.refs_1_ = bf16[112,512]{1,0:T(8,128)(2,1)S(1)} collective-permute-done((bf16[112,512]{1,0:T(8,128)(2,1)S(1)}, bf16[112,512]{1,0:T(8,128)(2,1)S(1)}, u32[]{:S(2)}, u32[]{:S(2)}) %collective-permute-start.38) | collective-permute-done | bytes 114720 | tf_op jit(solution)/shard_map/ppermute | solution.py:161
  113.3 1.1 place_late.1
  (71 shorter events, 14.9 us)
Async XLA Ops:
  0.0 23.6 %collective-permute-start.2 = (bf16[448,1024]{1,0:T(8,128)(2,1)}, bf16[448,1024]{1,0:T(8,128)(2,1)S(1)}, u32[]{:S(2)}, u32[]{:S(2)}) collective-permute-start(bf16[448,1024]{1,0:T(8,128)(2,1)} %refs_0_.1), channel_id=1, source_target_pairs={{0,1},{1,0},{2,3},{3,2},{4,5},{5,4},{6,7},{7,6},{8,9},{9,8},{10,11... | collective-permute-start | bytes 2752520 | tf_op jit(solution)/shard_map/ppermute | solution.py:161
  3.0 21.3 %collective-permute-start = (bf16[448,1024]{1,0:T(8,128)(2,1)}, bf16[448,1024]{1,0:T(8,128)(2,1)S(1)}, u32[]{:S(2)}, u32[]{:S(2)}) collective-permute-start(bf16[448,1024]{1,0:T(8,128)(2,1)} %refs_0_.1), channel_id=1, source_target_pairs={{1,2},{2,1},{5,6},{6,5},{9,10},{10,9},{13,14},{14,13},{17,18},{18,... | collective-permute-start | bytes 2752520 | tf_op jit(solution)/shard_map/ppermute | solution.py:369
  5.5 1.6 %copy-start = (bf16[1024,1024]{1,0:T(8,128)(2,1)S(1)}, bf16[1024,1024]{1,0:T(8,128)(2,1)}, u32[]{:S(2)}) copy-start(bf16[1024,1024]{1,0:T(8,128)(2,1)} %refs_2_.4) | copy-start | bytes 6291460
  7.1 1.2 %copy-start.2 = (bf16[448,1024]{1,0:T(8,128)(2,1)S(1)}, bf16[448,1024]{1,0:T(8,128)(2,1)}, u32[]{:S(2)}) copy-start(bf16[448,1024]{1,0:T(8,128)(2,1)} %refs_0_.1) | copy-start | bytes 2752516
  8.3 19.2 %copy-start.1 = (bf16[1024,1024]{1,0:T(8,128)(2,1)S(1)}, bf16[1024,1024]{1,0:T(8,128)(2,1)}, u32[]{:S(2)}) copy-start(bf16[1024,1024]{1,0:T(8,128)(2,1)} %refs_2_.4) | copy-start | bytes 6291460
  10.0 1.6 %collective-permute-start.4 = (bf16[224,512]{1,0:T(8,128)(2,1)S(1)}, bf16[224,512]{1,0:T(8,128)(2,1)S(1)}, u32[]{:S(2)}, u32[]{:S(2)}) collective-permute-start(bf16[224,512]{1,0:T(8,128)(2,1)S(1)} %get-tuple-element.40.refs_2_), channel_id=1, source_target_pairs={{0,4},{4,0},{8,12},{12,8},{16,20},{20,16},{24,28},{28,24},{1,5},{5... | collective-permute-start | bytes 688136 | tf_op jit(solution)/shard_map/ppermute | solution.py:161
  10.0 1.8 %collective-permute-start.5 = (bf16[224,512]{1,0:T(8,128)(2,1)S(1)}, bf16[224,512]{1,0:T(8,128)(2,1)S(1)}, u32[]{:S(2)}, u32[]{:S(2)}) collective-permute-start(bf16[224,512]{1,0:T(8,128)(2,1)S(1)} %get-tuple-element.41), channel_id=1, source_target_pairs={{0,4},{4,0},{8,12},{12,8},{16,20},{20,16},{24,28},{28,24},{1,5},{5... | collective-permute-start | bytes 688136 | tf_op jit(solution)/shard_map/ppermute | solution.py:161
  11.9 13.7 %collective-permute-start.6 = (bf16[448,512]{1,0:T(8,128)(2,1)S(1)}, bf16[448,512]{1,0:T(8,128)(2,1)S(1)}, u32[]{:S(2)}, u32[]{:S(2)}) collective-permute-start(bf16[448,512]{1,0:T(8,128)(2,1)S(1)} %add.27.mine.refs_1_), channel_id=1, source_target_pairs={{0,8},{4,12},{8,0},{12,4},{16,24},{20,28},{24,16},{28,20},{1,9},{5... | collective-permute-start | bytes 1376264 | tf_op jit(solution)/shard_map/ppermute | solution.py:161
  23.6 18.1 %collective-permute-start.3 = (bf16[448,1024]{1,0:T(8,128)(2,1)S(1)}, bf16[448,1024]{1,0:T(8,128)(2,1)S(1)}, u32[]{:S(2)}, u32[]{:S(2)}) collective-permute-start(bf16[448,1024]{1,0:T(8,128)(2,1)S(1)} %collective-permute-done.2.refs_0_), channel_id=1, source_target_pairs={{1,2},{2,1},{5,6},{6,5},{9,10},{10,9},{13,14},{14,13},{17,18},{18,... | collective-permute-start | bytes 2752520 | tf_op jit(solution)/shard_map/ppermute | solution.py:371
  24.3 25.5 %collective-permute-start.1 = (bf16[448,1024]{1,0:T(8,128)(2,1)S(1)}, bf16[448,1024]{1,0:T(8,128)(2,1)S(1)}, u32[]{:S(2)}, u32[]{:S(2)}) collective-permute-start(bf16[448,1024]{1,0:T(8,128)(2,1)S(1)} %collective-permute-done.refs_3_.refs_0_), channel_id=1, source_target_pairs={{1,0},{2,3},{5,4},{6,7},{9,8},{10,11},{13,12},{14,15},{17,16},{18,... | collective-permute-start | bytes 2752520 | tf_op jit(solution)/shard_map/ppermute | solution.py:370
  25.7 11.8 %collective-permute-start.7 = (bf16[448,512]{1,0:T(8,128)(2,1)S(1)}, bf16[448,512]{1,0:T(8,128)(2,1)S(1)}, u32[]{:S(2)}, u32[]{:S(2)}) collective-permute-start(bf16[448,512]{1,0:T(8,128)(2,1)S(1)} %add.28.refs_2_.refs_0_), channel_id=1, source_target_pairs={{0,16},{4,20},{8,24},{12,28},{16,0},{20,4},{24,8},{28,12},{1,17},{... | collective-permute-start | bytes 1376264 | tf_op jit(solution)/shard_map/ppermute | solution.py:161
  29.2 1.6 %collective-permute-start.8 = (bf16[224,512]{1,0:T(8,128)(2,1)S(1)}, bf16[224,512]{1,0:T(8,128)(2,1)S(1)}, u32[]{:S(2)}, u32[]{:S(2)}) collective-permute-start(bf16[224,512]{1,0:T(8,128)(2,1)S(1)} %get-tuple-element.43.refs_2_), channel_id=1, source_target_pairs={{0,4},{4,0},{8,12},{12,8},{16,20},{20,16},{24,28},{28,24},{1,5},{5... | collective-permute-start | bytes 688136 | tf_op jit(solution)/shard_map/ppermute | solution.py:161
  29.2 1.8 %collective-permute-start.9 = (bf16[224,512]{1,0:T(8,128)(2,1)S(1)}, bf16[224,512]{1,0:T(8,128)(2,1)S(1)}, u32[]{:S(2)}, u32[]{:S(2)}) collective-permute-start(bf16[224,512]{1,0:T(8,128)(2,1)S(1)} %get-tuple-element.44), channel_id=1, source_target_pairs={{0,4},{4,0},{8,12},{12,8},{16,20},{20,16},{24,28},{28,24},{1,5},{5... | collective-permute-start | bytes 688136 | tf_op jit(solution)/shard_map/ppermute | solution.py:161
  31.1 20.4 %collective-permute-start.14 = (bf16[448,512]{1,0:T(8,128)(2,1)S(1)}, bf16[448,512]{1,0:T(8,128)(2,1)S(1)}, u32[]{:S(2)}, u32[]{:S(2)}) collective-permute-start(bf16[448,512]{1,0:T(8,128)(2,1)S(1)} %add.29.refs_0_.mine), channel_id=1, source_target_pairs={{0,8},{4,12},{8,0},{12,4},{16,24},{20,28},{24,16},{28,20},{1,9},{5... | collective-permute-start | bytes 1376264 | tf_op jit(solution)/shard_map/ppermute | solution.py:161
  38.5 1.6 %collective-permute-start.10 = (bf16[2,112,512]{2,1,0:T(8,128)(2,1)S(1)}, bf16[2,112,512]{2,1,0:T(8,128)(2,1)S(1)}, u32[]{:S(2)}, u32[]{:S(2)}) collective-permute-start(bf16[2,112,512]{2,1,0:T(8,128)(2,1)S(1)} %get-tuple-element.46.refs_0_.refs_5_), channel_id=1, source_target_pairs={{0,4},{4,0},{8,12},{12,8},{16,20},{20,16},{24,28},{28,24},{1,5},{5... | collective-permute-start | bytes 688136 | tf_op jit(solution)/shard_map/ppermute | solution.py:161
  38.6 1.8 %collective-permute-start.11 = (bf16[2,112,512]{2,1,0:T(8,128)(2,1)S(1)}, bf16[2,112,512]{2,1,0:T(8,128)(2,1)S(1)}, u32[]{:S(2)}, u32[]{:S(2)}) collective-permute-start(bf16[2,112,512]{2,1,0:T(8,128)(2,1)S(1)} %get-tuple-element.47.refs_1_), channel_id=1, source_target_pairs={{0,4},{4,0},{8,12},{12,8},{16,20},{20,16},{24,28},{28,24},{1,5},{5... | collective-permute-start | bytes 688136 | tf_op jit(solution)/shard_map/ppermute | solution.py:161
  41.8 29.6 %collective-permute-start.21 = (bf16[448,1024]{1,0:T(8,128)(2,1)S(1)}, bf16[448,1024]{1,0:T(8,128)(2,1)S(1)}, u32[]{:S(2)}, u32[]{:S(2)}) collective-permute-start(bf16[448,1024]{1,0:T(8,128)(2,1)S(1)} %relay.1.refs_3_.refs_0_), channel_id=1, source_target_pairs={{1,0},{2,3},{5,4},{6,7},{9,8},{10,11},{13,12},{14,15},{17,16},{18,... | collective-permute-start | bytes 2752520 | tf_op jit(solution)/shard_map/ppermute | solution.py:375
  51.6 12.3 %collective-permute-start.16 = (bf16[448,512]{1,0:T(8,128)(2,1)S(1)}, bf16[448,512]{1,0:T(8,128)(2,1)S(1)}, u32[]{:S(2)}, u32[]{:S(2)}) collective-permute-start(bf16[448,512]{1,0:T(8,128)(2,1)S(1)} %add.30.refs_2_.refs_0_), channel_id=1, source_target_pairs={{0,16},{4,20},{8,24},{12,28},{16,0},{20,4},{24,8},{28,12},{1,17},{... | collective-permute-start | bytes 1376264 | tf_op jit(solution)/shard_map/ppermute | solution.py:161
  53.2 1.5 %collective-permute-start.12 = (bf16[224,512]{1,0:T(8,128)(2,1)S(1)}, bf16[224,512]{1,0:T(8,128)(2,1)S(1)}, u32[]{:S(2)}, u32[]{:S(2)}) collective-permute-start(bf16[224,512]{1,0:T(8,128)(2,1)S(1)} %get-tuple-element.49.refs_1_), channel_id=1, source_target_pairs={{0,4},{4,0},{8,12},{12,8},{16,20},{20,16},{24,28},{28,24},{1,5},{5... | collective-permute-start | bytes 688136 | tf_op jit(solution)/shard_map/ppermute | solution.py:161
  53.2 1.8 %collective-permute-start.13 = (bf16[224,512]{1,0:T(8,128)(2,1)S(1)}, bf16[224,512]{1,0:T(8,128)(2,1)S(1)}, u32[]{:S(2)}, u32[]{:S(2)}) collective-permute-start(bf16[224,512]{1,0:T(8,128)(2,1)S(1)} %get-tuple-element.50), channel_id=1, source_target_pairs={{0,4},{4,0},{8,12},{12,8},{16,20},{20,16},{24,28},{28,24},{1,5},{5... | collective-permute-start | bytes 688136 | tf_op jit(solution)/shard_map/ppermute | solution.py:161
  53.7 8.0 %collective-permute-start.17 = (bf16[112,512]{1,0:T(8,128)(2,1)S(1)}, bf16[112,512]{1,0:T(8,128)(2,1)S(1)}, u32[]{:S(2)}, u32[]{:S(2)}) collective-permute-start(bf16[112,512]{1,0:T(8,128)(2,1)S(1)} %merge.4.refs_0_), channel_id=1, source_target_pairs={{0,2},{1,3},{2,0},{3,1},{4,6},{5,7},{6,4},{7,5},{8,10},{9,11},{10,... | collective-permute-start | bytes 344072 | tf_op jit(solution)/shard_map/ppermute | solution.py:161
  55.2 10.4 %collective-permute-start.15 = (bf16[224,512]{1,0:T(8,128)(2,1)S(1)}, bf16[224,512]{1,0:T(8,128)(2,1)S(1)}, u32[]{:S(2)}, u32[]{:S(2)}) collective-permute-start(bf16[224,512]{1,0:T(8,128)(2,1)S(1)} %get-tuple-element.51.refs_5_.mine), channel_id=1, source_target_pairs={{0,8},{4,12},{8,0},{12,4},{16,24},{20,28},{24,16},{28,20},{1,9},{5... | collective-permute-start | bytes 688136 | tf_op jit(solution)/shard_map/ppermute | solution.py:161
  56.7 10.6 %collective-permute-start.18 = (bf16[224,512]{1,0:T(8,128)(2,1)S(1)}, bf16[224,512]{1,0:T(8,128)(2,1)S(1)}, u32[]{:S(2)}, u32[]{:S(2)}) collective-permute-start(bf16[224,512]{1,0:T(8,128)(2,1)S(1)} %get-tuple-element.54.mine), channel_id=1, source_target_pairs={{0,16},{4,20},{8,24},{12,28},{16,0},{20,4},{24,8},{28,12},{1,17},{... | collective-permute-start | bytes 688136 | tf_op jit(solution)/shard_map/ppermute | solution.py:161
  65.0 4.0 %collective-permute-start.22 = (bf16[2,112,512]{2,1,0:T(8,128)(2,1)S(1)}, bf16[2,112,512]{2,1,0:T(8,128)(2,1)S(1)}, u32[]{:S(2)}, u32[]{:S(2)}) collective-permute-start(bf16[2,112,512]{2,1,0:T(8,128)(2,1)S(1)} %get-tuple-element.53.refs_1_.refs_0_), channel_id=1, source_target_pairs={{0,4},{4,0},{8,12},{12,8},{16,20},{20,16},{24,28},{28,24},{1,5},{5... | collective-permute-start | bytes 688136 | tf_op jit(solution)/shard_map/ppermute | solution.py:161
  65.1 3.9 %collective-permute-start.23 = (bf16[2,112,512]{2,1,0:T(8,128)(2,1)S(1)}, bf16[2,112,512]{2,1,0:T(8,128)(2,1)S(1)}, u32[]{:S(2)}, u32[]{:S(2)}) collective-permute-start(bf16[2,112,512]{2,1,0:T(8,128)(2,1)S(1)} %get-tuple-element.56.refs_1_), channel_id=1, source_target_pairs={{0,4},{4,0},{8,12},{12,8},{16,20},{20,16},{24,28},{28,24},{1,5},{5... | collective-permute-start | bytes 688136 | tf_op jit(solution)/shard_map/ppermute | solution.py:161
  65.6 9.1 %collective-permute-start.19 = (bf16[224,512]{1,0:T(8,128)(2,1)S(1)}, bf16[224,512]{1,0:T(8,128)(2,1)S(1)}, u32[]{:S(2)}, u32[]{:S(2)}) collective-permute-start(bf16[224,512]{1,0:T(8,128)(2,1)S(1)} %add.32.refs_1_.refs_0_), channel_id=1, source_target_pairs={{0,16},{4,20},{8,24},{12,28},{16,0},{20,4},{24,8},{28,12},{1,17},{... | collective-permute-start | bytes 688136 | tf_op jit(solution)/shard_map/ppermute | solution.py:161
  67.4 7.4 %collective-permute-start.20 = (bf16[224,512]{1,0:T(8,128)(2,1)S(1)}, bf16[224,512]{1,0:T(8,128)(2,1)S(1)}, u32[]{:S(2)}, u32[]{:S(2)}) collective-permute-start(bf16[224,512]{1,0:T(8,128)(2,1)S(1)} %add.33.refs_5_.refs_1_), channel_id=1, source_target_pairs={{0,8},{4,12},{8,0},{12,4},{16,24},{20,28},{24,16},{28,20},{1,9},{5... | collective-permute-start | bytes 688136 | tf_op jit(solution)/shard_map/ppermute | solution.py:161
  73.1 2.5 %collective-permute-start.27 = (bf16[224,512]{1,0:T(8,128)(2,1)S(1)}, bf16[224,512]{1,0:T(8,128)(2,1)S(1)}, u32[]{:S(2)}, u32[]{:S(2)}) collective-permute-start(bf16[224,512]{1,0:T(8,128)(2,1)S(1)} %get-tuple-element.57.refs_7_), channel_id=1, source_target_pairs={{0,4},{4,0},{8,12},{12,8},{16,20},{20,16},{24,28},{28,24},{1,5},{5... | collective-permute-start | bytes 688136 | tf_op jit(solution)/shard_map/ppermute | solution.py:161
  73.2 2.5 %collective-permute-start.28 = (bf16[224,512]{1,0:T(8,128)(2,1)S(1)}, bf16[224,512]{1,0:T(8,128)(2,1)S(1)}, u32[]{:S(2)}, u32[]{:S(2)}) collective-permute-start(bf16[224,512]{1,0:T(8,128)(2,1)S(1)} %get-tuple-element.61), channel_id=1, source_target_pairs={{0,4},{4,0},{8,12},{12,8},{16,20},{20,16},{24,28},{28,24},{1,5},{5... | collective-permute-start | bytes 688136 | tf_op jit(solution)/shard_map/ppermute | solution.py:161
  75.7 7.1 %collective-permute-start.30 = (bf16[224,512]{1,0:T(8,128)(2,1)S(1)}, bf16[224,512]{1,0:T(8,128)(2,1)S(1)}, u32[]{:S(2)}, u32[]{:S(2)}) collective-permute-start(bf16[224,512]{1,0:T(8,128)(2,1)S(1)} %get-tuple-element.63.mine.refs_1_), channel_id=1, source_target_pairs={{0,8},{4,12},{8,0},{12,4},{16,24},{20,28},{24,16},{28,20},{1,9},{5... | collective-permute-start | bytes 688136 | tf_op jit(solution)/shard_map/ppermute | solution.py:161
  77.3 6.7 %collective-permute-start.29 = (bf16[224,512]{1,0:T(8,128)(2,1)S(1)}, bf16[224,512]{1,0:T(8,128)(2,1)S(1)}, u32[]{:S(2)}, u32[]{:S(2)}) collective-permute-start(bf16[224,512]{1,0:T(8,128)(2,1)S(1)} %get-tuple-element.62.mine), channel_id=1, source_target_pairs={{0,16},{4,20},{8,24},{12,28},{16,0},{20,4},{24,8},{28,12},{1,17},{... | collective-permute-start | bytes 688136 | tf_op jit(solution)/shard_map/ppermute | solution.py:161
  78.1 14.6 %collective-permute-start.24 = (bf16[2,112,512]{2,1,0:T(8,128)(2,1)S(1)}, bf16[2,112,512]{2,1,0:T(8,128)(2,1)S(1)}, u32[]{:S(2)}, u32[]{:S(2)}) collective-permute-start(bf16[2,112,512]{2,1,0:T(8,128)(2,1)S(1)} %get-tuple-element.58.refs_2_.refs_0_), channel_id=1, source_target_pairs={{0,4},{4,0},{8,12},{12,8},{16,20},{20,16},{24,28},{28,24},{1,5},{5... | collective-permute-start | bytes 688136 | tf_op jit(solution)/shard_map/ppermute | solution.py:161
  78.1 14.6 %collective-permute-start.25 = (bf16[2,112,512]{2,1,0:T(8,128)(2,1)S(1)}, bf16[2,112,512]{2,1,0:T(8,128)(2,1)S(1)}, u32[]{:S(2)}, u32[]{:S(2)}) collective-permute-start(bf16[2,112,512]{2,1,0:T(8,128)(2,1)S(1)} %get-tuple-element.59.refs_1_), channel_id=1, source_target_pairs={{0,4},{4,0},{8,12},{12,8},{16,20},{20,16},{24,28},{28,24},{1,5},{5... | collective-permute-start | bytes 688136 | tf_op jit(solution)/shard_map/ppermute | solution.py:161
  84.1 9.9 %collective-permute-start.33 = (bf16[224,512]{1,0:T(8,128)(2,1)S(1)}, bf16[224,512]{1,0:T(8,128)(2,1)S(1)}, u32[]{:S(2)}, u32[]{:S(2)}) collective-permute-start(bf16[224,512]{1,0:T(8,128)(2,1)S(1)} %add.36.refs_7_.refs_1_), channel_id=1, source_target_pairs={{0,8},{4,12},{8,0},{12,4},{16,24},{20,28},{24,16},{28,20},{1,9},{5... | collective-permute-start | bytes 688136 | tf_op jit(solution)/shard_map/ppermute | solution.py:161
  84.7 9.4 %collective-permute-start.32 = (bf16[224,512]{1,0:T(8,128)(2,1)S(1)}, bf16[224,512]{1,0:T(8,128)(2,1)S(1)}, u32[]{:S(2)}, u32[]{:S(2)}) collective-permute-start(bf16[224,512]{1,0:T(8,128)(2,1)S(1)} %add.35.refs_1_.refs_0_), channel_id=1, source_target_pairs={{0,16},{4,20},{8,24},{12,28},{16,0},{20,4},{24,8},{28,12},{1,17},{... | collective-permute-start | bytes 688136 | tf_op jit(solution)/shard_map/ppermute | solution.py:161
  86.2 6.5 %collective-permute-start.26 = (bf16[112,512]{1,0:T(8,128)(2,1)S(1)}, bf16[112,512]{1,0:T(8,128)(2,1)S(1)}, u32[]{:S(2)}, u32[]{:S(2)}) collective-permute-start(bf16[112,512]{1,0:T(8,128)(2,1)S(1)} %merge.5.refs_3_), channel_id=1, source_target_pairs={{0,2},{1,3},{2,0},{3,1},{4,6},{5,7},{6,4},{7,5},{8,10},{9,11},{10,... | collective-permute-start | bytes 344072 | tf_op jit(solution)/shard_map/ppermute | solution.py:161
  94.0 10.1 %copy-start.3 = (bf16[512,512]{1,0:T(8,128)(2,1)S(1)}, bf16[512,512]{1,0:T(8,128)(2,1)}, u32[]{:S(2)}) copy-start(bf16[512,512]{1,0:T(8,128)(2,1)} %refs_2_.5) | copy-start | bytes 1572868
  94.9 1.6 %collective-permute-start.34 = (bf16[2,112,512]{2,1,0:T(8,128)(2,1)S(1)}, bf16[2,112,512]{2,1,0:T(8,128)(2,1)S(1)}, u32[]{:S(2)}, u32[]{:S(2)}) collective-permute-start(bf16[2,112,512]{2,1,0:T(8,128)(2,1)S(1)} %get-tuple-element.67.refs_0_.refs_7_), channel_id=1, source_target_pairs={{0,4},{4,0},{8,12},{12,8},{16,20},{20,16},{24,28},{28,24},{1,5},{5... | collective-permute-start | bytes 688136 | tf_op jit(solution)/shard_map/ppermute | solution.py:161
  95.0 1.8 %collective-permute-start.35 = (bf16[2,112,512]{2,1,0:T(8,128)(2,1)S(1)}, bf16[2,112,512]{2,1,0:T(8,128)(2,1)S(1)}, u32[]{:S(2)}, u32[]{:S(2)}) collective-permute-start(bf16[2,112,512]{2,1,0:T(8,128)(2,1)S(1)} %get-tuple-element.68.refs_1_), channel_id=1, source_target_pairs={{0,4},{4,0},{8,12},{12,8},{16,20},{20,16},{24,28},{28,24},{1,5},{5... | collective-permute-start | bytes 688136 | tf_op jit(solution)/shard_map/ppermute | solution.py:161
  95.5 5.1 %collective-permute-start.31 = (bf16[112,512]{1,0:T(8,128)(2,1)S(1)}, bf16[112,512]{1,0:T(8,128)(2,1)S(1)}, u32[]{:S(2)}, u32[]{:S(2)}) collective-permute-start(bf16[112,512]{1,0:T(8,128)(2,1)S(1)} %get-tuple-element.65.refs_7_), channel_id=1, source_target_pairs={{0,1},{1,0},{2,3},{3,2},{4,5},{5,4},{6,7},{7,6},{8,9},{9,8},{10,11... | collective-permute-start | bytes 344072 | tf_op jit(solution)/shard_map/ppermute | solution.py:161
  98.1 5.3 %collective-permute-start.36 = (bf16[112,512]{1,0:T(8,128)(2,1)S(1)}, bf16[112,512]{1,0:T(8,128)(2,1)S(1)}, u32[]{:S(2)}, u32[]{:S(2)}) collective-permute-start(bf16[112,512]{1,0:T(8,128)(2,1)S(1)} %get-tuple-element.69.refs_1_), channel_id=1, source_target_pairs={{0,1},{1,0},{2,3},{3,2},{4,5},{5,4},{6,7},{7,6},{8,9},{9,8},{10,11... | collective-permute-start | bytes 344072 | tf_op jit(solution)/shard_map/ppermute | solution.py:161
  100.7 10.4 %collective-permute-start.37 = (bf16[112,512]{1,0:T(8,128)(2,1)S(1)}, bf16[112,512]{1,0:T(8,128)(2,1)S(1)}, u32[]{:S(2)}, u32[]{:S(2)}) collective-permute-start(bf16[112,512]{1,0:T(8,128)(2,1)S(1)} %add.37.refs_1_.refs_0_), channel_id=1, source_target_pairs={{0,2},{1,3},{2,0},{3,1},{4,6},{5,7},{6,4},{7,5},{8,10},{9,11},{10,... | collective-permute-start | bytes 344072 | tf_op jit(solution)/shard_map/ppermute | solution.py:161
  103.4 9.8 %collective-permute-start.38 = (bf16[112,512]{1,0:T(8,128)(2,1)S(1)}, bf16[112,512]{1,0:T(8,128)(2,1)S(1)}, u32[]{:S(2)}, u32[]{:S(2)}) collective-permute-start(bf16[112,512]{1,0:T(8,128)(2,1)S(1)} %add.38.refs_1_.refs_3_), channel_id=1, source_target_pairs={{0,2},{1,3},{2,0},{3,1},{4,6},{5,7},{6,4},{7,5},{8,10},{9,11},{10,... | collective-permute-start | bytes 344072 | tf_op jit(solution)/shard_map/ppermute | solution.py:161

commit v3 on v2

--- a/solution.py
+++ b/solution.py
@@ -12,13 +12,13 @@
 ANY = pl.BlockSpec(memory_space=pl.ANY)
 LITTLE = pl.CostEstimate(flops=1, bytes_accessed=1, transcendentals=0)
 ROOM = 8 * 1024 * 1024
-PARTS = (2, 2, 2, 2, 2)
+PARTS = (2, 2, 2, 2)
 SPLIT = (2, 3)
-CUT = 0
+SEEN = (2, 2, 2, 2)
 ORDER = (
     "down0", "sum0", "turn0", "down1:hop_b", "sum1", "residual", "hold", "see0",
     "merge0", "hop3", "down2:hop_d", "turn1", "sum2", "see1:far0", "turn2", "turn2",
-    "merge1", "down3", "see2", "sum3", "turn3", "turn3", "merge2", "see3",
+    "merge1", "down3", "see2", "sum3", "turn3:far1", "turn3:far0", "merge2", "see3:pair2",
     "merge3", "done2", "done3", "early",
 )
 
@@ -31,15 +31,17 @@
     return jnp.dot(a, b, preferred_element_type=F32)
 
 
-def _down_kernel(half, blocks, waits, info, *refs):
-    w, gives, keep = refs[blocks], refs[blocks + 1 + waits : -1], refs[-1]
+def _down_kernel(half, blocks, parts, info, *refs):
+    w, outs = refs[blocks], refs[-parts[0] - parts[1] :]
     mine = info[0]
     block = refs[0][...] if blocks == 1 else jnp.where(info[1] > 0, refs[0][...], refs[1][...])
-    give = _dot(block, w[:, pl.ds(pl.multiple_of((1 - mine) * half, half), half)]).astype(BF)
-    count = gives[0].shape[0]
-    for i, out in enumerate(gives):
-        out[...] = give[i * count : (i + 1) * count]
-    keep[...] = _dot(block, w[:, pl.ds(pl.multiple_of(mine * half, half), half)])
+    if parts[0]:
+        give = _dot(block, w[:, pl.ds(pl.multiple_of((1 - mine) * half, half), half)]).astype(BF)
+        count = outs[0].shape[0]
+        for i, out in enumerate(outs[: parts[0]]):
+            out[...] = give[i * count : (i + 1) * count]
+    if parts[1]:
+        outs[-1][...] = _dot(block, w[:, pl.ds(pl.multiple_of(mine * half, half), half)])
 
 
 def _add_kernel(ins, outs, mine, *refs):
@@ -51,10 +53,11 @@
         first += out.shape[0]
 
 
-def _vision_kernel(parts, *refs):
+def _vision_kernel(parts, seen, *refs):
     tokens, scale, info = refs[2 * parts], refs[2 * parts + 1], refs[2 * parts + 2]
     offset = info[0] * tokens.shape[1]
-    outs, spread = refs[-3:-1], refs[-1]
+    outs, spread = refs[-1 - seen : -1], refs[-1]
+    each = 4 // seen
     first = 0
     for mine, came in zip(refs[:parts], refs[parts : 2 * parts]):
         rows = pl.ds(first, mine.shape[0])
@@ -67,8 +70,8 @@
         first += mine.shape[0]
     for j in range(spread.shape[0]):
         for k in range(4):
-            out = outs[k // 2]
-            out[k % 2, :, pl.ds(j * 128, 128)] = spread[j, pl.ds(k, out.shape[1], stride=4), :].astype(BF)
+            out = outs[k // each]
+            out[k % each, :, pl.ds(j * 128, 128)] = spread[j, pl.ds(k, out.shape[1], stride=4), :].astype(BF)
 
 
 def _residual_kernel(half, pieces, info, tokens, *refs):
@@ -96,23 +99,21 @@
 
 
 def _merge_kernel(half, blocks, late, first, info, *refs):
-    own, other, weight = refs[: 2 * blocks], refs[2 * blocks : 4 * blocks], refs[4 * blocks]
+    own, other, weight = refs[:blocks], refs[blocks : 2 * blocks], refs[2 * blocks]
     mine = info[0]
     here = pl.ds(pl.multiple_of(mine * half, half), half)
     there = pl.ds(pl.multiple_of((1 - mine) * half, half), half)
 
-    def rows(these, k):
-        found = [these[2 * i + k // 2][k % 2] for i in range(blocks)]
-        return found[0] if blocks == 1 else jnp.concatenate(found, axis=0)
-
+    each = 4 // blocks
     part = None
     for k in range(4):
-        more = _dot(rows(own, k), weight[k, here, :]) + _dot(rows(other, k), weight[k, there, :])
+        i, j = k // each, k % each
+        more = _dot(own[i][j], weight[k, here, :]) + _dot(other[i][j], weight[k, there, :])
         part = more if part is None else part + more
     if late is None:
         refs[-1][...] = part.astype(BF)
         return
-    near, next_to = refs[4 * blocks + 1], refs[4 * blocks + 2]
+    near, next_to = refs[2 * blocks + 1], refs[2 * blocks + 2]
     second = info[1] > 0 if late == 0 else info[1] == 0
     found = pl.ds(first, part.shape[0])
     part = part + jnp.where(second, next_to[found, :], near[found, :]).astype(F32)
@@ -220,19 +221,21 @@
             after[:] = [same]
             return same
 
-        def down(*blocks, parts=2):
+        def down(*blocks, parts=2, keep=1):
             count = blocks[0].shape[0]
-            *gives, keep = pl.pallas_call(
-                functools.partial(_down_kernel, half, len(blocks), len(after)),
-                out_shape=(_near((count // parts, half), BF),) * parts + (_near((count, half), F32),),
+            outs = [_near((count // parts, half), BF)] * parts if parts else []
+            outs += [_near((count, half), F32)] * keep
+            given = pl.pallas_call(
+                functools.partial(_down_kernel, half, len(blocks), (parts, keep)),
+                out_shape=tuple(outs),
                 in_specs=[SMEM] + [VMEM] * (len(blocks) + 1) + [ANY] * len(after),
-                out_specs=(VMEM,) * (parts + 1),
+                out_specs=(VMEM,) * len(outs),
                 cost_estimate=LITTLE,
                 compiler_params=pltpu.CompilerParams(vmem_limit_bytes=ROOM),
                 name="down",
             )(info, *blocks, down_weight, *after)
-            after[:] = [gives[0]]
-            return tuple(gives), keep
+            after[:] = [given[0]]
+            return tuple(given[:parts]), given[-1]
 
         def add(total, came, *rows):
             counts = rows or (total.shape[0],)
@@ -249,13 +252,13 @@
             after[:] = [give[0]]
             return give if rows else give[0]
 
-        def see(mine_parts, came_parts, residual):
+        def see(mine_parts, came_parts, residual, parts=2):
             count = residual.shape[0]
             out = pl.pallas_call(
-                functools.partial(_vision_kernel, len(mine_parts)),
-                out_shape=(_near((2, count // 4, half), BF),) * 2,
+                functools.partial(_vision_kernel, len(mine_parts), parts),
+                out_shape=(_near((4 // parts, count // 4, half), BF),) * parts,
                 in_specs=[VMEM] * (2 * len(mine_parts) + 2) + [SMEM] + [ANY] * len(after),
-                out_specs=(VMEM, VMEM),
+                out_specs=(VMEM,) * parts,
                 scratch_shapes=[pltpu.VMEM((half // 128, count, 128), F32)],
                 cost_estimate=LITTLE,
                 compiler_params=pltpu.CompilerParams(vmem_limit_bytes=ROOM),
@@ -265,11 +268,11 @@
             return tuple(out)
 
         def merge(own, other, weight, came=None, late=None, first=0):
-            count = own[0].shape[1] * (len(own) // 2)
+            count = own[0].shape[1]
             extra = [] if came is None else list(came)
             outs = [_near((count, dec), BF)] + [_near((count, dec), F32)] * (len(extra) // 2)
             given = pl.pallas_call(
-                functools.partial(_merge_kernel, half, len(own) // 2, late, first),
+                functools.partial(_merge_kernel, half, len(own), late, first),
                 out_shape=tuple(outs),
                 in_specs=[SMEM] + [VMEM] * (2 * len(own) + 1 + len(extra)) + [ANY] * len(after),
                 out_specs=(VMEM,) * len(outs),
@@ -360,9 +363,7 @@
             ]
         )[None, :]
         after.extend([scale, where_to])
-        cut = CUT * patches // 7 if CUT else patches
-        pieces = [(i, 0, patches) for i in range(3)] + [(3, 0, cut)]
-        pieces += [(3, cut, patches - cut)] if CUT else []
+        pieces = [(i, 0, patches) for i in range(4)]
         last = len(pieces)
         v = {}
         v["hop_a"] = swap(hidden, "col", 1)
@@ -379,8 +380,12 @@
                 blocks = [[hidden], [v["hop_a"]], [v["hop_b"], v["hop_c"]]][i]
             else:
                 blocks = [v["mid", i], v["hop", i]]
-            give, v["keep", i] = down(*blocks, parts=PARTS[i])
+            v["block", i] = blocks
+            give, v["keep", i] = down(*blocks, parts=PARTS[i], keep=0 if f"keep{i}" in ORDER else 1)
             v["core", i] = core(give)
+
+        def stay_down(i):
+            _, v["keep", i] = down(*v["block", i], parts=0)
 
         def first_sum(i):
             if i in SPLIT:
@@ -398,7 +403,7 @@
             v["back", i].append((x if j else y)(v["turn", i][j]))
 
         def look(i):
-            seen = see(v["turn", i], v["back", i], v["residual"][i])
+            seen = see(v["turn", i], v["back", i], v["residual"][i], SEEN[i])
             v["seen", i], v["other", i] = seen, core(seen)
 
         def project(i):
@@ -425,6 +430,7 @@
         calls = {
             "hop": send_on,
             "down": send_down,
+            "keep": stay_down,
             "sum": first_sum,
             "turn": second_sum,
             "see": look,

time: 115 us -> 113 us (0.983)
  waiting for transfers between devices: 55.7 us -> 53.2 us
    ppermute x35, waiting for transfers between devices: 47.8 us -> 45.2 us  [swap(): return lax.ppermute(x, axis, [(i, i ^ bit) for i in range(size)])]
  transfers between devices with their start and end apart: 39 -> 39, of which waited for: 23 -> 22; matrix products, arithmetic and copies ran while one was open for 2% -> 2% of each run, Pallas kernels for 18% -> 17%
where the time goes in v3:
time: 113 us
  waiting for transfers between devices  53.2 us (47%)
  starting transfers between devices  31.9 us (28%)
  Pallas kernels  22.8 us (20%)
  local copies, waits for them, and re-layouts  3.55 us (3%)
    ppermute x35, waiting for transfers between devices, swap(): return lax.ppermute(x, axis, [(i, i ^ bit) for i in range(size)])  45.2 us
    ppermute x35, starting transfers between devices, swap(): return lax.ppermute(x, axis, [(i, i ^ bit) for i in range(size)])  27.9 us
    ppermute x1, waiting for transfers between devices, per_device(): v['hop_c'] = lax.ppermute(v['hop_b'], 'col', outward)  6.77 us
    pallas_call x4, Pallas kernels, down(): pl.pallas_call(functools.partial(_down_kernel, half, len(blocks), (parts,...  6.65 us
    pallas_call x4, Pallas kernels, merge(): pl.pallas_call(functools.partial(_merge_kernel, half, len(own), late, fir...  5.2 us
    pallas_call x4, Pallas kernels, see(): pl.pallas_call(functools.partial(_vision_kernel, len(mine_parts), parts),...  3.72 us
    unnamed x8, local copies, waits for them, and re-layouts  2.78 us
  transfers between devices with their start and end apart: 39, of which 22 were waited for; matrix products, arithmetic and copies ran while one was open for 2% of the time, Pallas kernels for 17%

profile of v3, /device:TPU:0, one launch (start us, length us, event | category | flops | bytes accessed | tf_op | source)
XLA Modules:
  0.0 112.8 jit_solution(9385799958155111317)
XLA Ops:
  0.0 3.0 %collective-permute-start.2 = (bf16[448,1024]{1,0:T(8,128)(2,1)}, bf16[448,1024]{1,0:T(8,128)(2,1)S(1)}, u32[]{:S(2)}, u32[]{:S(2)}) collective-permute-start(bf16[448,1024]{1,0:T(8,128)(2,1)} %refs_0_.1), channel_id=1, source_target_pairs={{0,1},{1,0},{2,3},{3,2},{4,5},{5,4},{6,7},{7,6},{8,9},{9,8},{10,11... | collective-permute-start | bytes 2752520 | tf_op jit(solution)/shard_map/ppermute | solution.py:162
  4.5 0.9 broadcast_select_fusion.3
  5.5 1.6 %copy-done = bf16[1024,1024]{1,0:T(8,128)(2,1)S(1)} copy-done((bf16[1024,1024]{1,0:T(8,128)(2,1)S(1)}, bf16[1024,1024]{1,0:T(8,128)(2,1)}, u32[]{:S(2)}) %copy-start) | copy-done | bytes 2097176
  7.1 1.2 %copy-done.2 = bf16[448,1024]{1,0:T(8,128)(2,1)S(1)} copy-done((bf16[448,1024]{1,0:T(8,128)(2,1)S(1)}, bf16[448,1024]{1,0:T(8,128)(2,1)}, u32[]{:S(2)}) %copy-start.2) | copy-done | bytes 917528
  8.3 1.7 %down.4 = (bf16[224,512]{1,0:T(8,128)(2,1)S(1)}, bf16[224,512]{1,0:T(8,128)(2,1)S(1)}, f32[448,512]{1,0:T(8,128)S(1)}) custom-call(s32[7]{0:T(128)S(1)} %stack.35.info.refs_4_.refs_6_, bf16[448,1024]{1,0:T(8,128)(2,1)S(1)} %copy-done.2, bf16[1024,1024]{1,0:T(8,128)(2,1)S(1)} %copy-done, bf16[1,1024]{1,0:T(2,128)(2,1)S(1)} %broadcast_in_dim.7.refs_2_.refs_3_.refs_5_, ...), custom_call_target="tpu_custom_call" | custom-call | flops 1 | bytes 1 | tf_op jit(solution)/shard_map/down/pallas_call | solution.py:228
  10.5 1.0 collective-permute-done.4.refs_0_
  11.9 1.6 %collective-permute-start.6 = (bf16[448,512]{1,0:T(8,128)(2,1)S(1)}, bf16[448,512]{1,0:T(8,128)(2,1)S(1)}, u32[]{:S(2)}, u32[]{:S(2)}) collective-permute-start(bf16[448,512]{1,0:T(8,128)(2,1)S(1)} %add.27.mine.refs_1_), channel_id=1, source_target_pairs={{0,8},{4,12},{8,0},{12,4},{16,24},{20,28},{24,16},{28,20},{1,9},{5... | collective-permute-start | bytes 1376264 | tf_op jit(solution)/shard_map/ppermute | solution.py:162
  13.5 10.1 %collective-permute-done.2.refs_0_ = bf16[448,1024]{1,0:T(8,128)(2,1)S(1)} collective-permute-done((bf16[448,1024]{1,0:T(8,128)(2,1)}, bf16[448,1024]{1,0:T(8,128)(2,1)S(1)}, u32[]{:S(2)}, u32[]{:S(2)}) %collective-permute-start.2) | collective-permute-done | bytes 917536 | tf_op jit(solution)/shard_map/ppermute | solution.py:162
  24.3 1.3 %collective-permute-start.1 = (bf16[448,1024]{1,0:T(8,128)(2,1)S(1)}, bf16[448,1024]{1,0:T(8,128)(2,1)S(1)}, u32[]{:S(2)}, u32[]{:S(2)}) collective-permute-start(bf16[448,1024]{1,0:T(8,128)(2,1)S(1)} %collective-permute-done.refs_3_.refs_0_), channel_id=1, source_target_pairs={{1,0},{2,3},{5,4},{6,7},{9,8},{10,11},{13,12},{14,15},{17,16},{18,... | collective-permute-start | bytes 2752520 | tf_op jit(solution)/shard_map/ppermute | solution.py:371
  25.7 1.8 %collective-permute-start.7 = (bf16[448,512]{1,0:T(8,128)(2,1)S(1)}, bf16[448,512]{1,0:T(8,128)(2,1)S(1)}, u32[]{:S(2)}, u32[]{:S(2)}) collective-permute-start(bf16[448,512]{1,0:T(8,128)(2,1)S(1)} %add.28.refs_2_.refs_0_), channel_id=1, source_target_pairs={{0,16},{4,20},{8,24},{12,28},{16,0},{20,4},{24,8},{28,12},{1,17},{... | collective-permute-start | bytes 1376264 | tf_op jit(solution)/shard_map/ppermute | solution.py:162
  27.5 1.7 %down.5 = (bf16[224,512]{1,0:T(8,128)(2,1)S(1)}, bf16[224,512]{1,0:T(8,128)(2,1)S(1)}, f32[448,512]{1,0:T(8,128)S(1)}) custom-call(s32[7]{0:T(128)S(1)} %stack.35.info.refs_4_.refs_6_, bf16[448,1024]{1,0:T(8,128)(2,1)S(1)} %collective-permute-done.2.refs_0_, bf16[1024,1024]{1,0:T(8,128)(2,1)S(1)} %copy-done.1, bf16[448,512]{1,0:T(8,128)(2,1)S(1)} %add.28.refs_2_.refs_0_, ...), custom_call_target="tpu_custom_call" | custom-call | flops 1 | bytes 1 | tf_op jit(solution)/shard_map/down/pallas_call | solution.py:228
  29.7 1.0 collective-permute-done.8.refs_0_
  31.1 1.6 %collective-permute-start.14 = (bf16[448,512]{1,0:T(8,128)(2,1)S(1)}, bf16[448,512]{1,0:T(8,128)(2,1)S(1)}, u32[]{:S(2)}, u32[]{:S(2)}) collective-permute-start(bf16[448,512]{1,0:T(8,128)(2,1)S(1)} %add.29.refs_0_.mine), channel_id=1, source_target_pairs={{0,8},{4,12},{8,0},{12,4},{16,24},{20,28},{24,16},{28,20},{1,9},{5... | collective-permute-start | bytes 1376264 | tf_op jit(solution)/shard_map/ppermute | solution.py:162
  32.7 2.0 %residuals.1 = (bf16[448,512]{1,0:T(8,128)(2,1)S(1)}, bf16[448,512]{1,0:T(8,128)(2,1)S(1)}, bf16[448,512]{1,0:T(8,128)(2,1)S(1)}, bf16[448,512]{1,0:T(8,128)(2,1)S(1)}) custom-call(s32[7]{0:T(128)S(1)} %stack.35.info.refs_4_.refs_6_, bf16[1792,1024]{1,0:T(8,128)(2,1)} %tokens.1, bf16[448,512]{1,0:T(8,128)(2,1)S(1)} %add.29.refs_0_.mine), custom_call_target="tpu_custom_call" | custom-call | flops 1 | bytes 1 | tf_op jit(solution)/shard_map/residuals/pallas_call | solution.py:198
  34.7 2.2 %hold.1.refs_5_.refs_4_ = bf16[4,1024,512]{2,1,0:T(8,128)(2,1)S(1)} custom-call(bf16[4,1024,512]{2,1,0:T(8,128)(2,1)} %weight.1, bf16[448,512]{1,0:T(8,128)(2,1)S(1)} %get-tuple-element.45.refs_0_.refs_2_), custom_call_target="tpu_custom_call" | custom-call | flops 1 | bytes 1 | tf_op jit(solution)/shard_map/hold/pallas_call | solution.py:184
  37.5 1.0 vision.4
  39.1 1.0 collective-permute-done.10.refs_2_
  40.4 1.3 %merge.4.refs_0_ = bf16[112,512]{1,0:T(8,128)(2,1)S(1)} custom-call(s32[7]{0:T(128)S(1)} %stack.35.info.refs_4_.refs_6_, bf16[2,112,512]{2,1,0:T(8,128)(2,1)S(1)} %get-tuple-element.46.refs_0_.refs_5_, bf16[2,112,512]{2,1,0:T(8,128)(2,1)S(1)} %get-tuple-element.47.refs_1_, bf16[2,112,512]{2,1,0:T(8,128)(2,1)S(1)} %collective-permute-done.10.refs_2_, ...), custom_call_target="tpu_custom_call" | custom-call | flops 1 | bytes 1 | tf_op jit(solution)/shard_map/merge/pallas_call | solution.py:274
  41.8 1.3 %collective-permute-start.21 = (bf16[448,1024]{1,0:T(8,128)(2,1)S(1)}, bf16[448,1024]{1,0:T(8,128)(2,1)S(1)}, u32[]{:S(2)}, u32[]{:S(2)}) collective-permute-start(bf16[448,1024]{1,0:T(8,128)(2,1)S(1)} %relay.1.refs_3_.refs_0_), channel_id=1, source_target_pairs={{1,0},{2,3},{5,4},{6,7},{9,8},{10,11},{13,12},{14,15},{17,16},{18,... | collective-permute-start | bytes 2752520 | tf_op jit(solution)/shard_map/ppermute | solution.py:376
  43.1 6.8 %collective-permute-done.1.refs_1_ = bf16[448,1024]{1,0:T(8,128)(2,1)S(1)} collective-permute-done((bf16[448,1024]{1,0:T(8,128)(2,1)S(1)}, bf16[448,1024]{1,0:T(8,128)(2,1)S(1)}, u32[]{:S(2)}, u32[]{:S(2)}) %collective-permute-start.1) | collective-permute-done | bytes 917536 | tf_op jit(solution)/shard_map/ppermute | solution.py:371
  49.8 1.7 %down.6 = (bf16[224,512]{1,0:T(8,128)(2,1)S(1)}, bf16[224,512]{1,0:T(8,128)(2,1)S(1)}, f32[448,512]{1,0:T(8,128)S(1)}) custom-call(s32[7]{0:T(128)S(1)} %stack.35.info.refs_4_.refs_6_, bf16[448,1024]{1,0:T(8,128)(2,1)S(1)} %collective-permute-done.refs_3_.refs_0_, bf16[448,1024]{1,0:T(8,128)(2,1)S(1)} %collective-permute-done.1.refs_1_, ...), custom_call_target="tpu_custom_call" | custom-call | flops 1 | bytes 1 | tf_op jit(solution)/shard_map/down/pallas_call | solution.py:228
  51.6 1.6 %collective-permute-start.16 = (bf16[448,512]{1,0:T(8,128)(2,1)S(1)}, bf16[448,512]{1,0:T(8,128)(2,1)S(1)}, u32[]{:S(2)}, u32[]{:S(2)}) collective-permute-start(bf16[448,512]{1,0:T(8,128)(2,1)S(1)} %add.30.refs_2_.refs_0_), channel_id=1, source_target_pairs={{0,16},{4,20},{8,24},{12,28},{16,0},{20,4},{24,8},{28,12},{1,17},{... | collective-permute-start | bytes 1376264 | tf_op jit(solution)/shard_map/ppermute | solution.py:162
  53.7 1.0 collective-permute-start.17
  55.2 1.6 %collective-permute-start.15 = (bf16[224,512]{1,0:T(8,128)(2,1)S(1)}, bf16[224,512]{1,0:T(8,128)(2,1)S(1)}, u32[]{:S(2)}, u32[]{:S(2)}) collective-permute-start(bf16[224,512]{1,0:T(8,128)(2,1)S(1)} %get-tuple-element.51.refs_5_.mine), channel_id=1, source_target_pairs={{0,8},{4,12},{8,0},{12,4},{16,24},{20,28},{24,16},{28,20},{1,9},{5... | collective-permute-start | bytes 688136 | tf_op jit(solution)/shard_map/ppermute | solution.py:162
  57.2 4.5 %collective-permute-done.17.refs_6_.refs_2_.refs_5_ = bf16[112,512]{1,0:T(8,128)(2,1)S(1)} collective-permute-done((bf16[112,512]{1,0:T(8,128)(2,1)S(1)}, bf16[112,512]{1,0:T(8,128)(2,1)S(1)}, u32[]{:S(2)}, u32[]{:S(2)}) %collective-permute-start.17) | collective-permute-done | bytes 114720 | tf_op jit(solution)/shard_map/ppermute | solution.py:162
  61.7 2.2 %collective-permute-done.16.refs_1_ = bf16[448,512]{1,0:T(8,128)(2,1)S(1)} collective-permute-done((bf16[448,512]{1,0:T(8,128)(2,1)S(1)}, bf16[448,512]{1,0:T(8,128)(2,1)S(1)}, u32[]{:S(2)}, u32[]{:S(2)}) %collective-permute-start.16) | collective-permute-done | bytes 458784 | tf_op jit(solution)/shard_map/ppermute | solution.py:162
  64.0 1.0 vision.5
  65.6 1.7 %collective-permute-start.19 = (bf16[224,512]{1,0:T(8,128)(2,1)S(1)}, bf16[224,512]{1,0:T(8,128)(2,1)S(1)}, u32[]{:S(2)}, u32[]{:S(2)}) collective-permute-start(bf16[224,512]{1,0:T(8,128)(2,1)S(1)} %add.32.refs_1_.refs_0_), channel_id=1, source_target_pairs={{0,16},{4,20},{8,24},{12,28},{16,0},{20,4},{24,8},{28,12},{1,17},{... | collective-permute-start | bytes 688136 | tf_op jit(solution)/shard_map/ppermute | solution.py:162
  67.4 1.6 %collective-permute-start.20 = (bf16[224,512]{1,0:T(8,128)(2,1)S(1)}, bf16[224,512]{1,0:T(8,128)(2,1)S(1)}, u32[]{:S(2)}, u32[]{:S(2)}) collective-permute-start(bf16[224,512]{1,0:T(8,128)(2,1)S(1)} %add.33.refs_5_.refs_1_), channel_id=1, source_target_pairs={{0,8},{4,12},{8,0},{12,4},{16,24},{20,28},{24,16},{28,20},{1,9},{5... | collective-permute-start | bytes 688136 | tf_op jit(solution)/shard_map/ppermute | solution.py:162
  68.9 1.3 %merge.5.refs_3_ = bf16[112,512]{1,0:T(8,128)(2,1)S(1)} custom-call(s32[7]{0:T(128)S(1)} %stack.35.info.refs_4_.refs_6_, bf16[2,112,512]{2,1,0:T(8,128)(2,1)S(1)} %get-tuple-element.53.refs_1_.refs_0_, bf16[2,112,512]{2,1,0:T(8,128)(2,1)S(1)} %get-tuple-element.56.refs_1_, bf16[2,112,512]{2,1,0:T(8,128)(2,1)S(1)} %collective-permute-done.22.refs_2_, ...), custom_call_target="tpu_custom_call" | custom-call | flops 1 | bytes 1 | tf_op jit(solution)/shard_map/merge/pallas_call | solution.py:274
  70.2 1.2 %collective-permute-done.21.refs_1_ = bf16[448,1024]{1,0:T(8,128)(2,1)S(1)} collective-permute-done((bf16[448,1024]{1,0:T(8,128)(2,1)S(1)}, bf16[448,1024]{1,0:T(8,128)(2,1)S(1)}, u32[]{:S(2)}, u32[]{:S(2)}) %collective-permute-start.21) | collective-permute-done | bytes 917536 | tf_op jit(solution)/shard_map/ppermute | solution.py:376
  71.4 1.7 %down.7 = (bf16[224,512]{1,0:T(8,128)(2,1)S(1)}, bf16[224,512]{1,0:T(8,128)(2,1)S(1)}, f32[448,512]{1,0:T(8,128)S(1)}) custom-call(s32[7]{0:T(128)S(1)} %stack.35.info.refs_4_.refs_6_, bf16[448,1024]{1,0:T(8,128)(2,1)S(1)} %relay.1.refs_3_.refs_0_, bf16[448,1024]{1,0:T(8,128)(2,1)S(1)} %collective-permute-done.21.refs_1_, bf16[1024,1024]{1,0:T(8,128)(2,1)S(1)} %copy-done.1, ...), custom_call_target="tpu_custom_call" | custom-call | flops 1 | bytes 1 | tf_op jit(solution)/shard_map/down/pallas_call | solution.py:228
  73.7 1.1 collective-permute-done.20.refs_3_
  74.8 0.9 vision.6
  75.7 1.6 %collective-permute-start.30 = (bf16[224,512]{1,0:T(8,128)(2,1)S(1)}, bf16[224,512]{1,0:T(8,128)(2,1)S(1)}, u32[]{:S(2)}, u32[]{:S(2)}) collective-permute-start(bf16[224,512]{1,0:T(8,128)(2,1)S(1)} %get-tuple-element.63.mine.refs_1_), channel_id=1, source_target_pairs={{0,8},{4,12},{8,0},{12,4},{16,24},{20,28},{24,16},{28,20},{1,9},{5... | collective-permute-start | bytes 688136 | tf_op jit(solution)/shard_map/ppermute | solution.py:162
  77.3 0.8 collective-permute-start.29
  78.1 1.2 %collective-permute-start.26 = (bf16[112,512]{1,0:T(8,128)(2,1)S(1)}, bf16[112,512]{1,0:T(8,128)(2,1)S(1)}, u32[]{:S(2)}, u32[]{:S(2)}) collective-permute-start(bf16[112,512]{1,0:T(8,128)(2,1)S(1)} %merge.5.refs_3_), channel_id=1, source_target_pairs={{0,2},{1,3},{2,0},{3,1},{4,6},{5,7},{6,4},{7,5},{8,10},{9,11},{10,... | collective-permute-start | bytes 344072 | tf_op jit(solution)/shard_map/ppermute | solution.py:162
  79.9 5.7 %collective-permute-done.26.refs_2_.refs_6_ = bf16[112,512]{1,0:T(8,128)(2,1)S(1)} collective-permute-done((bf16[112,512]{1,0:T(8,128)(2,1)S(1)}, bf16[112,512]{1,0:T(8,128)(2,1)S(1)}, u32[]{:S(2)}, u32[]{:S(2)}) %collective-permute-start.26) | collective-permute-done | bytes 114720 | tf_op jit(solution)/shard_map/ppermute | solution.py:162
  87.0 1.3 %merge.6 = (bf16[112,512]{1,0:T(8,128)(2,1)S(1)}, f32[112,512]{1,0:T(8,128)S(1)}) custom-call(s32[7]{0:T(128)S(1)} %stack.35.info.refs_4_.refs_6_, bf16[2,112,512]{2,1,0:T(8,128)(2,1)S(1)} %get-tuple-element.58.refs_2_.refs_0_, bf16[2,112,512]{2,1,0:T(8,128)(2,1)S(1)} %get-tuple-element.59.refs_1_, bf16[2,112,512]{2,1,0:T(8,128)(2,1)S(1)} %collective-permute-done.24.refs_2_, ...), custom_call_target="tpu_custom_call" | custom-call | flops 1 | bytes 1 | tf_op jit(solution)/shard_map/merge/pallas_call | solution.py:274
  88.4 4.8 %collective-permute-done.31.refs_8_.refs_0_ = bf16[112,512]{1,0:T(8,128)(2,1)S(1)} collective-permute-done((bf16[112,512]{1,0:T(8,128)(2,1)S(1)}, bf16[112,512]{1,0:T(8,128)(2,1)S(1)}, u32[]{:S(2)}, u32[]{:S(2)}) %collective-permute-start.31) | collective-permute-done | bytes 114720 | tf_op jit(solution)/shard_map/ppermute | solution.py:162
  93.5 0.9 vision.7
  94.9 1.0 collective-permute-done.34.refs_2_
  96.3 1.3 %merge.7 = (bf16[112,512]{1,0:T(8,128)(2,1)S(1)}, f32[112,512]{1,0:T(8,128)S(1)}) custom-call(s32[7]{0:T(128)S(1)} %stack.35.info.refs_4_.refs_6_, bf16[2,112,512]{2,1,0:T(8,128)(2,1)S(1)} %get-tuple-element.67.refs_0_.refs_7_, bf16[2,112,512]{2,1,0:T(8,128)(2,1)S(1)} %get-tuple-element.68.refs_1_, bf16[2,112,512]{2,1,0:T(8,128)(2,1)S(1)} %collective-permute-done.34.refs_2_, ...), custom_call_target="tpu_custom_call" | custom-call | flops 1 | bytes 1 | tf_op jit(solution)/shard_map/merge/pallas_call | solution.py:274
  97.7 2.6 %collective-permute-start.37 = (bf16[112,512]{1,0:T(8,128)(2,1)S(1)}, bf16[112,512]{1,0:T(8,128)(2,1)S(1)}, u32[]{:S(2)}, u32[]{:S(2)}) collective-permute-start(bf16[112,512]{1,0:T(8,128)(2,1)S(1)} %add.37.refs_1_.refs_0_), channel_id=1, source_target_pairs={{0,2},{1,3},{2,0},{3,1},{4,6},{5,7},{6,4},{7,5},{8,10},{9,11},{10,... | collective-permute-start | bytes 344072 | tf_op jit(solution)/shard_map/ppermute | solution.py:162
  100.3 4.3 %collective-permute-done.36.refs_0_ = bf16[112,512]{1,0:T(8,128)(2,1)S(1)} collective-permute-done((bf16[112,512]{1,0:T(8,128)(2,1)S(1)}, bf16[112,512]{1,0:T(8,128)(2,1)S(1)}, u32[]{:S(2)}, u32[]{:S(2)}) %collective-permute-start.36) | collective-permute-done | bytes 114720 | tf_op jit(solution)/shard_map/ppermute | solution.py:162
  104.7 1.0 place_early.1
  106.4 5.3 %collective-permute-done.38.refs_1_ = bf16[112,512]{1,0:T(8,128)(2,1)S(1)} collective-permute-done((bf16[112,512]{1,0:T(8,128)(2,1)S(1)}, bf16[112,512]{1,0:T(8,128)(2,1)S(1)}, u32[]{:S(2)}, u32[]{:S(2)}) %collective-permute-start.38) | collective-permute-done | bytes 114720 | tf_op jit(solution)/shard_map/ppermute | solution.py:162
  111.7 1.1 place_late.1
  (71 shorter events, 12.8 us)
Async XLA Ops:
  0.0 23.6 %collective-permute-start.2 = (bf16[448,1024]{1,0:T(8,128)(2,1)}, bf16[448,1024]{1,0:T(8,128)(2,1)S(1)}, u32[]{:S(2)}, u32[]{:S(2)}) collective-permute-start(bf16[448,1024]{1,0:T(8,128)(2,1)} %refs_0_.1), channel_id=1, source_target_pairs={{0,1},{1,0},{2,3},{3,2},{4,5},{5,4},{6,7},{7,6},{8,9},{9,8},{10,11... | collective-permute-start | bytes 2752520 | tf_op jit(solution)/shard_map/ppermute | solution.py:162
  3.0 21.3 %collective-permute-start = (bf16[448,1024]{1,0:T(8,128)(2,1)}, bf16[448,1024]{1,0:T(8,128)(2,1)S(1)}, u32[]{:S(2)}, u32[]{:S(2)}) collective-permute-start(bf16[448,1024]{1,0:T(8,128)(2,1)} %refs_0_.1), channel_id=1, source_target_pairs={{1,2},{2,1},{5,6},{6,5},{9,10},{10,9},{13,14},{14,13},{17,18},{18,... | collective-permute-start | bytes 2752520 | tf_op jit(solution)/shard_map/ppermute | solution.py:370
  5.5 1.6 %copy-start = (bf16[1024,1024]{1,0:T(8,128)(2,1)S(1)}, bf16[1024,1024]{1,0:T(8,128)(2,1)}, u32[]{:S(2)}) copy-start(bf16[1024,1024]{1,0:T(8,128)(2,1)} %refs_2_.4) | copy-start | bytes 6291460
  7.1 1.2 %copy-start.2 = (bf16[448,1024]{1,0:T(8,128)(2,1)S(1)}, bf16[448,1024]{1,0:T(8,128)(2,1)}, u32[]{:S(2)}) copy-start(bf16[448,1024]{1,0:T(8,128)(2,1)} %refs_0_.1) | copy-start | bytes 2752516
  8.3 19.2 %copy-start.1 = (bf16[1024,1024]{1,0:T(8,128)(2,1)S(1)}, bf16[1024,1024]{1,0:T(8,128)(2,1)}, u32[]{:S(2)}) copy-start(bf16[1024,1024]{1,0:T(8,128)(2,1)} %refs_2_.4) | copy-start | bytes 6291460
  10.0 1.6 %collective-permute-start.4 = (bf16[224,512]{1,0:T(8,128)(2,1)S(1)}, bf16[224,512]{1,0:T(8,128)(2,1)S(1)}, u32[]{:S(2)}, u32[]{:S(2)}) collective-permute-start(bf16[224,512]{1,0:T(8,128)(2,1)S(1)} %get-tuple-element.40.refs_2_), channel_id=1, source_target_pairs={{0,4},{4,0},{8,12},{12,8},{16,20},{20,16},{24,28},{28,24},{1,5},{5... | collective-permute-start | bytes 688136 | tf_op jit(solution)/shard_map/ppermute | solution.py:162
  10.0 1.8 %collective-permute-start.5 = (bf16[224,512]{1,0:T(8,128)(2,1)S(1)}, bf16[224,512]{1,0:T(8,128)(2,1)S(1)}, u32[]{:S(2)}, u32[]{:S(2)}) collective-permute-start(bf16[224,512]{1,0:T(8,128)(2,1)S(1)} %get-tuple-element.41), channel_id=1, source_target_pairs={{0,4},{4,0},{8,12},{12,8},{16,20},{20,16},{24,28},{28,24},{1,5},{5... | collective-permute-start | bytes 688136 | tf_op jit(solution)/shard_map/ppermute | solution.py:162
  11.9 13.7 %collective-permute-start.6 = (bf16[448,512]{1,0:T(8,128)(2,1)S(1)}, bf16[448,512]{1,0:T(8,128)(2,1)S(1)}, u32[]{:S(2)}, u32[]{:S(2)}) collective-permute-start(bf16[448,512]{1,0:T(8,128)(2,1)S(1)} %add.27.mine.refs_1_), channel_id=1, source_target_pairs={{0,8},{4,12},{8,0},{12,4},{16,24},{20,28},{24,16},{28,20},{1,9},{5... | collective-permute-start | bytes 1376264 | tf_op jit(solution)/shard_map/ppermute | solution.py:162
  23.6 18.1 %collective-permute-start.3 = (bf16[448,1024]{1,0:T(8,128)(2,1)S(1)}, bf16[448,1024]{1,0:T(8,128)(2,1)S(1)}, u32[]{:S(2)}, u32[]{:S(2)}) collective-permute-start(bf16[448,1024]{1,0:T(8,128)(2,1)S(1)} %collective-permute-done.2.refs_0_), channel_id=1, source_target_pairs={{1,2},{2,1},{5,6},{6,5},{9,10},{10,9},{13,14},{14,13},{17,18},{18,... | collective-permute-start | bytes 2752520 | tf_op jit(solution)/shard_map/ppermute | solution.py:372
  24.3 25.5 %collective-permute-start.1 = (bf16[448,1024]{1,0:T(8,128)(2,1)S(1)}, bf16[448,1024]{1,0:T(8,128)(2,1)S(1)}, u32[]{:S(2)}, u32[]{:S(2)}) collective-permute-start(bf16[448,1024]{1,0:T(8,128)(2,1)S(1)} %collective-permute-done.refs_3_.refs_0_), channel_id=1, source_target_pairs={{1,0},{2,3},{5,4},{6,7},{9,8},{10,11},{13,12},{14,15},{17,16},{18,... | collective-permute-start | bytes 2752520 | tf_op jit(solution)/shard_map/ppermute | solution.py:371
  25.7 11.8 %collective-permute-start.7 = (bf16[448,512]{1,0:T(8,128)(2,1)S(1)}, bf16[448,512]{1,0:T(8,128)(2,1)S(1)}, u32[]{:S(2)}, u32[]{:S(2)}) collective-permute-start(bf16[448,512]{1,0:T(8,128)(2,1)S(1)} %add.28.refs_2_.refs_0_), channel_id=1, source_target_pairs={{0,16},{4,20},{8,24},{12,28},{16,0},{20,4},{24,8},{28,12},{1,17},{... | collective-permute-start | bytes 1376264 | tf_op jit(solution)/shard_map/ppermute | solution.py:162
  29.2 1.6 %collective-permute-start.8 = (bf16[224,512]{1,0:T(8,128)(2,1)S(1)}, bf16[224,512]{1,0:T(8,128)(2,1)S(1)}, u32[]{:S(2)}, u32[]{:S(2)}) collective-permute-start(bf16[224,512]{1,0:T(8,128)(2,1)S(1)} %get-tuple-element.43.refs_2_), channel_id=1, source_target_pairs={{0,4},{4,0},{8,12},{12,8},{16,20},{20,16},{24,28},{28,24},{1,5},{5... | collective-permute-start | bytes 688136 | tf_op jit(solution)/shard_map/ppermute | solution.py:162
  29.2 1.8 %collective-permute-start.9 = (bf16[224,512]{1,0:T(8,128)(2,1)S(1)}, bf16[224,512]{1,0:T(8,128)(2,1)S(1)}, u32[]{:S(2)}, u32[]{:S(2)}) collective-permute-start(bf16[224,512]{1,0:T(8,128)(2,1)S(1)} %get-tuple-element.44), channel_id=1, source_target_pairs={{0,4},{4,0},{8,12},{12,8},{16,20},{20,16},{24,28},{28,24},{1,5},{5... | collective-permute-start | bytes 688136 | tf_op jit(solution)/shard_map/ppermute | solution.py:162
  31.1 20.4 %collective-permute-start.14 = (bf16[448,512]{1,0:T(8,128)(2,1)S(1)}, bf16[448,512]{1,0:T(8,128)(2,1)S(1)}, u32[]{:S(2)}, u32[]{:S(2)}) collective-permute-start(bf16[448,512]{1,0:T(8,128)(2,1)S(1)} %add.29.refs_0_.mine), channel_id=1, source_target_pairs={{0,8},{4,12},{8,0},{12,4},{16,24},{20,28},{24,16},{28,20},{1,9},{5... | collective-permute-start | bytes 1376264 | tf_op jit(solution)/shard_map/ppermute | solution.py:162
  38.5 1.6 %collective-permute-start.10 = (bf16[2,112,512]{2,1,0:T(8,128)(2,1)S(1)}, bf16[2,112,512]{2,1,0:T(8,128)(2,1)S(1)}, u32[]{:S(2)}, u32[]{:S(2)}) collective-permute-start(bf16[2,112,512]{2,1,0:T(8,128)(2,1)S(1)} %get-tuple-element.46.refs_0_.refs_5_), channel_id=1, source_target_pairs={{0,4},{4,0},{8,12},{12,8},{16,20},{20,16},{24,28},{28,24},{1,5},{5... | collective-permute-start | bytes 688136 | tf_op jit(solution)/shard_map/ppermute | solution.py:162
  38.6 1.8 %collective-permute-start.11 = (bf16[2,112,512]{2,1,0:T(8,128)(2,1)S(1)}, bf16[2,112,512]{2,1,0:T(8,128)(2,1)S(1)}, u32[]{:S(2)}, u32[]{:S(2)}) collective-permute-start(bf16[2,112,512]{2,1,0:T(8,128)(2,1)S(1)} %get-tuple-element.47.refs_1_), channel_id=1, source_target_pairs={{0,4},{4,0},{8,12},{12,8},{16,20},{20,16},{24,28},{28,24},{1,5},{5... | collective-permute-start | bytes 688136 | tf_op jit(solution)/shard_map/ppermute | solution.py:162
  41.8 29.6 %collective-permute-start.21 = (bf16[448,1024]{1,0:T(8,128)(2,1)S(1)}, bf16[448,1024]{1,0:T(8,128)(2,1)S(1)}, u32[]{:S(2)}, u32[]{:S(2)}) collective-permute-start(bf16[448,1024]{1,0:T(8,128)(2,1)S(1)} %relay.1.refs_3_.refs_0_), channel_id=1, source_target_pairs={{1,0},{2,3},{5,4},{6,7},{9,8},{10,11},{13,12},{14,15},{17,16},{18,... | collective-permute-start | bytes 2752520 | tf_op jit(solution)/shard_map/ppermute | solution.py:376
  51.6 12.3 %collective-permute-start.16 = (bf16[448,512]{1,0:T(8,128)(2,1)S(1)}, bf16[448,512]{1,0:T(8,128)(2,1)S(1)}, u32[]{:S(2)}, u32[]{:S(2)}) collective-permute-start(bf16[448,512]{1,0:T(8,128)(2,1)S(1)} %add.30.refs_2_.refs_0_), channel_id=1, source_target_pairs={{0,16},{4,20},{8,24},{12,28},{16,0},{20,4},{24,8},{28,12},{1,17},{... | collective-permute-start | bytes 1376264 | tf_op jit(solution)/shard_map/ppermute | solution.py:162
  53.2 1.5 %collective-permute-start.12 = (bf16[224,512]{1,0:T(8,128)(2,1)S(1)}, bf16[224,512]{1,0:T(8,128)(2,1)S(1)}, u32[]{:S(2)}, u32[]{:S(2)}) collective-permute-start(bf16[224,512]{1,0:T(8,128)(2,1)S(1)} %get-tuple-element.49.refs_1_), channel_id=1, source_target_pairs={{0,4},{4,0},{8,12},{12,8},{16,20},{20,16},{24,28},{28,24},{1,5},{5... | collective-permute-start | bytes 688136 | tf_op jit(solution)/shard_map/ppermute | solution.py:162
  53.2 1.8 %collective-permute-start.13 = (bf16[224,512]{1,0:T(8,128)(2,1)S(1)}, bf16[224,512]{1,0:T(8,128)(2,1)S(1)}, u32[]{:S(2)}, u32[]{:S(2)}) collective-permute-start(bf16[224,512]{1,0:T(8,128)(2,1)S(1)} %get-tuple-element.50), channel_id=1, source_target_pairs={{0,4},{4,0},{8,12},{12,8},{16,20},{20,16},{24,28},{28,24},{1,5},{5... | collective-permute-start | bytes 688136 | tf_op jit(solution)/shard_map/ppermute | solution.py:162
  53.7 8.0 %collective-permute-start.17 = (bf16[112,512]{1,0:T(8,128)(2,1)S(1)}, bf16[112,512]{1,0:T(8,128)(2,1)S(1)}, u32[]{:S(2)}, u32[]{:S(2)}) collective-permute-start(bf16[112,512]{1,0:T(8,128)(2,1)S(1)} %merge.4.refs_0_), channel_id=1, source_target_pairs={{0,2},{1,3},{2,0},{3,1},{4,6},{5,7},{6,4},{7,5},{8,10},{9,11},{10,... | collective-permute-start | bytes 344072 | tf_op jit(solution)/shard_map/ppermute | solution.py:162
  55.2 10.4 %collective-permute-start.15 = (bf16[224,512]{1,0:T(8,128)(2,1)S(1)}, bf16[224,512]{1,0:T(8,128)(2,1)S(1)}, u32[]{:S(2)}, u32[]{:S(2)}) collective-permute-start(bf16[224,512]{1,0:T(8,128)(2,1)S(1)} %get-tuple-element.51.refs_5_.mine), channel_id=1, source_target_pairs={{0,8},{4,12},{8,0},{12,4},{16,24},{20,28},{24,16},{28,20},{1,9},{5... | collective-permute-start | bytes 688136 | tf_op jit(solution)/shard_map/ppermute | solution.py:162
  56.7 10.6 %collective-permute-start.18 = (bf16[224,512]{1,0:T(8,128)(2,1)S(1)}, bf16[224,512]{1,0:T(8,128)(2,1)S(1)}, u32[]{:S(2)}, u32[]{:S(2)}) collective-permute-start(bf16[224,512]{1,0:T(8,128)(2,1)S(1)} %get-tuple-element.54.mine), channel_id=1, source_target_pairs={{0,16},{4,20},{8,24},{12,28},{16,0},{20,4},{24,8},{28,12},{1,17},{... | collective-permute-start | bytes 688136 | tf_op jit(solution)/shard_map/ppermute | solution.py:162
  65.0 4.0 %collective-permute-start.22 = (bf16[2,112,512]{2,1,0:T(8,128)(2,1)S(1)}, bf16[2,112,512]{2,1,0:T(8,128)(2,1)S(1)}, u32[]{:S(2)}, u32[]{:S(2)}) collective-permute-start(bf16[2,112,512]{2,1,0:T(8,128)(2,1)S(1)} %get-tuple-element.53.refs_1_.refs_0_), channel_id=1, source_target_pairs={{0,4},{4,0},{8,12},{12,8},{16,20},{20,16},{24,28},{28,24},{1,5},{5... | collective-permute-start | bytes 688136 | tf_op jit(solution)/shard_map/ppermute | solution.py:162
  65.1 3.9 %collective-permute-start.23 = (bf16[2,112,512]{2,1,0:T(8,128)(2,1)S(1)}, bf16[2,112,512]{2,1,0:T(8,128)(2,1)S(1)}, u32[]{:S(2)}, u32[]{:S(2)}) collective-permute-start(bf16[2,112,512]{2,1,0:T(8,128)(2,1)S(1)} %get-tuple-element.56.refs_1_), channel_id=1, source_target_pairs={{0,4},{4,0},{8,12},{12,8},{16,20},{20,16},{24,28},{28,24},{1,5},{5... | collective-permute-start | bytes 688136 | tf_op jit(solution)/shard_map/ppermute | solution.py:162
  65.6 9.1 %collective-permute-start.19 = (bf16[224,512]{1,0:T(8,128)(2,1)S(1)}, bf16[224,512]{1,0:T(8,128)(2,1)S(1)}, u32[]{:S(2)}, u32[]{:S(2)}) collective-permute-start(bf16[224,512]{1,0:T(8,128)(2,1)S(1)} %add.32.refs_1_.refs_0_), channel_id=1, source_target_pairs={{0,16},{4,20},{8,24},{12,28},{16,0},{20,4},{24,8},{28,12},{1,17},{... | collective-permute-start | bytes 688136 | tf_op jit(solution)/shard_map/ppermute | solution.py:162
  67.4 7.4 %collective-permute-start.20 = (bf16[224,512]{1,0:T(8,128)(2,1)S(1)}, bf16[224,512]{1,0:T(8,128)(2,1)S(1)}, u32[]{:S(2)}, u32[]{:S(2)}) collective-permute-start(bf16[224,512]{1,0:T(8,128)(2,1)S(1)} %add.33.refs_5_.refs_1_), channel_id=1, source_target_pairs={{0,8},{4,12},{8,0},{12,4},{16,24},{20,28},{24,16},{28,20},{1,9},{5... | collective-permute-start | bytes 688136 | tf_op jit(solution)/shard_map/ppermute | solution.py:162
  73.1 2.5 %collective-permute-start.27 = (bf16[224,512]{1,0:T(8,128)(2,1)S(1)}, bf16[224,512]{1,0:T(8,128)(2,1)S(1)}, u32[]{:S(2)}, u32[]{:S(2)}) collective-permute-start(bf16[224,512]{1,0:T(8,128)(2,1)S(1)} %get-tuple-element.57.refs_7_), channel_id=1, source_target_pairs={{0,4},{4,0},{8,12},{12,8},{16,20},{20,16},{24,28},{28,24},{1,5},{5... | collective-permute-start | bytes 688136 | tf_op jit(solution)/shard_map/ppermute | solution.py:162
  73.2 2.5 %collective-permute-start.28 = (bf16[224,512]{1,0:T(8,128)(2,1)S(1)}, bf16[224,512]{1,0:T(8,128)(2,1)S(1)}, u32[]{:S(2)}, u32[]{:S(2)}) collective-permute-start(bf16[224,512]{1,0:T(8,128)(2,1)S(1)} %get-tuple-element.61), channel_id=1, source_target_pairs={{0,4},{4,0},{8,12},{12,8},{16,20},{20,16},{24,28},{28,24},{1,5},{5... | collective-permute-start | bytes 688136 | tf_op jit(solution)/shard_map/ppermute | solution.py:162
  75.7 9.9 %collective-permute-start.30 = (bf16[224,512]{1,0:T(8,128)(2,1)S(1)}, bf16[224,512]{1,0:T(8,128)(2,1)S(1)}, u32[]{:S(2)}, u32[]{:S(2)}) collective-permute-start(bf16[224,512]{1,0:T(8,128)(2,1)S(1)} %get-tuple-element.63.mine.refs_1_), channel_id=1, source_target_pairs={{0,8},{4,12},{8,0},{12,4},{16,24},{20,28},{24,16},{28,20},{1,9},{5... | collective-permute-start | bytes 688136 | tf_op jit(solution)/shard_map/ppermute | solution.py:162
  77.3 8.4 %collective-permute-start.29 = (bf16[224,512]{1,0:T(8,128)(2,1)S(1)}, bf16[224,512]{1,0:T(8,128)(2,1)S(1)}, u32[]{:S(2)}, u32[]{:S(2)}) collective-permute-start(bf16[224,512]{1,0:T(8,128)(2,1)S(1)} %get-tuple-element.62.mine), channel_id=1, source_target_pairs={{0,16},{4,20},{8,24},{12,28},{16,0},{20,4},{24,8},{28,12},{1,17},{... | collective-permute-start | bytes 688136 | tf_op jit(solution)/shard_map/ppermute | solution.py:162
  78.1 7.5 %collective-permute-start.26 = (bf16[112,512]{1,0:T(8,128)(2,1)S(1)}, bf16[112,512]{1,0:T(8,128)(2,1)S(1)}, u32[]{:S(2)}, u32[]{:S(2)}) collective-permute-start(bf16[112,512]{1,0:T(8,128)(2,1)S(1)} %merge.5.refs_3_), channel_id=1, source_target_pairs={{0,2},{1,3},{2,0},{3,1},{4,6},{5,7},{6,4},{7,5},{8,10},{9,11},{10,... | collective-permute-start | bytes 344072 | tf_op jit(solution)/shard_map/ppermute | solution.py:162
  79.4 7.6 %collective-permute-start.24 = (bf16[2,112,512]{2,1,0:T(8,128)(2,1)S(1)}, bf16[2,112,512]{2,1,0:T(8,128)(2,1)S(1)}, u32[]{:S(2)}, u32[]{:S(2)}) collective-permute-start(bf16[2,112,512]{2,1,0:T(8,128)(2,1)S(1)} %get-tuple-element.58.refs_2_.refs_0_), channel_id=1, source_target_pairs={{0,4},{4,0},{8,12},{12,8},{16,20},{20,16},{24,28},{28,24},{1,5},{5... | collective-permute-start | bytes 688136 | tf_op jit(solution)/shard_map/ppermute | solution.py:162
  79.4 7.6 %collective-permute-start.25 = (bf16[2,112,512]{2,1,0:T(8,128)(2,1)S(1)}, bf16[2,112,512]{2,1,0:T(8,128)(2,1)S(1)}, u32[]{:S(2)}, u32[]{:S(2)}) collective-permute-start(bf16[2,112,512]{2,1,0:T(8,128)(2,1)S(1)} %get-tuple-element.59.refs_1_), channel_id=1, source_target_pairs={{0,4},{4,0},{8,12},{12,8},{16,20},{20,16},{24,28},{28,24},{1,5},{5... | collective-permute-start | bytes 688136 | tf_op jit(solution)/shard_map/ppermute | solution.py:162
  85.8 7.4 %collective-permute-start.33 = (bf16[224,512]{1,0:T(8,128)(2,1)S(1)}, bf16[224,512]{1,0:T(8,128)(2,1)S(1)}, u32[]{:S(2)}, u32[]{:S(2)}) collective-permute-start(bf16[224,512]{1,0:T(8,128)(2,1)S(1)} %add.36.refs_7_.refs_1_), channel_id=1, source_target_pairs={{0,8},{4,12},{8,0},{12,4},{16,24},{20,28},{24,16},{28,20},{1,9},{5... | collective-permute-start | bytes 688136 | tf_op jit(solution)/shard_map/ppermute | solution.py:162
  86.4 7.1 %collective-permute-start.32 = (bf16[224,512]{1,0:T(8,128)(2,1)S(1)}, bf16[224,512]{1,0:T(8,128)(2,1)S(1)}, u32[]{:S(2)}, u32[]{:S(2)}) collective-permute-start(bf16[224,512]{1,0:T(8,128)(2,1)S(1)} %add.35.refs_1_.refs_0_), channel_id=1, source_target_pairs={{0,16},{4,20},{8,24},{12,28},{16,0},{20,4},{24,8},{28,12},{1,17},{... | collective-permute-start | bytes 688136 | tf_op jit(solution)/shard_map/ppermute | solution.py:162
  88.3 16.4 %copy-start.3 = (bf16[512,512]{1,0:T(8,128)(2,1)S(1)}, bf16[512,512]{1,0:T(8,128)(2,1)}, u32[]{:S(2)}) copy-start(bf16[512,512]{1,0:T(8,128)(2,1)} %refs_2_.5) | copy-start | bytes 1572868
  88.3 4.9 %collective-permute-start.31 = (bf16[112,512]{1,0:T(8,128)(2,1)S(1)}, bf16[112,512]{1,0:T(8,128)(2,1)S(1)}, u32[]{:S(2)}, u32[]{:S(2)}) collective-permute-start(bf16[112,512]{1,0:T(8,128)(2,1)S(1)} %get-tuple-element.65.refs_7_), channel_id=1, source_target_pairs={{0,1},{1,0},{2,3},{3,2},{4,5},{5,4},{6,7},{7,6},{8,9},{9,8},{10,11... | collective-permute-start | bytes 344072 | tf_op jit(solution)/shard_map/ppermute | solution.py:162
  94.4 1.6 %collective-permute-start.34 = (bf16[2,112,512]{2,1,0:T(8,128)(2,1)S(1)}, bf16[2,112,512]{2,1,0:T(8,128)(2,1)S(1)}, u32[]{:S(2)}, u32[]{:S(2)}) collective-permute-start(bf16[2,112,512]{2,1,0:T(8,128)(2,1)S(1)} %get-tuple-element.67.refs_0_.refs_7_), channel_id=1, source_target_pairs={{0,4},{4,0},{8,12},{12,8},{16,20},{20,16},{24,28},{28,24},{1,5},{5... | collective-permute-start | bytes 688136 | tf_op jit(solution)/shard_map/ppermute | solution.py:162
  94.4 1.8 %collective-permute-start.35 = (bf16[2,112,512]{2,1,0:T(8,128)(2,1)S(1)}, bf16[2,112,512]{2,1,0:T(8,128)(2,1)S(1)}, u32[]{:S(2)}, u32[]{:S(2)}) collective-permute-start(bf16[2,112,512]{2,1,0:T(8,128)(2,1)S(1)} %get-tuple-element.68.refs_1_), channel_id=1, source_target_pairs={{0,4},{4,0},{8,12},{12,8},{16,20},{20,16},{24,28},{28,24},{1,5},{5... | collective-permute-start | bytes 688136 | tf_op jit(solution)/shard_map/ppermute | solution.py:162
  97.6 7.1 %collective-permute-start.36 = (bf16[112,512]{1,0:T(8,128)(2,1)S(1)}, bf16[112,512]{1,0:T(8,128)(2,1)S(1)}, u32[]{:S(2)}, u32[]{:S(2)}) collective-permute-start(bf16[112,512]{1,0:T(8,128)(2,1)S(1)} %get-tuple-element.69.refs_1_), channel_id=1, source_target_pairs={{0,1},{1,0},{2,3},{3,2},{4,5},{5,4},{6,7},{7,6},{8,9},{9,8},{10,11... | collective-permute-start | bytes 344072 | tf_op jit(solution)/shard_map/ppermute | solution.py:162
  97.7 8.7 %collective-permute-start.37 = (bf16[112,512]{1,0:T(8,128)(2,1)S(1)}, bf16[112,512]{1,0:T(8,128)(2,1)S(1)}, u32[]{:S(2)}, u32[]{:S(2)}) collective-permute-start(bf16[112,512]{1,0:T(8,128)(2,1)S(1)} %add.37.refs_1_.refs_0_), channel_id=1, source_target_pairs={{0,2},{1,3},{2,0},{3,1},{4,6},{5,7},{6,4},{7,5},{8,10},{9,11},{10,... | collective-permute-start | bytes 344072 | tf_op jit(solution)/shard_map/ppermute | solution.py:162
  104.6 7.0 %collective-permute-start.38 = (bf16[112,512]{1,0:T(8,128)(2,1)S(1)}, bf16[112,512]{1,0:T(8,128)(2,1)S(1)}, u32[]{:S(2)}, u32[]{:S(2)}) collective-permute-start(bf16[112,512]{1,0:T(8,128)(2,1)S(1)} %add.38.refs_1_.refs_3_), channel_id=1, source_target_pairs={{0,2},{1,3},{2,0},{3,1},{4,6},{5,7},{6,4},{7,5},{8,10},{9,11},{10,... | collective-permute-start | bytes 344072 | tf_op jit(solution)/shard_map/ppermute | solution.py:162

commit v4 on v3

--- a/solution.py
+++ b/solution.py
@@ -19,7 +19,7 @@
     "down0", "sum0", "turn0", "down1:hop_b", "sum1", "residual", "hold", "see0",
     "merge0", "hop3", "down2:hop_d", "turn1", "sum2", "see1:far0", "turn2", "turn2",
     "merge1", "down3", "see2", "sum3", "turn3:far1", "turn3:far0", "merge2", "see3:pair2",
-    "merge3", "done2", "done3", "early",
+    "head3", "merge3", "done2", "done3", "early",
 )
 
 
@@ -98,17 +98,30 @@
     copy.wait()
 
 
-def _merge_kernel(half, blocks, late, first, info, *refs):
+def _head_kernel(half, blocks, info, *refs):
+    own, weight = refs[:blocks], refs[blocks]
+    here = pl.ds(pl.multiple_of(info[0] * half, half), half)
+    each = 4 // blocks
+    part = None
+    for k in range(4):
+        more = _dot(own[k // each][k % each], weight[k, here, :])
+        part = more if part is None else part + more
+    refs[-1][...] = part
+
+
+def _merge_kernel(half, blocks, late, first, head, info, *refs):
     own, other, weight = refs[:blocks], refs[blocks : 2 * blocks], refs[2 * blocks]
     mine = info[0]
     here = pl.ds(pl.multiple_of(mine * half, half), half)
     there = pl.ds(pl.multiple_of((1 - mine) * half, half), half)
 
     each = 4 // blocks
-    part = None
+    part = refs[2 * blocks + 3][...] if head else None
     for k in range(4):
         i, j = k // each, k % each
-        more = _dot(own[i][j], weight[k, here, :]) + _dot(other[i][j], weight[k, there, :])
+        more = _dot(other[i][j], weight[k, there, :])
+        if not head:
+            more = more + _dot(own[i][j], weight[k, here, :])
         part = more if part is None else part + more
     if late is None:
         refs[-1][...] = part.astype(BF)
@@ -267,12 +280,27 @@
             after[:] = [out[0]]
             return tuple(out)
 
-        def merge(own, other, weight, came=None, late=None, first=0):
+        def merge_head(own, weight):
+            count = own[0].shape[1]
+            part = pl.pallas_call(
+                functools.partial(_head_kernel, half, len(own)),
+                out_shape=_near((count, dec), F32),
+                in_specs=[SMEM] + [VMEM] * (len(own) + 1) + [ANY] * len(after),
+                out_specs=VMEM,
+                cost_estimate=LITTLE,
+                compiler_params=pltpu.CompilerParams(vmem_limit_bytes=ROOM),
+                name="merge_head",
+            )(info, *own, stay(weight), *after)
+            after[:] = [part]
+            return part
+
+        def merge(own, other, weight, came=None, late=None, first=0, head=None):
             count = own[0].shape[1]
             extra = [] if came is None else list(came)
-            outs = [_near((count, dec), BF)] + [_near((count, dec), F32)] * (len(extra) // 2)
+            extra += [] if head is None else [stay(head)]
+            outs = [_near((count, dec), BF)] + [_near((count, dec), F32)] * (came is not None)
             given = pl.pallas_call(
-                functools.partial(_merge_kernel, half, len(own), late, first),
+                functools.partial(_merge_kernel, half, len(own), late, first, head is not None),
                 out_shape=tuple(outs),
                 in_specs=[SMEM] + [VMEM] * (2 * len(own) + 1 + len(extra)) + [ANY] * len(after),
                 out_specs=(VMEM,) * len(outs),
@@ -412,8 +440,11 @@
             else:
                 block, first, _ = pieces[i]
                 late = block - 2, first // 4
-                give, v["part", i] = merge(v["seen", i], v["other", i], v["held"], (v["far", 0], v["far", 1]), *late)
+                give, v["part", i] = merge(v["seen", i], v["other", i], v["held"], (v["far", 0], v["far", 1]), *late, v.get(("head", i)))
                 v["pair", i] = pairs(give)
+
+        def project_head(i):
+            v["head", i] = merge_head(v["seen", i], v["held"])
 
         def complete(i):
             v["away", i] = add(v["part", i], v["pair", i])
@@ -435,6 +466,7 @@
             "turn": second_sum,
             "see": look,
             "merge": project,
+            "head": project_head,
             "done": complete,
         }
         for step in ORDER:

time: 113 us -> 113 us (level)
  transfers between devices with their start and end apart: 39 -> 39, of which waited for: 22 -> 21; matrix products, arithmetic and copies ran while one was open for 2% -> 2% of each run, Pallas kernels for 17% -> 18%
where the time goes in v4:
time: 113 us; the launch traced here: 112 us
  waiting for transfers between devices  52.2 us (46%)
  starting transfers between devices  31.9 us (28%)
  Pallas kernels  23.5 us (21%)
  local copies, waits for them, and re-layouts  3.55 us (3%)
    ppermute x35, waiting for transfers between devices, swap(): return lax.ppermute(x, axis, [(i, i ^ bit) for i in range(size)])  44.2 us
    ppermute x35, starting transfers between devices, swap(): return lax.ppermute(x, axis, [(i, i ^ bit) for i in range(size)])  27.9 us
    ppermute x1, waiting for transfers between devices, per_device(): v['hop_c'] = lax.ppermute(v['hop_b'], 'col', outward)  6.77 us
    pallas_call x4, Pallas kernels, down(): pl.pallas_call(functools.partial(_down_kernel, half, len(blocks), (parts,...  6.65 us
    pallas_call x4, Pallas kernels, merge(): pl.pallas_call(functools.partial(_merge_kernel, half, len(own), late, fir...  4.89 us
    pallas_call x4, Pallas kernels, see(): pl.pallas_call(functools.partial(_vision_kernel, len(mine_parts), parts),...  3.72 us
    unnamed x8, local copies, waits for them, and re-layouts  2.78 us
  transfers between devices with their start and end apart: 39, of which 21 were waited for; matrix products, arithmetic and copies ran while one was open for 2% of the time, Pallas kernels for 18%

profile of v4, /device:TPU:0, one launch (start us, length us, event | category | flops | bytes accessed | tf_op | source)
XLA Modules:
  0.0 112.5 jit_solution(6737203408545866196)
XLA Ops:
  0.0 3.0 %collective-permute-start.2 = (bf16[448,1024]{1,0:T(8,128)(2,1)}, bf16[448,1024]{1,0:T(8,128)(2,1)S(1)}, u32[]{:S(2)}, u32[]{:S(2)}) collective-permute-start(bf16[448,1024]{1,0:T(8,128)(2,1)} %refs_0_.1), channel_id=1, source_target_pairs={{0,1},{1,0},{2,3},{3,2},{4,5},{5,4},{6,7},{7,6},{8,9},{9,8},{10,11... | collective-permute-start | bytes 2752520 | tf_op jit(solution)/shard_map/ppermute | solution.py:175
  4.5 0.9 broadcast_select_fusion.3
  5.5 1.6 %copy-done = bf16[1024,1024]{1,0:T(8,128)(2,1)S(1)} copy-done((bf16[1024,1024]{1,0:T(8,128)(2,1)S(1)}, bf16[1024,1024]{1,0:T(8,128)(2,1)}, u32[]{:S(2)}) %copy-start) | copy-done | bytes 2097176
  7.1 1.2 %copy-done.2 = bf16[448,1024]{1,0:T(8,128)(2,1)S(1)} copy-done((bf16[448,1024]{1,0:T(8,128)(2,1)S(1)}, bf16[448,1024]{1,0:T(8,128)(2,1)}, u32[]{:S(2)}) %copy-start.2) | copy-done | bytes 917528
  8.3 1.7 %down.4 = (bf16[224,512]{1,0:T(8,128)(2,1)S(1)}, bf16[224,512]{1,0:T(8,128)(2,1)S(1)}, f32[448,512]{1,0:T(8,128)S(1)}) custom-call(s32[7]{0:T(128)S(1)} %stack.35.info.refs_4_.refs_6_, bf16[448,1024]{1,0:T(8,128)(2,1)S(1)} %copy-done.2, bf16[1024,1024]{1,0:T(8,128)(2,1)S(1)} %copy-done, bf16[1,1024]{1,0:T(2,128)(2,1)S(1)} %broadcast_in_dim.7.refs_2_.refs_3_.refs_5_, ...), custom_call_target="tpu_custom_call" | custom-call | flops 1 | bytes 1 | tf_op jit(solution)/shard_map/down/pallas_call | solution.py:241
  10.5 1.0 collective-permute-done.4.refs_0_
  11.9 1.6 %collective-permute-start.6 = (bf16[448,512]{1,0:T(8,128)(2,1)S(1)}, bf16[448,512]{1,0:T(8,128)(2,1)S(1)}, u32[]{:S(2)}, u32[]{:S(2)}) collective-permute-start(bf16[448,512]{1,0:T(8,128)(2,1)S(1)} %add.27.mine.refs_1_), channel_id=1, source_target_pairs={{0,8},{4,12},{8,0},{12,4},{16,24},{20,28},{24,16},{28,20},{1,9},{5... | collective-permute-start | bytes 1376264 | tf_op jit(solution)/shard_map/ppermute | solution.py:175
  13.5 10.1 %collective-permute-done.2.refs_0_ = bf16[448,1024]{1,0:T(8,128)(2,1)S(1)} collective-permute-done((bf16[448,1024]{1,0:T(8,128)(2,1)}, bf16[448,1024]{1,0:T(8,128)(2,1)S(1)}, u32[]{:S(2)}, u32[]{:S(2)}) %collective-permute-start.2) | collective-permute-done | bytes 917536 | tf_op jit(solution)/shard_map/ppermute | solution.py:175
  24.3 1.3 %collective-permute-start.1 = (bf16[448,1024]{1,0:T(8,128)(2,1)S(1)}, bf16[448,1024]{1,0:T(8,128)(2,1)S(1)}, u32[]{:S(2)}, u32[]{:S(2)}) collective-permute-start(bf16[448,1024]{1,0:T(8,128)(2,1)S(1)} %collective-permute-done.refs_3_.refs_0_), channel_id=1, source_target_pairs={{1,0},{2,3},{5,4},{6,7},{9,8},{10,11},{13,12},{14,15},{17,16},{18,... | collective-permute-start | bytes 2752520 | tf_op jit(solution)/shard_map/ppermute | solution.py:399
  25.7 1.8 %collective-permute-start.7 = (bf16[448,512]{1,0:T(8,128)(2,1)S(1)}, bf16[448,512]{1,0:T(8,128)(2,1)S(1)}, u32[]{:S(2)}, u32[]{:S(2)}) collective-permute-start(bf16[448,512]{1,0:T(8,128)(2,1)S(1)} %add.28.refs_2_.refs_0_), channel_id=1, source_target_pairs={{0,16},{4,20},{8,24},{12,28},{16,0},{20,4},{24,8},{28,12},{1,17},{... | collective-permute-start | bytes 1376264 | tf_op jit(solution)/shard_map/ppermute | solution.py:175
  27.5 1.7 %down.5 = (bf16[224,512]{1,0:T(8,128)(2,1)S(1)}, bf16[224,512]{1,0:T(8,128)(2,1)S(1)}, f32[448,512]{1,0:T(8,128)S(1)}) custom-call(s32[7]{0:T(128)S(1)} %stack.35.info.refs_4_.refs_6_, bf16[448,1024]{1,0:T(8,128)(2,1)S(1)} %collective-permute-done.2.refs_0_, bf16[1024,1024]{1,0:T(8,128)(2,1)S(1)} %copy-done.1, bf16[448,512]{1,0:T(8,128)(2,1)S(1)} %add.28.refs_2_.refs_0_, ...), custom_call_target="tpu_custom_call" | custom-call | flops 1 | bytes 1 | tf_op jit(solution)/shard_map/down/pallas_call | solution.py:241
  29.7 1.0 collective-permute-done.8.refs_0_
  31.1 1.6 %collective-permute-start.14 = (bf16[448,512]{1,0:T(8,128)(2,1)S(1)}, bf16[448,512]{1,0:T(8,128)(2,1)S(1)}, u32[]{:S(2)}, u32[]{:S(2)}) collective-permute-start(bf16[448,512]{1,0:T(8,128)(2,1)S(1)} %add.29.refs_0_.mine), channel_id=1, source_target_pairs={{0,8},{4,12},{8,0},{12,4},{16,24},{20,28},{24,16},{28,20},{1,9},{5... | collective-permute-start | bytes 1376264 | tf_op jit(solution)/shard_map/ppermute | solution.py:175
  32.7 2.0 %residuals.1 = (bf16[448,512]{1,0:T(8,128)(2,1)S(1)}, bf16[448,512]{1,0:T(8,128)(2,1)S(1)}, bf16[448,512]{1,0:T(8,128)(2,1)S(1)}, bf16[448,512]{1,0:T(8,128)(2,1)S(1)}) custom-call(s32[7]{0:T(128)S(1)} %stack.35.info.refs_4_.refs_6_, bf16[1792,1024]{1,0:T(8,128)(2,1)} %tokens.1, bf16[448,512]{1,0:T(8,128)(2,1)S(1)} %add.29.refs_0_.mine), custom_call_target="tpu_custom_call" | custom-call | flops 1 | bytes 1 | tf_op jit(solution)/shard_map/residuals/pallas_call | solution.py:211
  34.7 2.2 %hold.1.refs_5_.refs_4_.refs_2_ = bf16[4,1024,512]{2,1,0:T(8,128)(2,1)S(1)} custom-call(bf16[4,1024,512]{2,1,0:T(8,128)(2,1)} %weight.1, bf16[448,512]{1,0:T(8,128)(2,1)S(1)} %get-tuple-element.45.refs_0_.refs_2_), custom_call_target="tpu_custom_call" | custom-call | flops 1 | bytes 1 | tf_op jit(solution)/shard_map/hold/pallas_call | solution.py:197
  37.5 1.0 vision.4
  39.1 1.0 collective-permute-done.10.refs_2_
  40.4 1.3 %merge.4.refs_0_ = bf16[112,512]{1,0:T(8,128)(2,1)S(1)} custom-call(s32[7]{0:T(128)S(1)} %stack.35.info.refs_4_.refs_6_, bf16[2,112,512]{2,1,0:T(8,128)(2,1)S(1)} %get-tuple-element.46.refs_0_.refs_5_, bf16[2,112,512]{2,1,0:T(8,128)(2,1)S(1)} %get-tuple-element.47.refs_1_, bf16[2,112,512]{2,1,0:T(8,128)(2,1)S(1)} %collective-permute-done.10.refs_2_, ...), custom_call_target="tpu_custom_call" | custom-call | flops 1 | bytes 1 | tf_op jit(solution)/shard_map/merge/pallas_call | solution.py:302
  41.8 1.3 %collective-permute-start.21 = (bf16[448,1024]{1,0:T(8,128)(2,1)S(1)}, bf16[448,1024]{1,0:T(8,128)(2,1)S(1)}, u32[]{:S(2)}, u32[]{:S(2)}) collective-permute-start(bf16[448,1024]{1,0:T(8,128)(2,1)S(1)} %relay.1.refs_3_.refs_0_), channel_id=1, source_target_pairs={{1,0},{2,3},{5,4},{6,7},{9,8},{10,11},{13,12},{14,15},{17,16},{18,... | collective-permute-start | bytes 2752520 | tf_op jit(solution)/shard_map/ppermute | solution.py:404
  43.1 6.8 %collective-permute-done.1.refs_1_ = bf16[448,1024]{1,0:T(8,128)(2,1)S(1)} collective-permute-done((bf16[448,1024]{1,0:T(8,128)(2,1)S(1)}, bf16[448,1024]{1,0:T(8,128)(2,1)S(1)}, u32[]{:S(2)}, u32[]{:S(2)}) %collective-permute-start.1) | collective-permute-done | bytes 917536 | tf_op jit(solution)/shard_map/ppermute | solution.py:399
  49.8 1.7 %down.6 = (bf16[224,512]{1,0:T(8,128)(2,1)S(1)}, bf16[224,512]{1,0:T(8,128)(2,1)S(1)}, f32[448,512]{1,0:T(8,128)S(1)}) custom-call(s32[7]{0:T(128)S(1)} %stack.35.info.refs_4_.refs_6_, bf16[448,1024]{1,0:T(8,128)(2,1)S(1)} %collective-permute-done.refs_3_.refs_0_, bf16[448,1024]{1,0:T(8,128)(2,1)S(1)} %collective-permute-done.1.refs_1_, ...), custom_call_target="tpu_custom_call" | custom-call | flops 1 | bytes 1 | tf_op jit(solution)/shard_map/down/pallas_call | solution.py:241
  51.6 1.6 %collective-permute-start.16 = (bf16[448,512]{1,0:T(8,128)(2,1)S(1)}, bf16[448,512]{1,0:T(8,128)(2,1)S(1)}, u32[]{:S(2)}, u32[]{:S(2)}) collective-permute-start(bf16[448,512]{1,0:T(8,128)(2,1)S(1)} %add.30.refs_2_.refs_0_), channel_id=1, source_target_pairs={{0,16},{4,20},{8,24},{12,28},{16,0},{20,4},{24,8},{28,12},{1,17},{... | collective-permute-start | bytes 1376264 | tf_op jit(solution)/shard_map/ppermute | solution.py:175
  53.7 1.0 collective-permute-start.17
  55.2 1.6 %collective-permute-start.15 = (bf16[224,512]{1,0:T(8,128)(2,1)S(1)}, bf16[224,512]{1,0:T(8,128)(2,1)S(1)}, u32[]{:S(2)}, u32[]{:S(2)}) collective-permute-start(bf16[224,512]{1,0:T(8,128)(2,1)S(1)} %get-tuple-element.51.refs_5_.mine), channel_id=1, source_target_pairs={{0,8},{4,12},{8,0},{12,4},{16,24},{20,28},{24,16},{28,20},{1,9},{5... | collective-permute-start | bytes 688136 | tf_op jit(solution)/shard_map/ppermute | solution.py:175
  57.2 4.5 %collective-permute-done.17.refs_6_.refs_2_.refs_5_ = bf16[112,512]{1,0:T(8,128)(2,1)S(1)} collective-permute-done((bf16[112,512]{1,0:T(8,128)(2,1)S(1)}, bf16[112,512]{1,0:T(8,128)(2,1)S(1)}, u32[]{:S(2)}, u32[]{:S(2)}) %collective-permute-start.17) | collective-permute-done | bytes 114720 | tf_op jit(solution)/shard_map/ppermute | solution.py:175
  61.7 2.2 %collective-permute-done.16.refs_1_ = bf16[448,512]{1,0:T(8,128)(2,1)S(1)} collective-permute-done((bf16[448,512]{1,0:T(8,128)(2,1)S(1)}, bf16[448,512]{1,0:T(8,128)(2,1)S(1)}, u32[]{:S(2)}, u32[]{:S(2)}) %collective-permute-start.16) | collective-permute-done | bytes 458784 | tf_op jit(solution)/shard_map/ppermute | solution.py:175
  64.0 1.0 vision.5
  65.6 1.7 %collective-permute-start.19 = (bf16[224,512]{1,0:T(8,128)(2,1)S(1)}, bf16[224,512]{1,0:T(8,128)(2,1)S(1)}, u32[]{:S(2)}, u32[]{:S(2)}) collective-permute-start(bf16[224,512]{1,0:T(8,128)(2,1)S(1)} %add.32.refs_1_.refs_0_), channel_id=1, source_target_pairs={{0,16},{4,20},{8,24},{12,28},{16,0},{20,4},{24,8},{28,12},{1,17},{... | collective-permute-start | bytes 688136 | tf_op jit(solution)/shard_map/ppermute | solution.py:175
  67.4 1.6 %collective-permute-start.20 = (bf16[224,512]{1,0:T(8,128)(2,1)S(1)}, bf16[224,512]{1,0:T(8,128)(2,1)S(1)}, u32[]{:S(2)}, u32[]{:S(2)}) collective-permute-start(bf16[224,512]{1,0:T(8,128)(2,1)S(1)} %add.33.refs_5_.refs_1_), channel_id=1, source_target_pairs={{0,8},{4,12},{8,0},{12,4},{16,24},{20,28},{24,16},{28,20},{1,9},{5... | collective-permute-start | bytes 688136 | tf_op jit(solution)/shard_map/ppermute | solution.py:175
  68.9 1.3 %merge.5.refs_3_ = bf16[112,512]{1,0:T(8,128)(2,1)S(1)} custom-call(s32[7]{0:T(128)S(1)} %stack.35.info.refs_4_.refs_6_, bf16[2,112,512]{2,1,0:T(8,128)(2,1)S(1)} %get-tuple-element.53.refs_1_.refs_0_, bf16[2,112,512]{2,1,0:T(8,128)(2,1)S(1)} %get-tuple-element.56.refs_1_, bf16[2,112,512]{2,1,0:T(8,128)(2,1)S(1)} %collective-permute-done.22.refs_2_, ...), custom_call_target="tpu_custom_call" | custom-call | flops 1 | bytes 1 | tf_op jit(solution)/shard_map/merge/pallas_call | solution.py:302
  70.2 1.2 %collective-permute-done.21.refs_1_ = bf16[448,1024]{1,0:T(8,128)(2,1)S(1)} collective-permute-done((bf16[448,1024]{1,0:T(8,128)(2,1)S(1)}, bf16[448,1024]{1,0:T(8,128)(2,1)S(1)}, u32[]{:S(2)}, u32[]{:S(2)}) %collective-permute-start.21) | collective-permute-done | bytes 917536 | tf_op jit(solution)/shard_map/ppermute | solution.py:404
  71.4 1.7 %down.7 = (bf16[224,512]{1,0:T(8,128)(2,1)S(1)}, bf16[224,512]{1,0:T(8,128)(2,1)S(1)}, f32[448,512]{1,0:T(8,128)S(1)}) custom-call(s32[7]{0:T(128)S(1)} %stack.35.info.refs_4_.refs_6_, bf16[448,1024]{1,0:T(8,128)(2,1)S(1)} %relay.1.refs_3_.refs_0_, bf16[448,1024]{1,0:T(8,128)(2,1)S(1)} %collective-permute-done.21.refs_1_, bf16[1024,1024]{1,0:T(8,128)(2,1)S(1)} %copy-done.1, ...), custom_call_target="tpu_custom_call" | custom-call | flops 1 | bytes 1 | tf_op jit(solution)/shard_map/down/pallas_call | solution.py:241
  73.7 1.1 collective-permute-done.20.refs_3_
  74.8 0.9 vision.6
  75.7 1.6 %collective-permute-start.30 = (bf16[224,512]{1,0:T(8,128)(2,1)S(1)}, bf16[224,512]{1,0:T(8,128)(2,1)S(1)}, u32[]{:S(2)}, u32[]{:S(2)}) collective-permute-start(bf16[224,512]{1,0:T(8,128)(2,1)S(1)} %get-tuple-element.63.mine.refs_1_), channel_id=1, source_target_pairs={{0,8},{4,12},{8,0},{12,4},{16,24},{20,28},{24,16},{28,20},{1,9},{5... | collective-permute-start | bytes 688136 | tf_op jit(solution)/shard_map/ppermute | solution.py:175
  77.3 0.8 collective-permute-start.29
  78.1 1.2 %collective-permute-start.26 = (bf16[112,512]{1,0:T(8,128)(2,1)S(1)}, bf16[112,512]{1,0:T(8,128)(2,1)S(1)}, u32[]{:S(2)}, u32[]{:S(2)}) collective-permute-start(bf16[112,512]{1,0:T(8,128)(2,1)S(1)} %merge.5.refs_3_), channel_id=1, source_target_pairs={{0,2},{1,3},{2,0},{3,1},{4,6},{5,7},{6,4},{7,5},{8,10},{9,11},{10,... | collective-permute-start | bytes 344072 | tf_op jit(solution)/shard_map/ppermute | solution.py:175
  79.9 5.7 %collective-permute-done.26.refs_2_.refs_6_ = bf16[112,512]{1,0:T(8,128)(2,1)S(1)} collective-permute-done((bf16[112,512]{1,0:T(8,128)(2,1)S(1)}, bf16[112,512]{1,0:T(8,128)(2,1)S(1)}, u32[]{:S(2)}, u32[]{:S(2)}) %collective-permute-start.26) | collective-permute-done | bytes 114720 | tf_op jit(solution)/shard_map/ppermute | solution.py:175
  87.0 1.3 %merge.6 = (bf16[112,512]{1,0:T(8,128)(2,1)S(1)}, f32[112,512]{1,0:T(8,128)S(1)}) custom-call(s32[7]{0:T(128)S(1)} %stack.35.info.refs_4_.refs_6_, bf16[2,112,512]{2,1,0:T(8,128)(2,1)S(1)} %get-tuple-element.58.refs_2_.refs_0_, bf16[2,112,512]{2,1,0:T(8,128)(2,1)S(1)} %get-tuple-element.59.refs_1_, bf16[2,112,512]{2,1,0:T(8,128)(2,1)S(1)} %collective-permute-done.24.refs_2_, ...), custom_call_target="tpu_custom_call" | custom-call | flops 1 | bytes 1 | tf_op jit(solution)/shard_map/merge/pallas_call | solution.py:302
  88.4 4.8 %collective-permute-done.31.refs_8_.refs_0_ = bf16[112,512]{1,0:T(8,128)(2,1)S(1)} collective-permute-done((bf16[112,512]{1,0:T(8,128)(2,1)S(1)}, bf16[112,512]{1,0:T(8,128)(2,1)S(1)}, u32[]{:S(2)}, u32[]{:S(2)}) %collective-permute-start.31) | collective-permute-done | bytes 114720 | tf_op jit(solution)/shard_map/ppermute | solution.py:175
  93.5 0.9 vision.7
  94.9 1.0 merge_head.1.refs_7_.refs_8_
  96.3 1.0 merge.7
  97.4 2.6 %collective-permute-start.37 = (bf16[112,512]{1,0:T(8,128)(2,1)S(1)}, bf16[112,512]{1,0:T(8,128)(2,1)S(1)}, u32[]{:S(2)}, u32[]{:S(2)}) collective-permute-start(bf16[112,512]{1,0:T(8,128)(2,1)S(1)} %add.37.refs_1_.refs_0_), channel_id=1, source_target_pairs={{0,2},{1,3},{2,0},{3,1},{4,6},{5,7},{6,4},{7,5},{8,10},{9,11},{10,... | collective-permute-start | bytes 344072 | tf_op jit(solution)/shard_map/ppermute | solution.py:175
  100.0 4.3 %collective-permute-done.36.refs_0_ = bf16[112,512]{1,0:T(8,128)(2,1)S(1)} collective-permute-done((bf16[112,512]{1,0:T(8,128)(2,1)S(1)}, bf16[112,512]{1,0:T(8,128)(2,1)S(1)}, u32[]{:S(2)}, u32[]{:S(2)}) %collective-permute-start.36) | collective-permute-done | bytes 114720 | tf_op jit(solution)/shard_map/ppermute | solution.py:175
  104.4 1.0 place_early.1
  106.1 5.3 %collective-permute-done.38.refs_1_ = bf16[112,512]{1,0:T(8,128)(2,1)S(1)} collective-permute-done((bf16[112,512]{1,0:T(8,128)(2,1)S(1)}, bf16[112,512]{1,0:T(8,128)(2,1)S(1)}, u32[]{:S(2)}, u32[]{:S(2)}) %collective-permute-start.38) | collective-permute-done | bytes 114720 | tf_op jit(solution)/shard_map/ppermute | solution.py:175
  111.4 1.1 place_late.1
  (72 shorter events, 12.8 us)
Async XLA Ops:
  0.0 23.6 %collective-permute-start.2 = (bf16[448,1024]{1,0:T(8,128)(2,1)}, bf16[448,1024]{1,0:T(8,128)(2,1)S(1)}, u32[]{:S(2)}, u32[]{:S(2)}) collective-permute-start(bf16[448,1024]{1,0:T(8,128)(2,1)} %refs_0_.1), channel_id=1, source_target_pairs={{0,1},{1,0},{2,3},{3,2},{4,5},{5,4},{6,7},{7,6},{8,9},{9,8},{10,11... | collective-permute-start | bytes 2752520 | tf_op jit(solution)/shard_map/ppermute | solution.py:175
  3.0 21.3 %collective-permute-start = (bf16[448,1024]{1,0:T(8,128)(2,1)}, bf16[448,1024]{1,0:T(8,128)(2,1)S(1)}, u32[]{:S(2)}, u32[]{:S(2)}) collective-permute-start(bf16[448,1024]{1,0:T(8,128)(2,1)} %refs_0_.1), channel_id=1, source_target_pairs={{1,2},{2,1},{5,6},{6,5},{9,10},{10,9},{13,14},{14,13},{17,18},{18,... | collective-permute-start | bytes 2752520 | tf_op jit(solution)/shard_map/ppermute | solution.py:398
  5.5 1.6 %copy-start = (bf16[1024,1024]{1,0:T(8,128)(2,1)S(1)}, bf16[1024,1024]{1,0:T(8,128)(2,1)}, u32[]{:S(2)}) copy-start(bf16[1024,1024]{1,0:T(8,128)(2,1)} %refs_2_.4) | copy-start | bytes 6291460
  7.1 1.2 %copy-start.2 = (bf16[448,1024]{1,0:T(8,128)(2,1)S(1)}, bf16[448,1024]{1,0:T(8,128)(2,1)}, u32[]{:S(2)}) copy-start(bf16[448,1024]{1,0:T(8,128)(2,1)} %refs_0_.1) | copy-start | bytes 2752516
  8.3 19.2 %copy-start.1 = (bf16[1024,1024]{1,0:T(8,128)(2,1)S(1)}, bf16[1024,1024]{1,0:T(8,128)(2,1)}, u32[]{:S(2)}) copy-start(bf16[1024,1024]{1,0:T(8,128)(2,1)} %refs_2_.4) | copy-start | bytes 6291460
  10.0 1.6 %collective-permute-start.4 = (bf16[224,512]{1,0:T(8,128)(2,1)S(1)}, bf16[224,512]{1,0:T(8,128)(2,1)S(1)}, u32[]{:S(2)}, u32[]{:S(2)}) collective-permute-start(bf16[224,512]{1,0:T(8,128)(2,1)S(1)} %get-tuple-element.40.refs_2_), channel_id=1, source_target_pairs={{0,4},{4,0},{8,12},{12,8},{16,20},{20,16},{24,28},{28,24},{1,5},{5... | collective-permute-start | bytes 688136 | tf_op jit(solution)/shard_map/ppermute | solution.py:175
  10.0 1.8 %collective-permute-start.5 = (bf16[224,512]{1,0:T(8,128)(2,1)S(1)}, bf16[224,512]{1,0:T(8,128)(2,1)S(1)}, u32[]{:S(2)}, u32[]{:S(2)}) collective-permute-start(bf16[224,512]{1,0:T(8,128)(2,1)S(1)} %get-tuple-element.41), channel_id=1, source_target_pairs={{0,4},{4,0},{8,12},{12,8},{16,20},{20,16},{24,28},{28,24},{1,5},{5... | collective-permute-start | bytes 688136 | tf_op jit(solution)/shard_map/ppermute | solution.py:175
  11.9 13.7 %collective-permute-start.6 = (bf16[448,512]{1,0:T(8,128)(2,1)S(1)}, bf16[448,512]{1,0:T(8,128)(2,1)S(1)}, u32[]{:S(2)}, u32[]{:S(2)}) collective-permute-start(bf16[448,512]{1,0:T(8,128)(2,1)S(1)} %add.27.mine.refs_1_), channel_id=1, source_target_pairs={{0,8},{4,12},{8,0},{12,4},{16,24},{20,28},{24,16},{28,20},{1,9},{5... | collective-permute-start | bytes 1376264 | tf_op jit(solution)/shard_map/ppermute | solution.py:175
  23.6 18.1 %collective-permute-start.3 = (bf16[448,1024]{1,0:T(8,128)(2,1)S(1)}, bf16[448,1024]{1,0:T(8,128)(2,1)S(1)}, u32[]{:S(2)}, u32[]{:S(2)}) collective-permute-start(bf16[448,1024]{1,0:T(8,128)(2,1)S(1)} %collective-permute-done.2.refs_0_), channel_id=1, source_target_pairs={{1,2},{2,1},{5,6},{6,5},{9,10},{10,9},{13,14},{14,13},{17,18},{18,... | collective-permute-start | bytes 2752520 | tf_op jit(solution)/shard_map/ppermute | solution.py:400
  24.3 25.5 %collective-permute-start.1 = (bf16[448,1024]{1,0:T(8,128)(2,1)S(1)}, bf16[448,1024]{1,0:T(8,128)(2,1)S(1)}, u32[]{:S(2)}, u32[]{:S(2)}) collective-permute-start(bf16[448,1024]{1,0:T(8,128)(2,1)S(1)} %collective-permute-done.refs_3_.refs_0_), channel_id=1, source_target_pairs={{1,0},{2,3},{5,4},{6,7},{9,8},{10,11},{13,12},{14,15},{17,16},{18,... | collective-permute-start | bytes 2752520 | tf_op jit(solution)/shard_map/ppermute | solution.py:399
  25.7 11.8 %collective-permute-start.7 = (bf16[448,512]{1,0:T(8,128)(2,1)S(1)}, bf16[448,512]{1,0:T(8,128)(2,1)S(1)}, u32[]{:S(2)}, u32[]{:S(2)}) collective-permute-start(bf16[448,512]{1,0:T(8,128)(2,1)S(1)} %add.28.refs_2_.refs_0_), channel_id=1, source_target_pairs={{0,16},{4,20},{8,24},{12,28},{16,0},{20,4},{24,8},{28,12},{1,17},{... | collective-permute-start | bytes 1376264 | tf_op jit(solution)/shard_map/ppermute | solution.py:175
  29.2 1.6 %collective-permute-start.8 = (bf16[224,512]{1,0:T(8,128)(2,1)S(1)}, bf16[224,512]{1,0:T(8,128)(2,1)S(1)}, u32[]{:S(2)}, u32[]{:S(2)}) collective-permute-start(bf16[224,512]{1,0:T(8,128)(2,1)S(1)} %get-tuple-element.43.refs_2_), channel_id=1, source_target_pairs={{0,4},{4,0},{8,12},{12,8},{16,20},{20,16},{24,28},{28,24},{1,5},{5... | collective-permute-start | bytes 688136 | tf_op jit(solution)/shard_map/ppermute | solution.py:175
  29.2 1.8 %collective-permute-start.9 = (bf16[224,512]{1,0:T(8,128)(2,1)S(1)}, bf16[224,512]{1,0:T(8,128)(2,1)S(1)}, u32[]{:S(2)}, u32[]{:S(2)}) collective-permute-start(bf16[224,512]{1,0:T(8,128)(2,1)S(1)} %get-tuple-element.44), channel_id=1, source_target_pairs={{0,4},{4,0},{8,12},{12,8},{16,20},{20,16},{24,28},{28,24},{1,5},{5... | collective-permute-start | bytes 688136 | tf_op jit(solution)/shard_map/ppermute | solution.py:175
  31.1 20.4 %collective-permute-start.14 = (bf16[448,512]{1,0:T(8,128)(2,1)S(1)}, bf16[448,512]{1,0:T(8,128)(2,1)S(1)}, u32[]{:S(2)}, u32[]{:S(2)}) collective-permute-start(bf16[448,512]{1,0:T(8,128)(2,1)S(1)} %add.29.refs_0_.mine), channel_id=1, source_target_pairs={{0,8},{4,12},{8,0},{12,4},{16,24},{20,28},{24,16},{28,20},{1,9},{5... | collective-permute-start | bytes 1376264 | tf_op jit(solution)/shard_map/ppermute | solution.py:175
  38.5 1.6 %collective-permute-start.10 = (bf16[2,112,512]{2,1,0:T(8,128)(2,1)S(1)}, bf16[2,112,512]{2,1,0:T(8,128)(2,1)S(1)}, u32[]{:S(2)}, u32[]{:S(2)}) collective-permute-start(bf16[2,112,512]{2,1,0:T(8,128)(2,1)S(1)} %get-tuple-element.46.refs_0_.refs_5_), channel_id=1, source_target_pairs={{0,4},{4,0},{8,12},{12,8},{16,20},{20,16},{24,28},{28,24},{1,5},{5... | collective-permute-start | bytes 688136 | tf_op jit(solution)/shard_map/ppermute | solution.py:175
  38.6 1.8 %collective-permute-start.11 = (bf16[2,112,512]{2,1,0:T(8,128)(2,1)S(1)}, bf16[2,112,512]{2,1,0:T(8,128)(2,1)S(1)}, u32[]{:S(2)}, u32[]{:S(2)}) collective-permute-start(bf16[2,112,512]{2,1,0:T(8,128)(2,1)S(1)} %get-tuple-element.47.refs_1_), channel_id=1, source_target_pairs={{0,4},{4,0},{8,12},{12,8},{16,20},{20,16},{24,28},{28,24},{1,5},{5... | collective-permute-start | bytes 688136 | tf_op jit(solution)/shard_map/ppermute | solution.py:175
  41.8 29.6 %collective-permute-start.21 = (bf16[448,1024]{1,0:T(8,128)(2,1)S(1)}, bf16[448,1024]{1,0:T(8,128)(2,1)S(1)}, u32[]{:S(2)}, u32[]{:S(2)}) collective-permute-start(bf16[448,1024]{1,0:T(8,128)(2,1)S(1)} %relay.1.refs_3_.refs_0_), channel_id=1, source_target_pairs={{1,0},{2,3},{5,4},{6,7},{9,8},{10,11},{13,12},{14,15},{17,16},{18,... | collective-permute-start | bytes 2752520 | tf_op jit(solution)/shard_map/ppermute | solution.py:404
  51.6 12.3 %collective-permute-start.16 = (bf16[448,512]{1,0:T(8,128)(2,1)S(1)}, bf16[448,512]{1,0:T(8,128)(2,1)S(1)}, u32[]{:S(2)}, u32[]{:S(2)}) collective-permute-start(bf16[448,512]{1,0:T(8,128)(2,1)S(1)} %add.30.refs_2_.refs_0_), channel_id=1, source_target_pairs={{0,16},{4,20},{8,24},{12,28},{16,0},{20,4},{24,8},{28,12},{1,17},{... | collective-permute-start | bytes 1376264 | tf_op jit(solution)/shard_map/ppermute | solution.py:175
  53.2 1.5 %collective-permute-start.12 = (bf16[224,512]{1,0:T(8,128)(2,1)S(1)}, bf16[224,512]{1,0:T(8,128)(2,1)S(1)}, u32[]{:S(2)}, u32[]{:S(2)}) collective-permute-start(bf16[224,512]{1,0:T(8,128)(2,1)S(1)} %get-tuple-element.49.refs_1_), channel_id=1, source_target_pairs={{0,4},{4,0},{8,12},{12,8},{16,20},{20,16},{24,28},{28,24},{1,5},{5... | collective-permute-start | bytes 688136 | tf_op jit(solution)/shard_map/ppermute | solution.py:175
  53.2 1.8 %collective-permute-start.13 = (bf16[224,512]{1,0:T(8,128)(2,1)S(1)}, bf16[224,512]{1,0:T(8,128)(2,1)S(1)}, u32[]{:S(2)}, u32[]{:S(2)}) collective-permute-start(bf16[224,512]{1,0:T(8,128)(2,1)S(1)} %get-tuple-element.50), channel_id=1, source_target_pairs={{0,4},{4,0},{8,12},{12,8},{16,20},{20,16},{24,28},{28,24},{1,5},{5... | collective-permute-start | bytes 688136 | tf_op jit(solution)/shard_map/ppermute | solution.py:175
  53.7 8.0 %collective-permute-start.17 = (bf16[112,512]{1,0:T(8,128)(2,1)S(1)}, bf16[112,512]{1,0:T(8,128)(2,1)S(1)}, u32[]{:S(2)}, u32[]{:S(2)}) collective-permute-start(bf16[112,512]{1,0:T(8,128)(2,1)S(1)} %merge.4.refs_0_), channel_id=1, source_target_pairs={{0,2},{1,3},{2,0},{3,1},{4,6},{5,7},{6,4},{7,5},{8,10},{9,11},{10,... | collective-permute-start | bytes 344072 | tf_op jit(solution)/shard_map/ppermute | solution.py:175
  55.2 10.4 %collective-permute-start.15 = (bf16[224,512]{1,0:T(8,128)(2,1)S(1)}, bf16[224,512]{1,0:T(8,128)(2,1)S(1)}, u32[]{:S(2)}, u32[]{:S(2)}) collective-permute-start(bf16[224,512]{1,0:T(8,128)(2,1)S(1)} %get-tuple-element.51.refs_5_.mine), channel_id=1, source_target_pairs={{0,8},{4,12},{8,0},{12,4},{16,24},{20,28},{24,16},{28,20},{1,9},{5... | collective-permute-start | bytes 688136 | tf_op jit(solution)/shard_map/ppermute | solution.py:175
  56.7 10.6 %collective-permute-start.18 = (bf16[224,512]{1,0:T(8,128)(2,1)S(1)}, bf16[224,512]{1,0:T(8,128)(2,1)S(1)}, u32[]{:S(2)}, u32[]{:S(2)}) collective-permute-start(bf16[224,512]{1,0:T(8,128)(2,1)S(1)} %get-tuple-element.54.mine), channel_id=1, source_target_pairs={{0,16},{4,20},{8,24},{12,28},{16,0},{20,4},{24,8},{28,12},{1,17},{... | collective-permute-start | bytes 688136 | tf_op jit(solution)/shard_map/ppermute | solution.py:175
  65.0 4.0 %collective-permute-start.22 = (bf16[2,112,512]{2,1,0:T(8,128)(2,1)S(1)}, bf16[2,112,512]{2,1,0:T(8,128)(2,1)S(1)}, u32[]{:S(2)}, u32[]{:S(2)}) collective-permute-start(bf16[2,112,512]{2,1,0:T(8,128)(2,1)S(1)} %get-tuple-element.53.refs_1_.refs_0_), channel_id=1, source_target_pairs={{0,4},{4,0},{8,12},{12,8},{16,20},{20,16},{24,28},{28,24},{1,5},{5... | collective-permute-start | bytes 688136 | tf_op jit(solution)/shard_map/ppermute | solution.py:175
  65.1 3.9 %collective-permute-start.23 = (bf16[2,112,512]{2,1,0:T(8,128)(2,1)S(1)}, bf16[2,112,512]{2,1,0:T(8,128)(2,1)S(1)}, u32[]{:S(2)}, u32[]{:S(2)}) collective-permute-start(bf16[2,112,512]{2,1,0:T(8,128)(2,1)S(1)} %get-tuple-element.56.refs_1_), channel_id=1, source_target_pairs={{0,4},{4,0},{8,12},{12,8},{16,20},{20,16},{24,28},{28,24},{1,5},{5... | collective-permute-start | bytes 688136 | tf_op jit(solution)/shard_map/ppermute | solution.py:175
  65.6 9.1 %collective-permute-start.19 = (bf16[224,512]{1,0:T(8,128)(2,1)S(1)}, bf16[224,512]{1,0:T(8,128)(2,1)S(1)}, u32[]{:S(2)}, u32[]{:S(2)}) collective-permute-start(bf16[224,512]{1,0:T(8,128)(2,1)S(1)} %add.32.refs_1_.refs_0_), channel_id=1, source_target_pairs={{0,16},{4,20},{8,24},{12,28},{16,0},{20,4},{24,8},{28,12},{1,17},{... | collective-permute-start | bytes 688136 | tf_op jit(solution)/shard_map/ppermute | solution.py:175
  67.4 7.4 %collective-permute-start.20 = (bf16[224,512]{1,0:T(8,128)(2,1)S(1)}, bf16[224,512]{1,0:T(8,128)(2,1)S(1)}, u32[]{:S(2)}, u32[]{:S(2)}) collective-permute-start(bf16[224,512]{1,0:T(8,128)(2,1)S(1)} %add.33.refs_5_.refs_1_), channel_id=1, source_target_pairs={{0,8},{4,12},{8,0},{12,4},{16,24},{20,28},{24,16},{28,20},{1,9},{5... | collective-permute-start | bytes 688136 | tf_op jit(solution)/shard_map/ppermute | solution.py:175
  73.1 2.5 %collective-permute-start.27 = (bf16[224,512]{1,0:T(8,128)(2,1)S(1)}, bf16[224,512]{1,0:T(8,128)(2,1)S(1)}, u32[]{:S(2)}, u32[]{:S(2)}) collective-permute-start(bf16[224,512]{1,0:T(8,128)(2,1)S(1)} %get-tuple-element.57.refs_7_), channel_id=1, source_target_pairs={{0,4},{4,0},{8,12},{12,8},{16,20},{20,16},{24,28},{28,24},{1,5},{5... | collective-permute-start | bytes 688136 | tf_op jit(solution)/shard_map/ppermute | solution.py:175
  73.2 2.5 %collective-permute-start.28 = (bf16[224,512]{1,0:T(8,128)(2,1)S(1)}, bf16[224,512]{1,0:T(8,128)(2,1)S(1)}, u32[]{:S(2)}, u32[]{:S(2)}) collective-permute-start(bf16[224,512]{1,0:T(8,128)(2,1)S(1)} %get-tuple-element.61), channel_id=1, source_target_pairs={{0,4},{4,0},{8,12},{12,8},{16,20},{20,16},{24,28},{28,24},{1,5},{5... | collective-permute-start | bytes 688136 | tf_op jit(solution)/shard_map/ppermute | solution.py:175
  75.7 9.9 %collective-permute-start.30 = (bf16[224,512]{1,0:T(8,128)(2,1)S(1)}, bf16[224,512]{1,0:T(8,128)(2,1)S(1)}, u32[]{:S(2)}, u32[]{:S(2)}) collective-permute-start(bf16[224,512]{1,0:T(8,128)(2,1)S(1)} %get-tuple-element.63.mine.refs_1_), channel_id=1, source_target_pairs={{0,8},{4,12},{8,0},{12,4},{16,24},{20,28},{24,16},{28,20},{1,9},{5... | collective-permute-start | bytes 688136 | tf_op jit(solution)/shard_map/ppermute | solution.py:175
  77.3 8.4 %collective-permute-start.29 = (bf16[224,512]{1,0:T(8,128)(2,1)S(1)}, bf16[224,512]{1,0:T(8,128)(2,1)S(1)}, u32[]{:S(2)}, u32[]{:S(2)}) collective-permute-start(bf16[224,512]{1,0:T(8,128)(2,1)S(1)} %get-tuple-element.62.mine), channel_id=1, source_target_pairs={{0,16},{4,20},{8,24},{12,28},{16,0},{20,4},{24,8},{28,12},{1,17},{... | collective-permute-start | bytes 688136 | tf_op jit(solution)/shard_map/ppermute | solution.py:175
  78.1 7.5 %collective-permute-start.26 = (bf16[112,512]{1,0:T(8,128)(2,1)S(1)}, bf16[112,512]{1,0:T(8,128)(2,1)S(1)}, u32[]{:S(2)}, u32[]{:S(2)}) collective-permute-start(bf16[112,512]{1,0:T(8,128)(2,1)S(1)} %merge.5.refs_3_), channel_id=1, source_target_pairs={{0,2},{1,3},{2,0},{3,1},{4,6},{5,7},{6,4},{7,5},{8,10},{9,11},{10,... | collective-permute-start | bytes 344072 | tf_op jit(solution)/shard_map/ppermute | solution.py:175
  79.4 7.6 %collective-permute-start.24 = (bf16[2,112,512]{2,1,0:T(8,128)(2,1)S(1)}, bf16[2,112,512]{2,1,0:T(8,128)(2,1)S(1)}, u32[]{:S(2)}, u32[]{:S(2)}) collective-permute-start(bf16[2,112,512]{2,1,0:T(8,128)(2,1)S(1)} %get-tuple-element.58.refs_2_.refs_0_), channel_id=1, source_target_pairs={{0,4},{4,0},{8,12},{12,8},{16,20},{20,16},{24,28},{28,24},{1,5},{5... | collective-permute-start | bytes 688136 | tf_op jit(solution)/shard_map/ppermute | solution.py:175
  79.4 7.6 %collective-permute-start.25 = (bf16[2,112,512]{2,1,0:T(8,128)(2,1)S(1)}, bf16[2,112,512]{2,1,0:T(8,128)(2,1)S(1)}, u32[]{:S(2)}, u32[]{:S(2)}) collective-permute-start(bf16[2,112,512]{2,1,0:T(8,128)(2,1)S(1)} %get-tuple-element.59.refs_1_), channel_id=1, source_target_pairs={{0,4},{4,0},{8,12},{12,8},{16,20},{20,16},{24,28},{28,24},{1,5},{5... | collective-permute-start | bytes 688136 | tf_op jit(solution)/shard_map/ppermute | solution.py:175
  85.8 7.4 %collective-permute-start.33 = (bf16[224,512]{1,0:T(8,128)(2,1)S(1)}, bf16[224,512]{1,0:T(8,128)(2,1)S(1)}, u32[]{:S(2)}, u32[]{:S(2)}) collective-permute-start(bf16[224,512]{1,0:T(8,128)(2,1)S(1)} %add.36.refs_7_.refs_1_), channel_id=1, source_target_pairs={{0,8},{4,12},{8,0},{12,4},{16,24},{20,28},{24,16},{28,20},{1,9},{5... | collective-permute-start | bytes 688136 | tf_op jit(solution)/shard_map/ppermute | solution.py:175
  86.4 7.1 %collective-permute-start.32 = (bf16[224,512]{1,0:T(8,128)(2,1)S(1)}, bf16[224,512]{1,0:T(8,128)(2,1)S(1)}, u32[]{:S(2)}, u32[]{:S(2)}) collective-permute-start(bf16[224,512]{1,0:T(8,128)(2,1)S(1)} %add.35.refs_1_.refs_0_), channel_id=1, source_target_pairs={{0,16},{4,20},{8,24},{12,28},{16,0},{20,4},{24,8},{28,12},{1,17},{... | collective-permute-start | bytes 688136 | tf_op jit(solution)/shard_map/ppermute | solution.py:175
  88.3 4.9 %collective-permute-start.31 = (bf16[112,512]{1,0:T(8,128)(2,1)S(1)}, bf16[112,512]{1,0:T(8,128)(2,1)S(1)}, u32[]{:S(2)}, u32[]{:S(2)}) collective-permute-start(bf16[112,512]{1,0:T(8,128)(2,1)S(1)} %get-tuple-element.65.refs_7_), channel_id=1, source_target_pairs={{0,1},{1,0},{2,3},{3,2},{4,5},{5,4},{6,7},{7,6},{8,9},{9,8},{10,11... | collective-permute-start | bytes 344072 | tf_op jit(solution)/shard_map/ppermute | solution.py:175
  94.4 1.6 %collective-permute-start.34 = (bf16[2,112,512]{2,1,0:T(8,128)(2,1)S(1)}, bf16[2,112,512]{2,1,0:T(8,128)(2,1)S(1)}, u32[]{:S(2)}, u32[]{:S(2)}) collective-permute-start(bf16[2,112,512]{2,1,0:T(8,128)(2,1)S(1)} %get-tuple-element.67.refs_0_.refs_3_), channel_id=1, source_target_pairs={{0,4},{4,0},{8,12},{12,8},{16,20},{20,16},{24,28},{28,24},{1,5},{5... | collective-permute-start | bytes 688136 | tf_op jit(solution)/shard_map/ppermute | solution.py:175
  94.4 1.8 %collective-permute-start.35 = (bf16[2,112,512]{2,1,0:T(8,128)(2,1)S(1)}, bf16[2,112,512]{2,1,0:T(8,128)(2,1)S(1)}, u32[]{:S(2)}, u32[]{:S(2)}) collective-permute-start(bf16[2,112,512]{2,1,0:T(8,128)(2,1)S(1)} %get-tuple-element.68.refs_1_), channel_id=1, source_target_pairs={{0,4},{4,0},{8,12},{12,8},{16,20},{20,16},{24,28},{28,24},{1,5},{5... | collective-permute-start | bytes 688136 | tf_op jit(solution)/shard_map/ppermute | solution.py:175
  95.9 8.5 %copy-start.3 = (bf16[512,512]{1,0:T(8,128)(2,1)S(1)}, bf16[512,512]{1,0:T(8,128)(2,1)}, u32[]{:S(2)}) copy-start(bf16[512,512]{1,0:T(8,128)(2,1)} %refs_2_.5) | copy-start | bytes 1572868
  97.3 7.0 %collective-permute-start.36 = (bf16[112,512]{1,0:T(8,128)(2,1)S(1)}, bf16[112,512]{1,0:T(8,128)(2,1)S(1)}, u32[]{:S(2)}, u32[]{:S(2)}) collective-permute-start(bf16[112,512]{1,0:T(8,128)(2,1)S(1)} %get-tuple-element.69.refs_1_), channel_id=1, source_target_pairs={{0,1},{1,0},{2,3},{3,2},{4,5},{5,4},{6,7},{7,6},{8,9},{9,8},{10,11... | collective-permute-start | bytes 344072 | tf_op jit(solution)/shard_map/ppermute | solution.py:175
  97.4 8.7 %collective-permute-start.37 = (bf16[112,512]{1,0:T(8,128)(2,1)S(1)}, bf16[112,512]{1,0:T(8,128)(2,1)S(1)}, u32[]{:S(2)}, u32[]{:S(2)}) collective-permute-start(bf16[112,512]{1,0:T(8,128)(2,1)S(1)} %add.37.refs_1_.refs_0_), channel_id=1, source_target_pairs={{0,2},{1,3},{2,0},{3,1},{4,6},{5,7},{6,4},{7,5},{8,10},{9,11},{10,... | collective-permute-start | bytes 344072 | tf_op jit(solution)/shard_map/ppermute | solution.py:175
  104.3 7.0 %collective-permute-start.38 = (bf16[112,512]{1,0:T(8,128)(2,1)S(1)}, bf16[112,512]{1,0:T(8,128)(2,1)S(1)}, u32[]{:S(2)}, u32[]{:S(2)}) collective-permute-start(bf16[112,512]{1,0:T(8,128)(2,1)S(1)} %add.38.refs_1_.refs_3_), channel_id=1, source_target_pairs={{0,2},{1,3},{2,0},{3,1},{4,6},{5,7},{6,4},{7,5},{8,10},{9,11},{10,... | collective-permute-start | bytes 344072 | tf_op jit(solution)/shard_map/ppermute | solution.py:175

commit v5 on v4

--- a/solution.py
+++ b/solution.py
@@ -54,8 +54,7 @@
 
 
 def _vision_kernel(parts, seen, *refs):
-    tokens, scale, info = refs[2 * parts], refs[2 * parts + 1], refs[2 * parts + 2]
-    offset = info[0] * tokens.shape[1]
+    tokens, scale = refs[2 * parts], refs[2 * parts + 1]
     outs, spread = refs[-1 - seen : -1], refs[-1]
     each = 4 // seen
     first = 0
@@ -63,9 +62,8 @@
         rows = pl.ds(first, mine.shape[0])
         for j in range(spread.shape[0]):
             lanes = pl.ds(j * 128, 128)
-            scales = scale[:, pl.ds(pl.multiple_of(offset + j * 128, 128), 128)].astype(F32)
             total = mine[:, lanes].astype(F32) + came[:, lanes].astype(F32)
-            vision = tokens[rows, lanes].astype(F32) + scales * total
+            vision = tokens[rows, lanes].astype(F32) + scale[:, lanes] * total
             spread[j, rows, :] = vision.astype(BF).astype(F32)
         first += mine.shape[0]
     for j in range(spread.shape[0]):
@@ -74,8 +72,8 @@
             out[k % each, :, pl.ds(j * 128, 128)] = spread[j, pl.ds(k, out.shape[1], stride=4), :].astype(BF)
 
 
-def _residual_kernel(half, pieces, info, tokens, *refs):
-    sems, outs = refs[-1], refs[-1 - len(pieces) : -1]
+def _residual_kernel(half, pieces, info, tokens, scale, *refs):
+    sems, outs = refs[-1], refs[-2 - len(pieces) : -2]
     lanes = pl.ds(pl.multiple_of(info[0] * half, half), half)
     patches = tokens.shape[0] // 4
     copies = []
@@ -83,6 +81,7 @@
         rows = pl.ds(pl.multiple_of(info[3 + block] * patches + first, 32), count)
         copies.append(pltpu.make_async_copy(tokens.at[rows, lanes], outs[i], sems.at[i]))
         copies[-1].start()
+    refs[-2][...] = scale[:, lanes].astype(F32)
     for copy in copies:
         copy.wait()
 
@@ -208,18 +207,18 @@
             return held
 
         def residuals(pieces):
-            copies = pl.pallas_call(
+            *copies, own_scale = pl.pallas_call(
                 functools.partial(_residual_kernel, half, pieces),
-                out_shape=tuple(_near((count, half), BF) for _, _, count in pieces),
-                in_specs=[SMEM, HBM] + [ANY] * len(after),
-                out_specs=(VMEM,) * len(pieces),
+                out_shape=tuple(_near((count, half), BF) for _, _, count in pieces) + (_near((1, half), F32),),
+                in_specs=[SMEM, HBM, VMEM] + [ANY] * len(after),
+                out_specs=(VMEM,) * (len(pieces) + 1),
                 scratch_shapes=[pltpu.SemaphoreType.DMA((len(pieces),))],
                 cost_estimate=LITTLE,
                 compiler_params=pltpu.CompilerParams(vmem_limit_bytes=ROOM),
                 name="residuals",
-            )(info, pltpu.with_memory_space_constraint(tokens, pltpu.HBM), *after)
+            )(info, pltpu.with_memory_space_constraint(tokens, pltpu.HBM), scale, *after)
             after[:] = [copies[0]]
-            return copies
+            return copies, own_scale
 
         def relay(block, first, count):
             same = pl.pallas_call(
@@ -265,18 +264,18 @@
             after[:] = [give[0]]
             return give if rows else give[0]
 
-        def see(mine_parts, came_parts, residual, parts=2):
+        def see(mine_parts, came_parts, residual, own_scale, parts=2):
             count = residual.shape[0]
             out = pl.pallas_call(
                 functools.partial(_vision_kernel, len(mine_parts), parts),
                 out_shape=(_near((4 // parts, count // 4, half), BF),) * parts,
-                in_specs=[VMEM] * (2 * len(mine_parts) + 2) + [SMEM] + [ANY] * len(after),
+                in_specs=[VMEM] * (2 * len(mine_parts) + 2) + [ANY] * len(after),
                 out_specs=(VMEM,) * parts,
                 scratch_shapes=[pltpu.VMEM((half // 128, count, 128), F32)],
                 cost_estimate=LITTLE,
                 compiler_params=pltpu.CompilerParams(vmem_limit_bytes=ROOM),
                 name="vision",
-            )(*mine_parts, *came_parts, stay(residual), scale, info, *after)
+            )(*mine_parts, *came_parts, stay(residual), stay(own_scale), *after)
             after[:] = [out[0]]
             return tuple(out)
 
@@ -358,7 +357,8 @@
                     total = add(total, came)
                     came = swap(total, "row", bit)
                 residual = lax.dynamic_slice(tokens, (owner * patches, mine * half), (patches, half))
-                own = see([total], [came], residual)
+                own_scale = lax.dynamic_slice(scale, (0, mine * half), (1, half)).astype(F32)
+                own = see([total], [came], residual, own_scale)
                 part = merge(own, tuple(swap(v, "row", 1) for v in own), held).astype(F32)
                 parts = lax.dynamic_update_slice(parts, part, (owner * merged_rows, 0))
             return place([lax.psum(parts, "col").astype(BF)], positions[None, :])
@@ -431,7 +431,7 @@
             v["back", i].append((x if j else y)(v["turn", i][j]))
 
         def look(i):
-            seen = see(v["turn", i], v["back", i], v["residual"][i], SEEN[i])
+            seen = see(v["turn", i], v["back", i], v["residual"][i], v["scale"], SEEN[i])
             v["seen", i], v["other", i] = seen, core(seen)
 
         def project(i):
@@ -454,7 +454,7 @@
             if name == "hold":
                 v["held"] = hold()
             elif name == "residual":
-                v["residual"] = residuals(pieces)
+                v["residual"], v["scale"] = residuals(pieces)
             elif name == "early":
                 v["base"] = place_early([v["away", i] for i in range(2, last)], 2 * merged_rows, where_to)
 

time: 113 us -> 112 us (level)
  waiting for transfers between devices: 52.2 us -> 54.5 us
  Pallas kernels: 23.5 us -> 21.3 us
    pallas_call x4, Pallas kernels: 3.72 us -> 1.55 us  [see(): pl.pallas_call(functools.partial(_vision_kernel, len(mine_parts), parts),...]
    ppermute x35, waiting for transfers between devices: 44.2 us -> 45.5 us  [swap(): return lax.ppermute(x, axis, [(i, i ^ bit) for i in range(size)])]
  transfers between devices with their start and end apart: 39 -> 39, of which waited for: 21 -> 24; matrix products, arithmetic and copies ran while one was open for 2% -> 2% of each run, Pallas kernels for 18% -> 17%
where the time goes in v5:
time: 112 us
  waiting for transfers between devices  54.5 us (49%)
  starting transfers between devices  31.4 us (28%)
  Pallas kernels  21.3 us (19%)
  local copies, waits for them, and re-layouts  3.55 us (3%)
    ppermute x35, waiting for transfers between devices, swap(): return lax.ppermute(x, axis, [(i, i ^ bit) for i in range(size)])  45.5 us
    ppermute x35, starting transfers between devices, swap(): return lax.ppermute(x, axis, [(i, i ^ bit) for i in range(size)])  27.4 us
    ppermute x1, waiting for transfers between devices, per_device(): v['hop_c'] = lax.ppermute(v['hop_b'], 'col', outward)  7.32 us
    pallas_call x4, Pallas kernels, down(): pl.pallas_call(functools.partial(_down_kernel, half, len(blocks), (parts,...  6.65 us
    pallas_call x4, Pallas kernels, merge(): pl.pallas_call(functools.partial(_merge_kernel, half, len(own), late, fir...  4.89 us
    unnamed x8, local copies, waits for them, and re-layouts  2.78 us
  transfers between devices with their start and end apart: 39, of which 24 were waited for; matrix products, arithmetic and copies ran while one was open for 2% of the time, Pallas kernels for 17%

profile of v5, /device:TPU:0, one launch (start us, length us, event | category | flops | bytes accessed | tf_op | source)
XLA Modules:
  0.0 112.0 jit_solution(5739567198101895497)
XLA Ops:
  0.0 3.0 %collective-permute-start.2 = (bf16[448,1024]{1,0:T(8,128)(2,1)}, bf16[448,1024]{1,0:T(8,128)(2,1)S(1)}, u32[]{:S(2)}, u32[]{:S(2)}) collective-permute-start(bf16[448,1024]{1,0:T(8,128)(2,1)} %refs_0_.1), channel_id=1, source_target_pairs={{0,1},{1,0},{2,3},{3,2},{4,5},{5,4},{6,7},{7,6},{8,9},{9,8},{10,11... | collective-permute-start | bytes 2752520 | tf_op jit(solution)/shard_map/ppermute | solution.py:174
  3.0 0.7 collective-permute-start
  3.8 0.7 broadcast_in_dim.7.refs_2_.scale
  4.5 0.9 broadcast_select_fusion.3
  5.5 1.6 %copy-done = bf16[1024,1024]{1,0:T(8,128)(2,1)S(1)} copy-done((bf16[1024,1024]{1,0:T(8,128)(2,1)S(1)}, bf16[1024,1024]{1,0:T(8,128)(2,1)}, u32[]{:S(2)}) %copy-start) | copy-done | bytes 2097176
  7.1 1.2 %copy-done.2 = bf16[448,1024]{1,0:T(8,128)(2,1)S(1)} copy-done((bf16[448,1024]{1,0:T(8,128)(2,1)S(1)}, bf16[448,1024]{1,0:T(8,128)(2,1)}, u32[]{:S(2)}) %copy-start.2) | copy-done | bytes 917528
  8.3 1.7 %down.4 = (bf16[224,512]{1,0:T(8,128)(2,1)S(1)}, bf16[224,512]{1,0:T(8,128)(2,1)S(1)}, f32[448,512]{1,0:T(8,128)S(1)}) custom-call(s32[7]{0:T(128)S(1)} %stack.35.info, bf16[448,1024]{1,0:T(8,128)(2,1)S(1)} %copy-done.2, bf16[1024,1024]{1,0:T(8,128)(2,1)S(1)} %copy-done, bf16[1,1024]{1,0:T(2,128)(2,1)S(1)} %broadcast_in_dim.7.refs_2_.scale, s32[1,448]{1,0:T(1,128)S(1)} %bitcast.8), custom_call_target="tpu_custom_call" | custom-call | flops 1 | bytes 1 | tf_op jit(solution)/shard_map/down/pallas_call | solution.py:240
  10.5 1.0 collective-permute-done.4.refs_0_
  11.9 1.6 %collective-permute-start.6 = (bf16[448,512]{1,0:T(8,128)(2,1)S(1)}, bf16[448,512]{1,0:T(8,128)(2,1)S(1)}, u32[]{:S(2)}, u32[]{:S(2)}) collective-permute-start(bf16[448,512]{1,0:T(8,128)(2,1)S(1)} %add.27.mine.refs_1_), channel_id=1, source_target_pairs={{0,8},{4,12},{8,0},{12,4},{16,24},{20,28},{24,16},{28,20},{1,9},{5... | collective-permute-start | bytes 1376264 | tf_op jit(solution)/shard_map/ppermute | solution.py:174
  13.5 10.1 %collective-permute-done.2.refs_0_ = bf16[448,1024]{1,0:T(8,128)(2,1)S(1)} collective-permute-done((bf16[448,1024]{1,0:T(8,128)(2,1)}, bf16[448,1024]{1,0:T(8,128)(2,1)S(1)}, u32[]{:S(2)}, u32[]{:S(2)}) %collective-permute-start.2) | collective-permute-done | bytes 917536 | tf_op jit(solution)/shard_map/ppermute | solution.py:174
  23.6 0.7 collective-permute-start.3
  24.3 1.3 %collective-permute-start.1 = (bf16[448,1024]{1,0:T(8,128)(2,1)S(1)}, bf16[448,1024]{1,0:T(8,128)(2,1)S(1)}, u32[]{:S(2)}, u32[]{:S(2)}) collective-permute-start(bf16[448,1024]{1,0:T(8,128)(2,1)S(1)} %collective-permute-done.refs_3_.refs_0_), channel_id=1, source_target_pairs={{1,0},{2,3},{5,4},{6,7},{9,8},{10,11},{13,12},{14,15},{17,16},{18,... | collective-permute-start | bytes 2752520 | tf_op jit(solution)/shard_map/ppermute | solution.py:399
  25.7 1.8 %collective-permute-start.7 = (bf16[448,512]{1,0:T(8,128)(2,1)S(1)}, bf16[448,512]{1,0:T(8,128)(2,1)S(1)}, u32[]{:S(2)}, u32[]{:S(2)}) collective-permute-start(bf16[448,512]{1,0:T(8,128)(2,1)S(1)} %add.28.refs_2_.refs_0_), channel_id=1, source_target_pairs={{0,16},{4,20},{8,24},{12,28},{16,0},{20,4},{24,8},{28,12},{1,17},{... | collective-permute-start | bytes 1376264 | tf_op jit(solution)/shard_map/ppermute | solution.py:174
  27.5 1.7 %down.5 = (bf16[224,512]{1,0:T(8,128)(2,1)S(1)}, bf16[224,512]{1,0:T(8,128)(2,1)S(1)}, f32[448,512]{1,0:T(8,128)S(1)}) custom-call(s32[7]{0:T(128)S(1)} %stack.35.info, bf16[448,1024]{1,0:T(8,128)(2,1)S(1)} %collective-permute-done.2.refs_0_, bf16[1024,1024]{1,0:T(8,128)(2,1)S(1)} %copy-done.1, bf16[448,512]{1,0:T(8,128)(2,1)S(1)} %add.28.refs_2_.refs_0_, ...), custom_call_target="tpu_custom_call" | custom-call | flops 1 | bytes 1 | tf_op jit(solution)/shard_map/down/pallas_call | solution.py:240
  29.7 1.0 collective-permute-done.8.refs_0_
  31.1 1.6 %collective-permute-start.14 = (bf16[448,512]{1,0:T(8,128)(2,1)S(1)}, bf16[448,512]{1,0:T(8,128)(2,1)S(1)}, u32[]{:S(2)}, u32[]{:S(2)}) collective-permute-start(bf16[448,512]{1,0:T(8,128)(2,1)S(1)} %add.29.refs_0_.mine), channel_id=1, source_target_pairs={{0,8},{4,12},{8,0},{12,4},{16,24},{20,28},{24,16},{28,20},{1,9},{5... | collective-permute-start | bytes 1376264 | tf_op jit(solution)/shard_map/ppermute | solution.py:174
  32.7 2.0 %residuals.1 = (bf16[448,512]{1,0:T(8,128)(2,1)S(1)}, bf16[448,512]{1,0:T(8,128)(2,1)S(1)}, bf16[448,512]{1,0:T(8,128)(2,1)S(1)}, bf16[448,512]{1,0:T(8,128)(2,1)S(1)}, f32[1,512]{1,0:T(1,128)S(1)}) custom-call(s32[7]{0:T(128)S(1)} %stack.35.info, bf16[1792,1024]{1,0:T(8,128)(2,1)} %tokens.1, bf16[1,1024]{1,0:T(2,128)(2,1)S(1)} %broadcast_in_dim.7.refs_2_.scale, ...), custom_call_target="tpu_custom_call" | custom-call | flops 1 | bytes 1 | tf_op jit(solution)/shard_map/residuals/pallas_call | solution.py:210
  34.7 2.2 %hold.1.refs_4_.refs_2_ = bf16[4,1024,512]{2,1,0:T(8,128)(2,1)S(1)} custom-call(bf16[4,1024,512]{2,1,0:T(8,128)(2,1)} %weight.1, bf16[448,512]{1,0:T(8,128)(2,1)S(1)} %get-tuple-element.46.refs_0_.refs_2_), custom_call_target="tpu_custom_call" | custom-call | flops 1 | bytes 1 | tf_op jit(solution)/shard_map/hold/pallas_call | solution.py:196
  36.9 0.6 collective-permute-done.7.refs_1_
  38.5 1.0 collective-permute-done.10.refs_2_
  39.8 1.3 %merge.4.refs_0_ = bf16[112,512]{1,0:T(8,128)(2,1)S(1)} custom-call(s32[7]{0:T(128)S(1)} %stack.35.info, bf16[2,112,512]{2,1,0:T(8,128)(2,1)S(1)} %get-tuple-element.48.refs_0_.refs_5_, bf16[2,112,512]{2,1,0:T(8,128)(2,1)S(1)} %get-tuple-element.49.refs_1_, bf16[2,112,512]{2,1,0:T(8,128)(2,1)S(1)} %collective-permute-done.10.refs_2_, ...), custom_call_target="tpu_custom_call" | custom-call | flops 1 | bytes 1 | tf_op jit(solution)/shard_map/merge/pallas_call | solution.py:301
  41.2 1.3 %collective-permute-start.21 = (bf16[448,1024]{1,0:T(8,128)(2,1)S(1)}, bf16[448,1024]{1,0:T(8,128)(2,1)S(1)}, u32[]{:S(2)}, u32[]{:S(2)}) collective-permute-start(bf16[448,1024]{1,0:T(8,128)(2,1)S(1)} %relay.1.refs_3_.refs_0_), channel_id=1, source_target_pairs={{1,0},{2,3},{5,4},{6,7},{9,8},{10,11},{13,12},{14,15},{17,16},{18,... | collective-permute-start | bytes 2752520 | tf_op jit(solution)/shard_map/ppermute | solution.py:404
  42.5 7.3 %collective-permute-done.1.refs_1_ = bf16[448,1024]{1,0:T(8,128)(2,1)S(1)} collective-permute-done((bf16[448,1024]{1,0:T(8,128)(2,1)S(1)}, bf16[448,1024]{1,0:T(8,128)(2,1)S(1)}, u32[]{:S(2)}, u32[]{:S(2)}) %collective-permute-start.1) | collective-permute-done | bytes 917536 | tf_op jit(solution)/shard_map/ppermute | solution.py:399
  49.8 1.7 %down.6 = (bf16[224,512]{1,0:T(8,128)(2,1)S(1)}, bf16[224,512]{1,0:T(8,128)(2,1)S(1)}, f32[448,512]{1,0:T(8,128)S(1)}) custom-call(s32[7]{0:T(128)S(1)} %stack.35.info, bf16[448,1024]{1,0:T(8,128)(2,1)S(1)} %collective-permute-done.refs_3_.refs_0_, bf16[448,1024]{1,0:T(8,128)(2,1)S(1)} %collective-permute-done.1.refs_1_, bf16[1024,1024]{1,0:T(8,128)(2,1)S(1)} %copy-done.1, ...), custom_call_target="tpu_custom_call" | custom-call | flops 1 | bytes 1 | tf_op jit(solution)/shard_map/down/pallas_call | solution.py:240
  51.6 1.6 %collective-permute-start.16 = (bf16[448,512]{1,0:T(8,128)(2,1)S(1)}, bf16[448,512]{1,0:T(8,128)(2,1)S(1)}, u32[]{:S(2)}, u32[]{:S(2)}) collective-permute-start(bf16[448,512]{1,0:T(8,128)(2,1)S(1)} %add.30.refs_2_.refs_0_), channel_id=1, source_target_pairs={{0,16},{4,20},{8,24},{12,28},{16,0},{20,4},{24,8},{28,12},{1,17},{... | collective-permute-start | bytes 1376264 | tf_op jit(solution)/shard_map/ppermute | solution.py:174
  53.7 1.0 collective-permute-start.17
  55.1 1.6 %collective-permute-start.15 = (bf16[224,512]{1,0:T(8,128)(2,1)S(1)}, bf16[224,512]{1,0:T(8,128)(2,1)S(1)}, u32[]{:S(2)}, u32[]{:S(2)}) collective-permute-start(bf16[224,512]{1,0:T(8,128)(2,1)S(1)} %get-tuple-element.53.refs_4_.mine), channel_id=1, source_target_pairs={{0,8},{4,12},{8,0},{12,4},{16,24},{20,28},{24,16},{28,20},{1,9},{5... | collective-permute-start | bytes 688136 | tf_op jit(solution)/shard_map/ppermute | solution.py:174
  57.2 4.5 %collective-permute-done.17.refs_5_.refs_2_ = bf16[112,512]{1,0:T(8,128)(2,1)S(1)} collective-permute-done((bf16[112,512]{1,0:T(8,128)(2,1)S(1)}, bf16[112,512]{1,0:T(8,128)(2,1)S(1)}, u32[]{:S(2)}, u32[]{:S(2)}) %collective-permute-start.17) | collective-permute-done | bytes 114720 | tf_op jit(solution)/shard_map/ppermute | solution.py:174
  61.7 2.2 %collective-permute-done.16.refs_1_ = bf16[448,512]{1,0:T(8,128)(2,1)S(1)} collective-permute-done((bf16[448,512]{1,0:T(8,128)(2,1)S(1)}, bf16[448,512]{1,0:T(8,128)(2,1)S(1)}, u32[]{:S(2)}, u32[]{:S(2)}) %collective-permute-start.16) | collective-permute-done | bytes 458784 | tf_op jit(solution)/shard_map/ppermute | solution.py:174
  65.1 1.7 %collective-permute-start.19 = (bf16[224,512]{1,0:T(8,128)(2,1)S(1)}, bf16[224,512]{1,0:T(8,128)(2,1)S(1)}, u32[]{:S(2)}, u32[]{:S(2)}) collective-permute-start(bf16[224,512]{1,0:T(8,128)(2,1)S(1)} %add.32.refs_1_.refs_0_), channel_id=1, source_target_pairs={{0,16},{4,20},{8,24},{12,28},{16,0},{20,4},{24,8},{28,12},{1,17},{... | collective-permute-start | bytes 688136 | tf_op jit(solution)/shard_map/ppermute | solution.py:174
  66.8 1.6 %collective-permute-start.20 = (bf16[224,512]{1,0:T(8,128)(2,1)S(1)}, bf16[224,512]{1,0:T(8,128)(2,1)S(1)}, u32[]{:S(2)}, u32[]{:S(2)}) collective-permute-start(bf16[224,512]{1,0:T(8,128)(2,1)S(1)} %add.33.refs_5_.refs_1_), channel_id=1, source_target_pairs={{0,8},{4,12},{8,0},{12,4},{16,24},{20,28},{24,16},{28,20},{1,9},{5... | collective-permute-start | bytes 688136 | tf_op jit(solution)/shard_map/ppermute | solution.py:174
  68.4 1.3 %merge.5.refs_3_ = bf16[112,512]{1,0:T(8,128)(2,1)S(1)} custom-call(s32[7]{0:T(128)S(1)} %stack.35.info, bf16[2,112,512]{2,1,0:T(8,128)(2,1)S(1)} %get-tuple-element.55.refs_1_.refs_0_, bf16[2,112,512]{2,1,0:T(8,128)(2,1)S(1)} %get-tuple-element.58.refs_1_, bf16[2,112,512]{2,1,0:T(8,128)(2,1)S(1)} %collective-permute-done.22.refs_2_, ...), custom_call_target="tpu_custom_call" | custom-call | flops 1 | bytes 1 | tf_op jit(solution)/shard_map/merge/pallas_call | solution.py:301
  69.7 1.7 %collective-permute-done.21.refs_1_ = bf16[448,1024]{1,0:T(8,128)(2,1)S(1)} collective-permute-done((bf16[448,1024]{1,0:T(8,128)(2,1)S(1)}, bf16[448,1024]{1,0:T(8,128)(2,1)S(1)}, u32[]{:S(2)}, u32[]{:S(2)}) %collective-permute-start.21) | collective-permute-done | bytes 917536 | tf_op jit(solution)/shard_map/ppermute | solution.py:404
  71.4 1.7 %down.7 = (bf16[224,512]{1,0:T(8,128)(2,1)S(1)}, bf16[224,512]{1,0:T(8,128)(2,1)S(1)}, f32[448,512]{1,0:T(8,128)S(1)}) custom-call(s32[7]{0:T(128)S(1)} %stack.35.info, bf16[448,1024]{1,0:T(8,128)(2,1)S(1)} %relay.1.refs_3_.refs_0_, bf16[448,1024]{1,0:T(8,128)(2,1)S(1)} %collective-permute-done.21.refs_1_, bf16[1024,1024]{1,0:T(8,128)(2,1)S(1)} %copy-done.1, ...), custom_call_target="tpu_custom_call" | custom-call | flops 1 | bytes 1 | tf_op jit(solution)/shard_map/down/pallas_call | solution.py:240
  75.1 1.6 %collective-permute-start.30 = (bf16[224,512]{1,0:T(8,128)(2,1)S(1)}, bf16[224,512]{1,0:T(8,128)(2,1)S(1)}, u32[]{:S(2)}, u32[]{:S(2)}) collective-permute-start(bf16[224,512]{1,0:T(8,128)(2,1)S(1)} %get-tuple-element.65.mine.refs_1_), channel_id=1, source_target_pairs={{0,8},{4,12},{8,0},{12,4},{16,24},{20,28},{24,16},{28,20},{1,9},{5... | collective-permute-start | bytes 688136 | tf_op jit(solution)/shard_map/ppermute | solution.py:174
  76.6 1.5 %collective-permute-start.29 = (bf16[224,512]{1,0:T(8,128)(2,1)S(1)}, bf16[224,512]{1,0:T(8,128)(2,1)S(1)}, u32[]{:S(2)}, u32[]{:S(2)}) collective-permute-start(bf16[224,512]{1,0:T(8,128)(2,1)S(1)} %get-tuple-element.64.mine), channel_id=1, source_target_pairs={{0,16},{4,20},{8,24},{12,28},{16,0},{20,4},{24,8},{28,12},{1,17},{... | collective-permute-start | bytes 688136 | tf_op jit(solution)/shard_map/ppermute | solution.py:174
  78.8 6.8 %collective-permute-done.26.refs_2_.refs_6_ = bf16[112,512]{1,0:T(8,128)(2,1)S(1)} collective-permute-done((bf16[112,512]{1,0:T(8,128)(2,1)S(1)}, bf16[112,512]{1,0:T(8,128)(2,1)S(1)}, u32[]{:S(2)}, u32[]{:S(2)}) %collective-permute-start.26) | collective-permute-done | bytes 114720 | tf_op jit(solution)/shard_map/ppermute | solution.py:174
  85.8 0.6 collective-permute-start.33
  86.9 1.3 %merge.6 = (bf16[112,512]{1,0:T(8,128)(2,1)S(1)}, f32[112,512]{1,0:T(8,128)S(1)}) custom-call(s32[7]{0:T(128)S(1)} %stack.35.info, bf16[2,112,512]{2,1,0:T(8,128)(2,1)S(1)} %get-tuple-element.60.refs_2_.refs_0_, bf16[2,112,512]{2,1,0:T(8,128)(2,1)S(1)} %get-tuple-element.61.refs_1_, bf16[2,112,512]{2,1,0:T(8,128)(2,1)S(1)} %collective-permute-done.24.refs_2_, ...), custom_call_target="tpu_custom_call" | custom-call | flops 1 | bytes 1 | tf_op jit(solution)/shard_map/merge/pallas_call | solution.py:301
  88.3 4.8 %collective-permute-done.31.refs_7_.refs_0_ = bf16[112,512]{1,0:T(8,128)(2,1)S(1)} collective-permute-done((bf16[112,512]{1,0:T(8,128)(2,1)S(1)}, bf16[112,512]{1,0:T(8,128)(2,1)S(1)}, u32[]{:S(2)}, u32[]{:S(2)}) %collective-permute-start.31) | collective-permute-done | bytes 114720 | tf_op jit(solution)/shard_map/ppermute | solution.py:174
  94.5 1.0 merge_head.1.refs_7_.refs_8_
  95.8 1.0 merge.7
  97.0 2.3 %collective-permute-start.37 = (bf16[112,512]{1,0:T(8,128)(2,1)S(1)}, bf16[112,512]{1,0:T(8,128)(2,1)S(1)}, u32[]{:S(2)}, u32[]{:S(2)}) collective-permute-start(bf16[112,512]{1,0:T(8,128)(2,1)S(1)} %add.37.refs_1_.refs_0_), channel_id=1, source_target_pairs={{0,2},{1,3},{2,0},{3,1},{4,6},{5,7},{6,4},{7,5},{8,10},{9,11},{10,... | collective-permute-start | bytes 344072 | tf_op jit(solution)/shard_map/ppermute | solution.py:174
  99.3 4.3 %collective-permute-done.36.refs_0_ = bf16[112,512]{1,0:T(8,128)(2,1)S(1)} collective-permute-done((bf16[112,512]{1,0:T(8,128)(2,1)S(1)}, bf16[112,512]{1,0:T(8,128)(2,1)S(1)}, u32[]{:S(2)}, u32[]{:S(2)}) %collective-permute-start.36) | collective-permute-done | bytes 114720 | tf_op jit(solution)/shard_map/ppermute | solution.py:174
  103.9 1.0 place_early.1
  104.9 0.8 collective-permute-done.37.refs_0_
  105.7 5.3 %collective-permute-done.38.refs_1_ = bf16[112,512]{1,0:T(8,128)(2,1)S(1)} collective-permute-done((bf16[112,512]{1,0:T(8,128)(2,1)S(1)}, bf16[112,512]{1,0:T(8,128)(2,1)S(1)}, u32[]{:S(2)}, u32[]{:S(2)}) %collective-permute-start.38) | collective-permute-done | bytes 114720 | tf_op jit(solution)/shard_map/ppermute | solution.py:174
  111.0 1.1 place_late.1
  (72 shorter events, 11.8 us)
Async XLA Ops:
  0.0 23.6 %collective-permute-start.2 = (bf16[448,1024]{1,0:T(8,128)(2,1)}, bf16[448,1024]{1,0:T(8,128)(2,1)S(1)}, u32[]{:S(2)}, u32[]{:S(2)}) collective-permute-start(bf16[448,1024]{1,0:T(8,128)(2,1)} %refs_0_.1), channel_id=1, source_target_pairs={{0,1},{1,0},{2,3},{3,2},{4,5},{5,4},{6,7},{7,6},{8,9},{9,8},{10,11... | collective-permute-start | bytes 2752520 | tf_op jit(solution)/shard_map/ppermute | solution.py:174
  3.0 21.3 %collective-permute-start = (bf16[448,1024]{1,0:T(8,128)(2,1)}, bf16[448,1024]{1,0:T(8,128)(2,1)S(1)}, u32[]{:S(2)}, u32[]{:S(2)}) collective-permute-start(bf16[448,1024]{1,0:T(8,128)(2,1)} %refs_0_.1), channel_id=1, source_target_pairs={{1,2},{2,1},{5,6},{6,5},{9,10},{10,9},{13,14},{14,13},{17,18},{18,... | collective-permute-start | bytes 2752520 | tf_op jit(solution)/shard_map/ppermute | solution.py:398
  5.5 1.6 %copy-start = (bf16[1024,1024]{1,0:T(8,128)(2,1)S(1)}, bf16[1024,1024]{1,0:T(8,128)(2,1)}, u32[]{:S(2)}) copy-start(bf16[1024,1024]{1,0:T(8,128)(2,1)} %refs_2_.4) | copy-start | bytes 6291460
  7.1 1.2 %copy-start.2 = (bf16[448,1024]{1,0:T(8,128)(2,1)S(1)}, bf16[448,1024]{1,0:T(8,128)(2,1)}, u32[]{:S(2)}) copy-start(bf16[448,1024]{1,0:T(8,128)(2,1)} %refs_0_.1) | copy-start | bytes 2752516
  8.3 19.2 %copy-start.1 = (bf16[1024,1024]{1,0:T(8,128)(2,1)S(1)}, bf16[1024,1024]{1,0:T(8,128)(2,1)}, u32[]{:S(2)}) copy-start(bf16[1024,1024]{1,0:T(8,128)(2,1)} %refs_2_.4) | copy-start | bytes 6291460
  10.0 1.6 %collective-permute-start.4 = (bf16[224,512]{1,0:T(8,128)(2,1)S(1)}, bf16[224,512]{1,0:T(8,128)(2,1)S(1)}, u32[]{:S(2)}, u32[]{:S(2)}) collective-permute-start(bf16[224,512]{1,0:T(8,128)(2,1)S(1)} %get-tuple-element.41.refs_2_), channel_id=1, source_target_pairs={{0,4},{4,0},{8,12},{12,8},{16,20},{20,16},{24,28},{28,24},{1,5},{5... | collective-permute-start | bytes 688136 | tf_op jit(solution)/shard_map/ppermute | solution.py:174
  10.0 1.8 %collective-permute-start.5 = (bf16[224,512]{1,0:T(8,128)(2,1)S(1)}, bf16[224,512]{1,0:T(8,128)(2,1)S(1)}, u32[]{:S(2)}, u32[]{:S(2)}) collective-permute-start(bf16[224,512]{1,0:T(8,128)(2,1)S(1)} %get-tuple-element.42), channel_id=1, source_target_pairs={{0,4},{4,0},{8,12},{12,8},{16,20},{20,16},{24,28},{28,24},{1,5},{5... | collective-permute-start | bytes 688136 | tf_op jit(solution)/shard_map/ppermute | solution.py:174
  11.9 13.7 %collective-permute-start.6 = (bf16[448,512]{1,0:T(8,128)(2,1)S(1)}, bf16[448,512]{1,0:T(8,128)(2,1)S(1)}, u32[]{:S(2)}, u32[]{:S(2)}) collective-permute-start(bf16[448,512]{1,0:T(8,128)(2,1)S(1)} %add.27.mine.refs_1_), channel_id=1, source_target_pairs={{0,8},{4,12},{8,0},{12,4},{16,24},{20,28},{24,16},{28,20},{1,9},{5... | collective-permute-start | bytes 1376264 | tf_op jit(solution)/shard_map/ppermute | solution.py:174
  23.6 17.6 %collective-permute-start.3 = (bf16[448,1024]{1,0:T(8,128)(2,1)S(1)}, bf16[448,1024]{1,0:T(8,128)(2,1)S(1)}, u32[]{:S(2)}, u32[]{:S(2)}) collective-permute-start(bf16[448,1024]{1,0:T(8,128)(2,1)S(1)} %collective-permute-done.2.refs_0_), channel_id=1, source_target_pairs={{1,2},{2,1},{5,6},{6,5},{9,10},{10,9},{13,14},{14,13},{17,18},{18,... | collective-permute-start | bytes 2752520 | tf_op jit(solution)/shard_map/ppermute | solution.py:400
  24.3 25.5 %collective-permute-start.1 = (bf16[448,1024]{1,0:T(8,128)(2,1)S(1)}, bf16[448,1024]{1,0:T(8,128)(2,1)S(1)}, u32[]{:S(2)}, u32[]{:S(2)}) collective-permute-start(bf16[448,1024]{1,0:T(8,128)(2,1)S(1)} %collective-permute-done.refs_3_.refs_0_), channel_id=1, source_target_pairs={{1,0},{2,3},{5,4},{6,7},{9,8},{10,11},{13,12},{14,15},{17,16},{18,... | collective-permute-start | bytes 2752520 | tf_op jit(solution)/shard_map/ppermute | solution.py:399
  25.7 11.8 %collective-permute-start.7 = (bf16[448,512]{1,0:T(8,128)(2,1)S(1)}, bf16[448,512]{1,0:T(8,128)(2,1)S(1)}, u32[]{:S(2)}, u32[]{:S(2)}) collective-permute-start(bf16[448,512]{1,0:T(8,128)(2,1)S(1)} %add.28.refs_2_.refs_0_), channel_id=1, source_target_pairs={{0,16},{4,20},{8,24},{12,28},{16,0},{20,4},{24,8},{28,12},{1,17},{... | collective-permute-start | bytes 1376264 | tf_op jit(solution)/shard_map/ppermute | solution.py:174
  29.2 1.6 %collective-permute-start.8 = (bf16[224,512]{1,0:T(8,128)(2,1)S(1)}, bf16[224,512]{1,0:T(8,128)(2,1)S(1)}, u32[]{:S(2)}, u32[]{:S(2)}) collective-permute-start(bf16[224,512]{1,0:T(8,128)(2,1)S(1)} %get-tuple-element.44.refs_2_), channel_id=1, source_target_pairs={{0,4},{4,0},{8,12},{12,8},{16,20},{20,16},{24,28},{28,24},{1,5},{5... | collective-permute-start | bytes 688136 | tf_op jit(solution)/shard_map/ppermute | solution.py:174
  29.2 1.8 %collective-permute-start.9 = (bf16[224,512]{1,0:T(8,128)(2,1)S(1)}, bf16[224,512]{1,0:T(8,128)(2,1)S(1)}, u32[]{:S(2)}, u32[]{:S(2)}) collective-permute-start(bf16[224,512]{1,0:T(8,128)(2,1)S(1)} %get-tuple-element.45), channel_id=1, source_target_pairs={{0,4},{4,0},{8,12},{12,8},{16,20},{20,16},{24,28},{28,24},{1,5},{5... | collective-permute-start | bytes 688136 | tf_op jit(solution)/shard_map/ppermute | solution.py:174
  31.1 20.4 %collective-permute-start.14 = (bf16[448,512]{1,0:T(8,128)(2,1)S(1)}, bf16[448,512]{1,0:T(8,128)(2,1)S(1)}, u32[]{:S(2)}, u32[]{:S(2)}) collective-permute-start(bf16[448,512]{1,0:T(8,128)(2,1)S(1)} %add.29.refs_0_.mine), channel_id=1, source_target_pairs={{0,8},{4,12},{8,0},{12,4},{16,24},{20,28},{24,16},{28,20},{1,9},{5... | collective-permute-start | bytes 1376264 | tf_op jit(solution)/shard_map/ppermute | solution.py:174
  38.0 1.6 %collective-permute-start.10 = (bf16[2,112,512]{2,1,0:T(8,128)(2,1)S(1)}, bf16[2,112,512]{2,1,0:T(8,128)(2,1)S(1)}, u32[]{:S(2)}, u32[]{:S(2)}) collective-permute-start(bf16[2,112,512]{2,1,0:T(8,128)(2,1)S(1)} %get-tuple-element.48.refs_0_.refs_5_), channel_id=1, source_target_pairs={{0,4},{4,0},{8,12},{12,8},{16,20},{20,16},{24,28},{28,24},{1,5},{5... | collective-permute-start | bytes 688136 | tf_op jit(solution)/shard_map/ppermute | solution.py:174
  38.0 1.8 %collective-permute-start.11 = (bf16[2,112,512]{2,1,0:T(8,128)(2,1)S(1)}, bf16[2,112,512]{2,1,0:T(8,128)(2,1)S(1)}, u32[]{:S(2)}, u32[]{:S(2)}) collective-permute-start(bf16[2,112,512]{2,1,0:T(8,128)(2,1)S(1)} %get-tuple-element.49.refs_1_), channel_id=1, source_target_pairs={{0,4},{4,0},{8,12},{12,8},{16,20},{20,16},{24,28},{28,24},{1,5},{5... | collective-permute-start | bytes 688136 | tf_op jit(solution)/shard_map/ppermute | solution.py:174
  41.2 30.2 %collective-permute-start.21 = (bf16[448,1024]{1,0:T(8,128)(2,1)S(1)}, bf16[448,1024]{1,0:T(8,128)(2,1)S(1)}, u32[]{:S(2)}, u32[]{:S(2)}) collective-permute-start(bf16[448,1024]{1,0:T(8,128)(2,1)S(1)} %relay.1.refs_3_.refs_0_), channel_id=1, source_target_pairs={{1,0},{2,3},{5,4},{6,7},{9,8},{10,11},{13,12},{14,15},{17,16},{18,... | collective-permute-start | bytes 2752520 | tf_op jit(solution)/shard_map/ppermute | solution.py:404
  51.6 12.3 %collective-permute-start.16 = (bf16[448,512]{1,0:T(8,128)(2,1)S(1)}, bf16[448,512]{1,0:T(8,128)(2,1)S(1)}, u32[]{:S(2)}, u32[]{:S(2)}) collective-permute-start(bf16[448,512]{1,0:T(8,128)(2,1)S(1)} %add.30.refs_2_.refs_0_), channel_id=1, source_target_pairs={{0,16},{4,20},{8,24},{12,28},{16,0},{20,4},{24,8},{28,12},{1,17},{... | collective-permute-start | bytes 1376264 | tf_op jit(solution)/shard_map/ppermute | solution.py:174
  53.2 1.5 %collective-permute-start.12 = (bf16[224,512]{1,0:T(8,128)(2,1)S(1)}, bf16[224,512]{1,0:T(8,128)(2,1)S(1)}, u32[]{:S(2)}, u32[]{:S(2)}) collective-permute-start(bf16[224,512]{1,0:T(8,128)(2,1)S(1)} %get-tuple-element.51.refs_1_), channel_id=1, source_target_pairs={{0,4},{4,0},{8,12},{12,8},{16,20},{20,16},{24,28},{28,24},{1,5},{5... | collective-permute-start | bytes 688136 | tf_op jit(solution)/shard_map/ppermute | solution.py:174
  53.2 1.8 %collective-permute-start.13 = (bf16[224,512]{1,0:T(8,128)(2,1)S(1)}, bf16[224,512]{1,0:T(8,128)(2,1)S(1)}, u32[]{:S(2)}, u32[]{:S(2)}) collective-permute-start(bf16[224,512]{1,0:T(8,128)(2,1)S(1)} %get-tuple-element.52), channel_id=1, source_target_pairs={{0,4},{4,0},{8,12},{12,8},{16,20},{20,16},{24,28},{28,24},{1,5},{5... | collective-permute-start | bytes 688136 | tf_op jit(solution)/shard_map/ppermute | solution.py:174
  53.7 8.0 %collective-permute-start.17 = (bf16[112,512]{1,0:T(8,128)(2,1)S(1)}, bf16[112,512]{1,0:T(8,128)(2,1)S(1)}, u32[]{:S(2)}, u32[]{:S(2)}) collective-permute-start(bf16[112,512]{1,0:T(8,128)(2,1)S(1)} %merge.4.refs_0_), channel_id=1, source_target_pairs={{0,2},{1,3},{2,0},{3,1},{4,6},{5,7},{6,4},{7,5},{8,10},{9,11},{10,... | collective-permute-start | bytes 344072 | tf_op jit(solution)/shard_map/ppermute | solution.py:174
  55.1 9.9 %collective-permute-start.15 = (bf16[224,512]{1,0:T(8,128)(2,1)S(1)}, bf16[224,512]{1,0:T(8,128)(2,1)S(1)}, u32[]{:S(2)}, u32[]{:S(2)}) collective-permute-start(bf16[224,512]{1,0:T(8,128)(2,1)S(1)} %get-tuple-element.53.refs_4_.mine), channel_id=1, source_target_pairs={{0,8},{4,12},{8,0},{12,4},{16,24},{20,28},{24,16},{28,20},{1,9},{5... | collective-permute-start | bytes 688136 | tf_op jit(solution)/shard_map/ppermute | solution.py:174
  56.7 10.1 %collective-permute-start.18 = (bf16[224,512]{1,0:T(8,128)(2,1)S(1)}, bf16[224,512]{1,0:T(8,128)(2,1)S(1)}, u32[]{:S(2)}, u32[]{:S(2)}) collective-permute-start(bf16[224,512]{1,0:T(8,128)(2,1)S(1)} %get-tuple-element.56.mine), channel_id=1, source_target_pairs={{0,16},{4,20},{8,24},{12,28},{16,0},{20,4},{24,8},{28,12},{1,17},{... | collective-permute-start | bytes 688136 | tf_op jit(solution)/shard_map/ppermute | solution.py:174
  64.4 4.0 %collective-permute-start.22 = (bf16[2,112,512]{2,1,0:T(8,128)(2,1)S(1)}, bf16[2,112,512]{2,1,0:T(8,128)(2,1)S(1)}, u32[]{:S(2)}, u32[]{:S(2)}) collective-permute-start(bf16[2,112,512]{2,1,0:T(8,128)(2,1)S(1)} %get-tuple-element.55.refs_1_.refs_0_), channel_id=1, source_target_pairs={{0,4},{4,0},{8,12},{12,8},{16,20},{20,16},{24,28},{28,24},{1,5},{5... | collective-permute-start | bytes 688136 | tf_op jit(solution)/shard_map/ppermute | solution.py:174
  64.5 3.9 %collective-permute-start.23 = (bf16[2,112,512]{2,1,0:T(8,128)(2,1)S(1)}, bf16[2,112,512]{2,1,0:T(8,128)(2,1)S(1)}, u32[]{:S(2)}, u32[]{:S(2)}) collective-permute-start(bf16[2,112,512]{2,1,0:T(8,128)(2,1)S(1)} %get-tuple-element.58.refs_1_), channel_id=1, source_target_pairs={{0,4},{4,0},{8,12},{12,8},{16,20},{20,16},{24,28},{28,24},{1,5},{5... | collective-permute-start | bytes 688136 | tf_op jit(solution)/shard_map/ppermute | solution.py:174
  65.1 9.1 %collective-permute-start.19 = (bf16[224,512]{1,0:T(8,128)(2,1)S(1)}, bf16[224,512]{1,0:T(8,128)(2,1)S(1)}, u32[]{:S(2)}, u32[]{:S(2)}) collective-permute-start(bf16[224,512]{1,0:T(8,128)(2,1)S(1)} %add.32.refs_1_.refs_0_), channel_id=1, source_target_pairs={{0,16},{4,20},{8,24},{12,28},{16,0},{20,4},{24,8},{28,12},{1,17},{... | collective-permute-start | bytes 688136 | tf_op jit(solution)/shard_map/ppermute | solution.py:174
  66.8 7.4 %collective-permute-start.20 = (bf16[224,512]{1,0:T(8,128)(2,1)S(1)}, bf16[224,512]{1,0:T(8,128)(2,1)S(1)}, u32[]{:S(2)}, u32[]{:S(2)}) collective-permute-start(bf16[224,512]{1,0:T(8,128)(2,1)S(1)} %add.33.refs_5_.refs_1_), channel_id=1, source_target_pairs={{0,8},{4,12},{8,0},{12,4},{16,24},{20,28},{24,16},{28,20},{1,9},{5... | collective-permute-start | bytes 688136 | tf_op jit(solution)/shard_map/ppermute | solution.py:174
  73.1 1.6 %collective-permute-start.27 = (bf16[224,512]{1,0:T(8,128)(2,1)S(1)}, bf16[224,512]{1,0:T(8,128)(2,1)S(1)}, u32[]{:S(2)}, u32[]{:S(2)}) collective-permute-start(bf16[224,512]{1,0:T(8,128)(2,1)S(1)} %get-tuple-element.59.refs_6_), channel_id=1, source_target_pairs={{0,4},{4,0},{8,12},{12,8},{16,20},{20,16},{24,28},{28,24},{1,5},{5... | collective-permute-start | bytes 688136 | tf_op jit(solution)/shard_map/ppermute | solution.py:174
  73.2 1.8 %collective-permute-start.28 = (bf16[224,512]{1,0:T(8,128)(2,1)S(1)}, bf16[224,512]{1,0:T(8,128)(2,1)S(1)}, u32[]{:S(2)}, u32[]{:S(2)}) collective-permute-start(bf16[224,512]{1,0:T(8,128)(2,1)S(1)} %get-tuple-element.63), channel_id=1, source_target_pairs={{0,4},{4,0},{8,12},{12,8},{16,20},{20,16},{24,28},{28,24},{1,5},{5... | collective-permute-start | bytes 688136 | tf_op jit(solution)/shard_map/ppermute | solution.py:174
  75.1 10.6 %collective-permute-start.30 = (bf16[224,512]{1,0:T(8,128)(2,1)S(1)}, bf16[224,512]{1,0:T(8,128)(2,1)S(1)}, u32[]{:S(2)}, u32[]{:S(2)}) collective-permute-start(bf16[224,512]{1,0:T(8,128)(2,1)S(1)} %get-tuple-element.65.mine.refs_1_), channel_id=1, source_target_pairs={{0,8},{4,12},{8,0},{12,4},{16,24},{20,28},{24,16},{28,20},{1,9},{5... | collective-permute-start | bytes 688136 | tf_op jit(solution)/shard_map/ppermute | solution.py:174
  76.6 9.1 %collective-permute-start.29 = (bf16[224,512]{1,0:T(8,128)(2,1)S(1)}, bf16[224,512]{1,0:T(8,128)(2,1)S(1)}, u32[]{:S(2)}, u32[]{:S(2)}) collective-permute-start(bf16[224,512]{1,0:T(8,128)(2,1)S(1)} %get-tuple-element.64.mine), channel_id=1, source_target_pairs={{0,16},{4,20},{8,24},{12,28},{16,0},{20,4},{24,8},{28,12},{1,17},{... | collective-permute-start | bytes 688136 | tf_op jit(solution)/shard_map/ppermute | solution.py:174
  78.1 7.5 %collective-permute-start.26 = (bf16[112,512]{1,0:T(8,128)(2,1)S(1)}, bf16[112,512]{1,0:T(8,128)(2,1)S(1)}, u32[]{:S(2)}, u32[]{:S(2)}) collective-permute-start(bf16[112,512]{1,0:T(8,128)(2,1)S(1)} %merge.5.refs_3_), channel_id=1, source_target_pairs={{0,2},{1,3},{2,0},{3,1},{4,6},{5,7},{6,4},{7,5},{8,10},{9,11},{10,... | collective-permute-start | bytes 344072 | tf_op jit(solution)/shard_map/ppermute | solution.py:174
  78.3 8.6 %collective-permute-start.24 = (bf16[2,112,512]{2,1,0:T(8,128)(2,1)S(1)}, bf16[2,112,512]{2,1,0:T(8,128)(2,1)S(1)}, u32[]{:S(2)}, u32[]{:S(2)}) collective-permute-start(bf16[2,112,512]{2,1,0:T(8,128)(2,1)S(1)} %get-tuple-element.60.refs_2_.refs_0_), channel_id=1, source_target_pairs={{0,4},{4,0},{8,12},{12,8},{16,20},{20,16},{24,28},{28,24},{1,5},{5... | collective-permute-start | bytes 688136 | tf_op jit(solution)/shard_map/ppermute | solution.py:174
  78.3 8.6 %collective-permute-start.25 = (bf16[2,112,512]{2,1,0:T(8,128)(2,1)S(1)}, bf16[2,112,512]{2,1,0:T(8,128)(2,1)S(1)}, u32[]{:S(2)}, u32[]{:S(2)}) collective-permute-start(bf16[2,112,512]{2,1,0:T(8,128)(2,1)S(1)} %get-tuple-element.61.refs_1_), channel_id=1, source_target_pairs={{0,4},{4,0},{8,12},{12,8},{16,20},{20,16},{24,28},{28,24},{1,5},{5... | collective-permute-start | bytes 688136 | tf_op jit(solution)/shard_map/ppermute | solution.py:174
  85.8 7.6 %collective-permute-start.33 = (bf16[224,512]{1,0:T(8,128)(2,1)S(1)}, bf16[224,512]{1,0:T(8,128)(2,1)S(1)}, u32[]{:S(2)}, u32[]{:S(2)}) collective-permute-start(bf16[224,512]{1,0:T(8,128)(2,1)S(1)} %add.36.refs_7_.refs_1_), channel_id=1, source_target_pairs={{0,8},{4,12},{8,0},{12,4},{16,24},{20,28},{24,16},{28,20},{1,9},{5... | collective-permute-start | bytes 688136 | tf_op jit(solution)/shard_map/ppermute | solution.py:174
  86.4 7.2 %collective-permute-start.32 = (bf16[224,512]{1,0:T(8,128)(2,1)S(1)}, bf16[224,512]{1,0:T(8,128)(2,1)S(1)}, u32[]{:S(2)}, u32[]{:S(2)}) collective-permute-start(bf16[224,512]{1,0:T(8,128)(2,1)S(1)} %add.35.refs_1_.refs_0_), channel_id=1, source_target_pairs={{0,16},{4,20},{8,24},{12,28},{16,0},{20,4},{24,8},{28,12},{1,17},{... | collective-permute-start | bytes 688136 | tf_op jit(solution)/shard_map/ppermute | solution.py:174
  88.2 4.9 %collective-permute-start.31 = (bf16[112,512]{1,0:T(8,128)(2,1)S(1)}, bf16[112,512]{1,0:T(8,128)(2,1)S(1)}, u32[]{:S(2)}, u32[]{:S(2)}) collective-permute-start(bf16[112,512]{1,0:T(8,128)(2,1)S(1)} %get-tuple-element.67.refs_6_), channel_id=1, source_target_pairs={{0,1},{1,0},{2,3},{3,2},{4,5},{5,4},{6,7},{7,6},{8,9},{9,8},{10,11... | collective-permute-start | bytes 344072 | tf_op jit(solution)/shard_map/ppermute | solution.py:174
  94.0 1.6 %collective-permute-start.34 = (bf16[2,112,512]{2,1,0:T(8,128)(2,1)S(1)}, bf16[2,112,512]{2,1,0:T(8,128)(2,1)S(1)}, u32[]{:S(2)}, u32[]{:S(2)}) collective-permute-start(bf16[2,112,512]{2,1,0:T(8,128)(2,1)S(1)} %get-tuple-element.69.refs_0_.refs_3_), channel_id=1, source_target_pairs={{0,4},{4,0},{8,12},{12,8},{16,20},{20,16},{24,28},{28,24},{1,5},{5... | collective-permute-start | bytes 688136 | tf_op jit(solution)/shard_map/ppermute | solution.py:174
  94.0 1.8 %collective-permute-start.35 = (bf16[2,112,512]{2,1,0:T(8,128)(2,1)S(1)}, bf16[2,112,512]{2,1,0:T(8,128)(2,1)S(1)}, u32[]{:S(2)}, u32[]{:S(2)}) collective-permute-start(bf16[2,112,512]{2,1,0:T(8,128)(2,1)S(1)} %get-tuple-element.70.refs_1_), channel_id=1, source_target_pairs={{0,4},{4,0},{8,12},{12,8},{16,20},{20,16},{24,28},{28,24},{1,5},{5... | collective-permute-start | bytes 688136 | tf_op jit(solution)/shard_map/ppermute | solution.py:174
  95.5 8.4 %copy-start.3 = (bf16[512,512]{1,0:T(8,128)(2,1)S(1)}, bf16[512,512]{1,0:T(8,128)(2,1)}, u32[]{:S(2)}) copy-start(bf16[512,512]{1,0:T(8,128)(2,1)} %refs_2_.5) | copy-start | bytes 1572868
  96.9 6.8 %collective-permute-start.36 = (bf16[112,512]{1,0:T(8,128)(2,1)S(1)}, bf16[112,512]{1,0:T(8,128)(2,1)S(1)}, u32[]{:S(2)}, u32[]{:S(2)}) collective-permute-start(bf16[112,512]{1,0:T(8,128)(2,1)S(1)} %get-tuple-element.71.refs_1_), channel_id=1, source_target_pairs={{0,1},{1,0},{2,3},{3,2},{4,5},{5,4},{6,7},{7,6},{8,9},{9,8},{10,11... | collective-permute-start | bytes 344072 | tf_op jit(solution)/shard_map/ppermute | solution.py:174
  97.0 8.7 %collective-permute-start.37 = (bf16[112,512]{1,0:T(8,128)(2,1)S(1)}, bf16[112,512]{1,0:T(8,128)(2,1)S(1)}, u32[]{:S(2)}, u32[]{:S(2)}) collective-permute-start(bf16[112,512]{1,0:T(8,128)(2,1)S(1)} %add.37.refs_1_.refs_0_), channel_id=1, source_target_pairs={{0,2},{1,3},{2,0},{3,1},{4,6},{5,7},{6,4},{7,5},{8,10},{9,11},{10,... | collective-permute-start | bytes 344072 | tf_op jit(solution)/shard_map/ppermute | solution.py:174
  103.6 7.3 %collective-permute-start.38 = (bf16[112,512]{1,0:T(8,128)(2,1)S(1)}, bf16[112,512]{1,0:T(8,128)(2,1)S(1)}, u32[]{:S(2)}, u32[]{:S(2)}) collective-permute-start(bf16[112,512]{1,0:T(8,128)(2,1)S(1)} %add.38.refs_1_.refs_3_), channel_id=1, source_target_pairs={{0,2},{1,3},{2,0},{3,1},{4,6},{5,7},{6,4},{7,5},{8,10},{9,11},{10,... | collective-permute-start | bytes 344072 | tf_op jit(solution)/shard_map/ppermute | solution.py:174

commit v6 on v5

--- a/solution.py
+++ b/solution.py
@@ -18,7 +18,7 @@
 ORDER = (
     "down0", "sum0", "turn0", "down1:hop_b", "sum1", "residual", "hold", "see0",
     "merge0", "hop3", "down2:hop_d", "turn1", "sum2", "see1:far0", "turn2", "turn2",
-    "merge1", "down3", "see2", "sum3", "turn3:far1", "turn3:far0", "merge2", "see3:pair2",
+    "merge1", "down3", "see2", "keep3", "sum3", "turn3:far1", "turn3:far0", "merge2", "see3:pair2",
     "head3", "merge3", "done2", "done3", "early",
 )
 

time: 112 us -> 112 us (level)
  waiting for transfers between devices: 54.5 us -> 52.3 us
    ppermute x35, waiting for transfers between devices: 45.5 us -> 43.3 us  [swap(): return lax.ppermute(x, axis, [(i, i ^ bit) for i in range(size)])]
    pallas_call x4 -> x5, Pallas kernels: 6.65 us -> 7.36 us  [down(): pl.pallas_call(functools.partial(_down_kernel, half, len(blocks), (parts,...]
  transfers between devices with their start and end apart: 39 -> 39, of which waited for: 24 -> 20; matrix products, arithmetic and copies ran while one was open for 2% -> 2% of each run, Pallas kernels for 17% -> 17%
where the time goes in v6:
time: 112 us
  waiting for transfers between devices  52.3 us (47%)
  starting transfers between devices  32.5 us (29%)
  Pallas kernels  22 us (20%)
  local copies, waits for them, and re-layouts  3.55 us (3%)
    ppermute x35, waiting for transfers between devices, swap(): return lax.ppermute(x, axis, [(i, i ^ bit) for i in range(size)])  43.3 us
    ppermute x35, starting transfers between devices, swap(): return lax.ppermute(x, axis, [(i, i ^ bit) for i in range(size)])  28.5 us
    pallas_call x5, Pallas kernels, down(): pl.pallas_call(functools.partial(_down_kernel, half, len(blocks), (parts,...  7.36 us
    ppermute x1, waiting for transfers between devices, per_device(): v['hop_c'] = lax.ppermute(v['hop_b'], 'col', outward)  7.32 us
    pallas_call x4, Pallas kernels, merge(): pl.pallas_call(functools.partial(_merge_kernel, half, len(own), late, fir...  4.9 us
    unnamed x8, local copies, waits for them, and re-layouts  2.78 us
  transfers between devices with their start and end apart: 39, of which 20 were waited for; matrix products, arithmetic and copies ran while one was open for 2% of the time, Pallas kernels for 17%

profile of v6, /device:TPU:0, one launch (start us, length us, event | category | flops | bytes accessed | tf_op | source)
XLA Modules:
  0.0 111.7 jit_solution(13124959125906333077)
XLA Ops:
  0.0 3.0 %collective-permute-start.2 = (bf16[448,1024]{1,0:T(8,128)(2,1)}, bf16[448,1024]{1,0:T(8,128)(2,1)S(1)}, u32[]{:S(2)}, u32[]{:S(2)}) collective-permute-start(bf16[448,1024]{1,0:T(8,128)(2,1)} %refs_0_.1), channel_id=1, source_target_pairs={{0,1},{1,0},{2,3},{3,2},{4,5},{5,4},{6,7},{7,6},{8,9},{9,8},{10,11... | collective-permute-start | bytes 2752520 | tf_op jit(solution)/shard_map/ppermute | solution.py:174
  3.0 0.7 collective-permute-start
  3.8 0.7 broadcast_in_dim.7.refs_2_.scale
  4.5 0.9 broadcast_select_fusion.3
  5.5 1.6 %copy-done = bf16[1024,1024]{1,0:T(8,128)(2,1)S(1)} copy-done((bf16[1024,1024]{1,0:T(8,128)(2,1)S(1)}, bf16[1024,1024]{1,0:T(8,128)(2,1)}, u32[]{:S(2)}) %copy-start) | copy-done | bytes 2097176
  7.1 1.2 %copy-done.2 = bf16[448,1024]{1,0:T(8,128)(2,1)S(1)} copy-done((bf16[448,1024]{1,0:T(8,128)(2,1)S(1)}, bf16[448,1024]{1,0:T(8,128)(2,1)}, u32[]{:S(2)}) %copy-start.2) | copy-done | bytes 917528
  8.3 1.7 %down.5 = (bf16[224,512]{1,0:T(8,128)(2,1)S(1)}, bf16[224,512]{1,0:T(8,128)(2,1)S(1)}, f32[448,512]{1,0:T(8,128)S(1)}) custom-call(s32[7]{0:T(128)S(1)} %stack.35.info, bf16[448,1024]{1,0:T(8,128)(2,1)S(1)} %copy-done.2, bf16[1024,1024]{1,0:T(8,128)(2,1)S(1)} %copy-done, bf16[1,1024]{1,0:T(2,128)(2,1)S(1)} %broadcast_in_dim.7.refs_2_.scale, s32[1,448]{1,0:T(1,128)S(1)} %bitcast.8), custom_call_target="tpu_custom_call" | custom-call | flops 1 | bytes 1 | tf_op jit(solution)/shard_map/down/pallas_call | solution.py:240
  10.5 1.0 collective-permute-done.4.refs_0_
  11.9 1.6 %collective-permute-start.6 = (bf16[448,512]{1,0:T(8,128)(2,1)S(1)}, bf16[448,512]{1,0:T(8,128)(2,1)S(1)}, u32[]{:S(2)}, u32[]{:S(2)}) collective-permute-start(bf16[448,512]{1,0:T(8,128)(2,1)S(1)} %add.27.mine.refs_1_), channel_id=1, source_target_pairs={{0,8},{4,12},{8,0},{12,4},{16,24},{20,28},{24,16},{28,20},{1,9},{5... | collective-permute-start | bytes 1376264 | tf_op jit(solution)/shard_map/ppermute | solution.py:174
  13.5 10.1 %collective-permute-done.2.refs_0_ = bf16[448,1024]{1,0:T(8,128)(2,1)S(1)} collective-permute-done((bf16[448,1024]{1,0:T(8,128)(2,1)}, bf16[448,1024]{1,0:T(8,128)(2,1)S(1)}, u32[]{:S(2)}, u32[]{:S(2)}) %collective-permute-start.2) | collective-permute-done | bytes 917536 | tf_op jit(solution)/shard_map/ppermute | solution.py:174
  23.6 0.7 collective-permute-start.3
  24.3 1.3 %collective-permute-start.1 = (bf16[448,1024]{1,0:T(8,128)(2,1)S(1)}, bf16[448,1024]{1,0:T(8,128)(2,1)S(1)}, u32[]{:S(2)}, u32[]{:S(2)}) collective-permute-start(bf16[448,1024]{1,0:T(8,128)(2,1)S(1)} %collective-permute-done.refs_3_.refs_0_), channel_id=1, source_target_pairs={{1,0},{2,3},{5,4},{6,7},{9,8},{10,11},{13,12},{14,15},{17,16},{18,... | collective-permute-start | bytes 2752520 | tf_op jit(solution)/shard_map/ppermute | solution.py:399
  25.7 1.8 %collective-permute-start.7 = (bf16[448,512]{1,0:T(8,128)(2,1)S(1)}, bf16[448,512]{1,0:T(8,128)(2,1)S(1)}, u32[]{:S(2)}, u32[]{:S(2)}) collective-permute-start(bf16[448,512]{1,0:T(8,128)(2,1)S(1)} %add.28.refs_2_.refs_0_), channel_id=1, source_target_pairs={{0,16},{4,20},{8,24},{12,28},{16,0},{20,4},{24,8},{28,12},{1,17},{... | collective-permute-start | bytes 1376264 | tf_op jit(solution)/shard_map/ppermute | solution.py:174
  27.5 1.7 %down.6 = (bf16[224,512]{1,0:T(8,128)(2,1)S(1)}, bf16[224,512]{1,0:T(8,128)(2,1)S(1)}, f32[448,512]{1,0:T(8,128)S(1)}) custom-call(s32[7]{0:T(128)S(1)} %stack.35.info, bf16[448,1024]{1,0:T(8,128)(2,1)S(1)} %collective-permute-done.2.refs_0_, bf16[1024,1024]{1,0:T(8,128)(2,1)S(1)} %copy-done.1, bf16[448,512]{1,0:T(8,128)(2,1)S(1)} %add.28.refs_2_.refs_0_, ...), custom_call_target="tpu_custom_call" | custom-call | flops 1 | bytes 1 | tf_op jit(solution)/shard_map/down/pallas_call | solution.py:240
  29.7 1.0 collective-permute-done.8.refs_0_
  31.1 1.6 %collective-permute-start.14 = (bf16[448,512]{1,0:T(8,128)(2,1)S(1)}, bf16[448,512]{1,0:T(8,128)(2,1)S(1)}, u32[]{:S(2)}, u32[]{:S(2)}) collective-permute-start(bf16[448,512]{1,0:T(8,128)(2,1)S(1)} %add.29.refs_0_.mine), channel_id=1, source_target_pairs={{0,8},{4,12},{8,0},{12,4},{16,24},{20,28},{24,16},{28,20},{1,9},{5... | collective-permute-start | bytes 1376264 | tf_op jit(solution)/shard_map/ppermute | solution.py:174
  32.7 2.0 %residuals.1 = (bf16[448,512]{1,0:T(8,128)(2,1)S(1)}, bf16[448,512]{1,0:T(8,128)(2,1)S(1)}, bf16[448,512]{1,0:T(8,128)(2,1)S(1)}, bf16[448,512]{1,0:T(8,128)(2,1)S(1)}, f32[1,512]{1,0:T(1,128)S(1)}) custom-call(s32[7]{0:T(128)S(1)} %stack.35.info, bf16[1792,1024]{1,0:T(8,128)(2,1)} %tokens.1, bf16[1,1024]{1,0:T(2,128)(2,1)S(1)} %broadcast_in_dim.7.refs_2_.scale, ...), custom_call_target="tpu_custom_call" | custom-call | flops 1 | bytes 1 | tf_op jit(solution)/shard_map/residuals/pallas_call | solution.py:210
  34.7 2.2 %hold.1.refs_4_.refs_2_ = bf16[4,1024,512]{2,1,0:T(8,128)(2,1)S(1)} custom-call(bf16[4,1024,512]{2,1,0:T(8,128)(2,1)} %weight.1, bf16[448,512]{1,0:T(8,128)(2,1)S(1)} %get-tuple-element.45.refs_0_.refs_2_), custom_call_target="tpu_custom_call" | custom-call | flops 1 | bytes 1 | tf_op jit(solution)/shard_map/hold/pallas_call | solution.py:196
  38.5 1.0 collective-permute-done.10.refs_2_
  39.8 1.3 %merge.4.refs_0_ = bf16[112,512]{1,0:T(8,128)(2,1)S(1)} custom-call(s32[7]{0:T(128)S(1)} %stack.35.info, bf16[2,112,512]{2,1,0:T(8,128)(2,1)S(1)} %get-tuple-element.47.refs_0_.refs_5_, bf16[2,112,512]{2,1,0:T(8,128)(2,1)S(1)} %get-tuple-element.48.refs_1_, bf16[2,112,512]{2,1,0:T(8,128)(2,1)S(1)} %collective-permute-done.10.refs_2_, ...), custom_call_target="tpu_custom_call" | custom-call | flops 1 | bytes 1 | tf_op jit(solution)/shard_map/merge/pallas_call | solution.py:301
  41.2 1.3 %collective-permute-start.21 = (bf16[448,1024]{1,0:T(8,128)(2,1)S(1)}, bf16[448,1024]{1,0:T(8,128)(2,1)S(1)}, u32[]{:S(2)}, u32[]{:S(2)}) collective-permute-start(bf16[448,1024]{1,0:T(8,128)(2,1)S(1)} %relay.1.refs_3_.refs_0_), channel_id=1, source_target_pairs={{1,0},{2,3},{5,4},{6,7},{9,8},{10,11},{13,12},{14,15},{17,16},{18,... | collective-permute-start | bytes 2752520 | tf_op jit(solution)/shard_map/ppermute | solution.py:404
  42.5 7.3 %collective-permute-done.1.refs_1_ = bf16[448,1024]{1,0:T(8,128)(2,1)S(1)} collective-permute-done((bf16[448,1024]{1,0:T(8,128)(2,1)S(1)}, bf16[448,1024]{1,0:T(8,128)(2,1)S(1)}, u32[]{:S(2)}, u32[]{:S(2)}) %collective-permute-start.1) | collective-permute-done | bytes 917536 | tf_op jit(solution)/shard_map/ppermute | solution.py:399
  49.8 1.7 %down.7 = (bf16[224,512]{1,0:T(8,128)(2,1)S(1)}, bf16[224,512]{1,0:T(8,128)(2,1)S(1)}, f32[448,512]{1,0:T(8,128)S(1)}) custom-call(s32[7]{0:T(128)S(1)} %stack.35.info, bf16[448,1024]{1,0:T(8,128)(2,1)S(1)} %collective-permute-done.refs_3_.refs_0_, bf16[448,1024]{1,0:T(8,128)(2,1)S(1)} %collective-permute-done.1.refs_1_, bf16[1024,1024]{1,0:T(8,128)(2,1)S(1)} %copy-done.1, ...), custom_call_target="tpu_custom_call" | custom-call | flops 1 | bytes 1 | tf_op jit(solution)/shard_map/down/pallas_call | solution.py:240
  51.6 1.6 %collective-permute-start.16 = (bf16[448,512]{1,0:T(8,128)(2,1)S(1)}, bf16[448,512]{1,0:T(8,128)(2,1)S(1)}, u32[]{:S(2)}, u32[]{:S(2)}) collective-permute-start(bf16[448,512]{1,0:T(8,128)(2,1)S(1)} %add.30.refs_2_.refs_0_), channel_id=1, source_target_pairs={{0,16},{4,20},{8,24},{12,28},{16,0},{20,4},{24,8},{28,12},{1,17},{... | collective-permute-start | bytes 1376264 | tf_op jit(solution)/shard_map/ppermute | solution.py:174
  53.7 1.0 collective-permute-start.17
  55.1 1.6 %collective-permute-start.15 = (bf16[224,512]{1,0:T(8,128)(2,1)S(1)}, bf16[224,512]{1,0:T(8,128)(2,1)S(1)}, u32[]{:S(2)}, u32[]{:S(2)}) collective-permute-start(bf16[224,512]{1,0:T(8,128)(2,1)S(1)} %get-tuple-element.52.refs_4_.mine), channel_id=1, source_target_pairs={{0,8},{4,12},{8,0},{12,4},{16,24},{20,28},{24,16},{28,20},{1,9},{5... | collective-permute-start | bytes 688136 | tf_op jit(solution)/shard_map/ppermute | solution.py:174
  57.2 4.5 %collective-permute-done.17.refs_5_.refs_2_ = bf16[112,512]{1,0:T(8,128)(2,1)S(1)} collective-permute-done((bf16[112,512]{1,0:T(8,128)(2,1)S(1)}, bf16[112,512]{1,0:T(8,128)(2,1)S(1)}, u32[]{:S(2)}, u32[]{:S(2)}) %collective-permute-start.17) | collective-permute-done | bytes 114720 | tf_op jit(solution)/shard_map/ppermute | solution.py:174
  61.7 2.3 %collective-permute-done.16.refs_1_ = bf16[448,512]{1,0:T(8,128)(2,1)S(1)} collective-permute-done((bf16[448,512]{1,0:T(8,128)(2,1)S(1)}, bf16[448,512]{1,0:T(8,128)(2,1)S(1)}, u32[]{:S(2)}, u32[]{:S(2)}) %collective-permute-start.16) | collective-permute-done | bytes 458784 | tf_op jit(solution)/shard_map/ppermute | solution.py:174
  65.1 1.7 %collective-permute-start.19 = (bf16[224,512]{1,0:T(8,128)(2,1)S(1)}, bf16[224,512]{1,0:T(8,128)(2,1)S(1)}, u32[]{:S(2)}, u32[]{:S(2)}) collective-permute-start(bf16[224,512]{1,0:T(8,128)(2,1)S(1)} %add.32.refs_1_.refs_0_), channel_id=1, source_target_pairs={{0,16},{4,20},{8,24},{12,28},{16,0},{20,4},{24,8},{28,12},{1,17},{... | collective-permute-start | bytes 688136 | tf_op jit(solution)/shard_map/ppermute | solution.py:174
  66.8 1.6 %collective-permute-start.20 = (bf16[224,512]{1,0:T(8,128)(2,1)S(1)}, bf16[224,512]{1,0:T(8,128)(2,1)S(1)}, u32[]{:S(2)}, u32[]{:S(2)}) collective-permute-start(bf16[224,512]{1,0:T(8,128)(2,1)S(1)} %add.33.refs_5_.refs_1_), channel_id=1, source_target_pairs={{0,8},{4,12},{8,0},{12,4},{16,24},{20,28},{24,16},{28,20},{1,9},{5... | collective-permute-start | bytes 688136 | tf_op jit(solution)/shard_map/ppermute | solution.py:174
  68.4 1.3 %merge.5.refs_3_ = bf16[112,512]{1,0:T(8,128)(2,1)S(1)} custom-call(s32[7]{0:T(128)S(1)} %stack.35.info, bf16[2,112,512]{2,1,0:T(8,128)(2,1)S(1)} %get-tuple-element.54.refs_1_.refs_0_, bf16[2,112,512]{2,1,0:T(8,128)(2,1)S(1)} %get-tuple-element.57.refs_1_, bf16[2,112,512]{2,1,0:T(8,128)(2,1)S(1)} %collective-permute-done.22.refs_2_, ...), custom_call_target="tpu_custom_call" | custom-call | flops 1 | bytes 1 | tf_op jit(solution)/shard_map/merge/pallas_call | solution.py:301
  69.7 1.7 %collective-permute-done.21.refs_1_ = bf16[448,1024]{1,0:T(8,128)(2,1)S(1)} collective-permute-done((bf16[448,1024]{1,0:T(8,128)(2,1)S(1)}, bf16[448,1024]{1,0:T(8,128)(2,1)S(1)}, u32[]{:S(2)}, u32[]{:S(2)}) %collective-permute-start.21) | collective-permute-done | bytes 917536 | tf_op jit(solution)/shard_map/ppermute | solution.py:404
  71.4 1.2 %down.8 = (bf16[224,512]{1,0:T(8,128)(2,1)S(1)}, bf16[224,512]{1,0:T(8,128)(2,1)S(1)}) custom-call(s32[7]{0:T(128)S(1)} %stack.35.info, bf16[448,1024]{1,0:T(8,128)(2,1)S(1)} %relay.1.refs_3_.refs_0_, bf16[448,1024]{1,0:T(8,128)(2,1)S(1)} %collective-permute-done.21.refs_1_, bf16[1024,1024]{1,0:T(8,128)(2,1)S(1)} %copy-done.1, bf16[112,512]{1,0:T(8,128)(2,1)S(1)} %merge.5.refs_3_), custom_call_target="tpu_custom_call" | custom-call | flops 1 | bytes 1 | tf_op jit(solution)/shard_map/down/pallas_call | solution.py:240
  73.2 1.0 collective-permute-done.20.refs_3_
  74.5 1.2 %down.9.mine.refs_2_ = f32[448,512]{1,0:T(8,128)S(1)} custom-call(s32[7]{0:T(128)S(1)} %stack.35.info, bf16[448,1024]{1,0:T(8,128)(2,1)S(1)} %relay.1.refs_3_.refs_0_, bf16[448,1024]{1,0:T(8,128)(2,1)S(1)} %collective-permute-done.21.refs_1_, bf16[1024,1024]{1,0:T(8,128)(2,1)S(1)} %copy-done.1, bf16[2,112,512]{2,1,0:T(8,128)(2,1)S(1)} %get-tuple-element.59.refs_3_.refs_0_), custom_call_target="tpu_custom_call" | custom-call | flops 1 | bytes 1 | tf_op jit(solution)/shard_map/down/pallas_call | solution.py:240
  75.8 1.6 %collective-permute-start.30 = (bf16[224,512]{1,0:T(8,128)(2,1)S(1)}, bf16[224,512]{1,0:T(8,128)(2,1)S(1)}, u32[]{:S(2)}, u32[]{:S(2)}) collective-permute-start(bf16[224,512]{1,0:T(8,128)(2,1)S(1)} %get-tuple-element.63.mine.refs_1_), channel_id=1, source_target_pairs={{0,8},{4,12},{8,0},{12,4},{16,24},{20,28},{24,16},{28,20},{1,9},{5... | collective-permute-start | bytes 688136 | tf_op jit(solution)/shard_map/ppermute | solution.py:174
  77.9 1.6 %collective-permute-start.26 = (bf16[112,512]{1,0:T(8,128)(2,1)S(1)}, bf16[112,512]{1,0:T(8,128)(2,1)S(1)}, u32[]{:S(2)}, u32[]{:S(2)}) collective-permute-start(bf16[112,512]{1,0:T(8,128)(2,1)S(1)} %merge.5.refs_3_), channel_id=1, source_target_pairs={{0,2},{1,3},{2,0},{3,1},{4,6},{5,7},{6,4},{7,5},{8,10},{9,11},{10,... | collective-permute-start | bytes 344072 | tf_op jit(solution)/shard_map/ppermute | solution.py:174
  80.0 5.3 %collective-permute-done.26.refs_2_.refs_6_ = bf16[112,512]{1,0:T(8,128)(2,1)S(1)} collective-permute-done((bf16[112,512]{1,0:T(8,128)(2,1)S(1)}, bf16[112,512]{1,0:T(8,128)(2,1)S(1)}, u32[]{:S(2)}, u32[]{:S(2)}) %collective-permute-start.26) | collective-permute-done | bytes 114720 | tf_op jit(solution)/shard_map/ppermute | solution.py:174
  86.1 1.0 collective-permute-start.32
  87.1 1.3 %merge.6 = (bf16[112,512]{1,0:T(8,128)(2,1)S(1)}, f32[112,512]{1,0:T(8,128)S(1)}) custom-call(s32[7]{0:T(128)S(1)} %stack.35.info, bf16[2,112,512]{2,1,0:T(8,128)(2,1)S(1)} %get-tuple-element.59.refs_3_.refs_0_, bf16[2,112,512]{2,1,0:T(8,128)(2,1)S(1)} %get-tuple-element.60.refs_1_, bf16[2,112,512]{2,1,0:T(8,128)(2,1)S(1)} %collective-permute-done.24.refs_2_, ...), custom_call_target="tpu_custom_call" | custom-call | flops 1 | bytes 1 | tf_op jit(solution)/shard_map/merge/pallas_call | solution.py:301
  88.5 4.8 %collective-permute-done.31.refs_7_.refs_0_ = bf16[112,512]{1,0:T(8,128)(2,1)S(1)} collective-permute-done((bf16[112,512]{1,0:T(8,128)(2,1)S(1)}, bf16[112,512]{1,0:T(8,128)(2,1)S(1)}, u32[]{:S(2)}, u32[]{:S(2)}) %collective-permute-start.31) | collective-permute-done | bytes 114720 | tf_op jit(solution)/shard_map/ppermute | solution.py:174
  94.2 1.0 merge_head.1.refs_7_.refs_8_
  95.5 1.0 merge.7
  96.6 2.7 %collective-permute-start.37 = (bf16[112,512]{1,0:T(8,128)(2,1)S(1)}, bf16[112,512]{1,0:T(8,128)(2,1)S(1)}, u32[]{:S(2)}, u32[]{:S(2)}) collective-permute-start(bf16[112,512]{1,0:T(8,128)(2,1)S(1)} %add.37.refs_1_.refs_0_), channel_id=1, source_target_pairs={{0,2},{1,3},{2,0},{3,1},{4,6},{5,7},{6,4},{7,5},{8,10},{9,11},{10,... | collective-permute-start | bytes 344072 | tf_op jit(solution)/shard_map/ppermute | solution.py:174
  99.3 4.3 %collective-permute-done.36.refs_0_ = bf16[112,512]{1,0:T(8,128)(2,1)S(1)} collective-permute-done((bf16[112,512]{1,0:T(8,128)(2,1)S(1)}, bf16[112,512]{1,0:T(8,128)(2,1)S(1)}, u32[]{:S(2)}, u32[]{:S(2)}) %collective-permute-start.36) | collective-permute-done | bytes 114720 | tf_op jit(solution)/shard_map/ppermute | solution.py:174
  103.8 1.0 place_early.1
  105.3 5.3 %collective-permute-done.38.refs_1_ = bf16[112,512]{1,0:T(8,128)(2,1)S(1)} collective-permute-done((bf16[112,512]{1,0:T(8,128)(2,1)S(1)}, bf16[112,512]{1,0:T(8,128)(2,1)S(1)}, u32[]{:S(2)}, u32[]{:S(2)}) %collective-permute-start.38) | collective-permute-done | bytes 114720 | tf_op jit(solution)/shard_map/ppermute | solution.py:174
  110.6 1.1 place_late.1
  (73 shorter events, 11.6 us)
Async XLA Ops:
  0.0 23.6 %collective-permute-start.2 = (bf16[448,1024]{1,0:T(8,128)(2,1)}, bf16[448,1024]{1,0:T(8,128)(2,1)S(1)}, u32[]{:S(2)}, u32[]{:S(2)}) collective-permute-start(bf16[448,1024]{1,0:T(8,128)(2,1)} %refs_0_.1), channel_id=1, source_target_pairs={{0,1},{1,0},{2,3},{3,2},{4,5},{5,4},{6,7},{7,6},{8,9},{9,8},{10,11... | collective-permute-start | bytes 2752520 | tf_op jit(solution)/shard_map/ppermute | solution.py:174
  3.0 21.3 %collective-permute-start = (bf16[448,1024]{1,0:T(8,128)(2,1)}, bf16[448,1024]{1,0:T(8,128)(2,1)S(1)}, u32[]{:S(2)}, u32[]{:S(2)}) collective-permute-start(bf16[448,1024]{1,0:T(8,128)(2,1)} %refs_0_.1), channel_id=1, source_target_pairs={{1,2},{2,1},{5,6},{6,5},{9,10},{10,9},{13,14},{14,13},{17,18},{18,... | collective-permute-start | bytes 2752520 | tf_op jit(solution)/shard_map/ppermute | solution.py:398
  5.5 1.6 %copy-start = (bf16[1024,1024]{1,0:T(8,128)(2,1)S(1)}, bf16[1024,1024]{1,0:T(8,128)(2,1)}, u32[]{:S(2)}) copy-start(bf16[1024,1024]{1,0:T(8,128)(2,1)} %refs_2_.6) | copy-start | bytes 6291460
  7.1 1.2 %copy-start.2 = (bf16[448,1024]{1,0:T(8,128)(2,1)S(1)}, bf16[448,1024]{1,0:T(8,128)(2,1)}, u32[]{:S(2)}) copy-start(bf16[448,1024]{1,0:T(8,128)(2,1)} %refs_0_.1) | copy-start | bytes 2752516
  8.3 19.2 %copy-start.1 = (bf16[1024,1024]{1,0:T(8,128)(2,1)S(1)}, bf16[1024,1024]{1,0:T(8,128)(2,1)}, u32[]{:S(2)}) copy-start(bf16[1024,1024]{1,0:T(8,128)(2,1)} %refs_2_.6) | copy-start | bytes 6291460
  10.0 1.6 %collective-permute-start.4 = (bf16[224,512]{1,0:T(8,128)(2,1)S(1)}, bf16[224,512]{1,0:T(8,128)(2,1)S(1)}, u32[]{:S(2)}, u32[]{:S(2)}) collective-permute-start(bf16[224,512]{1,0:T(8,128)(2,1)S(1)} %get-tuple-element.40.refs_2_), channel_id=1, source_target_pairs={{0,4},{4,0},{8,12},{12,8},{16,20},{20,16},{24,28},{28,24},{1,5},{5... | collective-permute-start | bytes 688136 | tf_op jit(solution)/shard_map/ppermute | solution.py:174
  10.0 1.8 %collective-permute-start.5 = (bf16[224,512]{1,0:T(8,128)(2,1)S(1)}, bf16[224,512]{1,0:T(8,128)(2,1)S(1)}, u32[]{:S(2)}, u32[]{:S(2)}) collective-permute-start(bf16[224,512]{1,0:T(8,128)(2,1)S(1)} %get-tuple-element.41), channel_id=1, source_target_pairs={{0,4},{4,0},{8,12},{12,8},{16,20},{20,16},{24,28},{28,24},{1,5},{5... | collective-permute-start | bytes 688136 | tf_op jit(solution)/shard_map/ppermute | solution.py:174
  11.9 13.7 %collective-permute-start.6 = (bf16[448,512]{1,0:T(8,128)(2,1)S(1)}, bf16[448,512]{1,0:T(8,128)(2,1)S(1)}, u32[]{:S(2)}, u32[]{:S(2)}) collective-permute-start(bf16[448,512]{1,0:T(8,128)(2,1)S(1)} %add.27.mine.refs_1_), channel_id=1, source_target_pairs={{0,8},{4,12},{8,0},{12,4},{16,24},{20,28},{24,16},{28,20},{1,9},{5... | collective-permute-start | bytes 1376264 | tf_op jit(solution)/shard_map/ppermute | solution.py:174
  23.6 17.6 %collective-permute-start.3 = (bf16[448,1024]{1,0:T(8,128)(2,1)S(1)}, bf16[448,1024]{1,0:T(8,128)(2,1)S(1)}, u32[]{:S(2)}, u32[]{:S(2)}) collective-permute-start(bf16[448,1024]{1,0:T(8,128)(2,1)S(1)} %collective-permute-done.2.refs_0_), channel_id=1, source_target_pairs={{1,2},{2,1},{5,6},{6,5},{9,10},{10,9},{13,14},{14,13},{17,18},{18,... | collective-permute-start | bytes 2752520 | tf_op jit(solution)/shard_map/ppermute | solution.py:400
  24.3 25.5 %collective-permute-start.1 = (bf16[448,1024]{1,0:T(8,128)(2,1)S(1)}, bf16[448,1024]{1,0:T(8,128)(2,1)S(1)}, u32[]{:S(2)}, u32[]{:S(2)}) collective-permute-start(bf16[448,1024]{1,0:T(8,128)(2,1)S(1)} %collective-permute-done.refs_3_.refs_0_), channel_id=1, source_target_pairs={{1,0},{2,3},{5,4},{6,7},{9,8},{10,11},{13,12},{14,15},{17,16},{18,... | collective-permute-start | bytes 2752520 | tf_op jit(solution)/shard_map/ppermute | solution.py:399
  25.7 11.8 %collective-permute-start.7 = (bf16[448,512]{1,0:T(8,128)(2,1)S(1)}, bf16[448,512]{1,0:T(8,128)(2,1)S(1)}, u32[]{:S(2)}, u32[]{:S(2)}) collective-permute-start(bf16[448,512]{1,0:T(8,128)(2,1)S(1)} %add.28.refs_2_.refs_0_), channel_id=1, source_target_pairs={{0,16},{4,20},{8,24},{12,28},{16,0},{20,4},{24,8},{28,12},{1,17},{... | collective-permute-start | bytes 1376264 | tf_op jit(solution)/shard_map/ppermute | solution.py:174
  29.2 1.6 %collective-permute-start.8 = (bf16[224,512]{1,0:T(8,128)(2,1)S(1)}, bf16[224,512]{1,0:T(8,128)(2,1)S(1)}, u32[]{:S(2)}, u32[]{:S(2)}) collective-permute-start(bf16[224,512]{1,0:T(8,128)(2,1)S(1)} %get-tuple-element.43.refs_2_), channel_id=1, source_target_pairs={{0,4},{4,0},{8,12},{12,8},{16,20},{20,16},{24,28},{28,24},{1,5},{5... | collective-permute-start | bytes 688136 | tf_op jit(solution)/shard_map/ppermute | solution.py:174
  29.2 1.8 %collective-permute-start.9 = (bf16[224,512]{1,0:T(8,128)(2,1)S(1)}, bf16[224,512]{1,0:T(8,128)(2,1)S(1)}, u32[]{:S(2)}, u32[]{:S(2)}) collective-permute-start(bf16[224,512]{1,0:T(8,128)(2,1)S(1)} %get-tuple-element.44), channel_id=1, source_target_pairs={{0,4},{4,0},{8,12},{12,8},{16,20},{20,16},{24,28},{28,24},{1,5},{5... | collective-permute-start | bytes 688136 | tf_op jit(solution)/shard_map/ppermute | solution.py:174
  31.1 20.4 %collective-permute-start.14 = (bf16[448,512]{1,0:T(8,128)(2,1)S(1)}, bf16[448,512]{1,0:T(8,128)(2,1)S(1)}, u32[]{:S(2)}, u32[]{:S(2)}) collective-permute-start(bf16[448,512]{1,0:T(8,128)(2,1)S(1)} %add.29.refs_0_.mine), channel_id=1, source_target_pairs={{0,8},{4,12},{8,0},{12,4},{16,24},{20,28},{24,16},{28,20},{1,9},{5... | collective-permute-start | bytes 1376264 | tf_op jit(solution)/shard_map/ppermute | solution.py:174
  38.0 1.6 %collective-permute-start.10 = (bf16[2,112,512]{2,1,0:T(8,128)(2,1)S(1)}, bf16[2,112,512]{2,1,0:T(8,128)(2,1)S(1)}, u32[]{:S(2)}, u32[]{:S(2)}) collective-permute-start(bf16[2,112,512]{2,1,0:T(8,128)(2,1)S(1)} %get-tuple-element.47.refs_0_.refs_5_), channel_id=1, source_target_pairs={{0,4},{4,0},{8,12},{12,8},{16,20},{20,16},{24,28},{28,24},{1,5},{5... | collective-permute-start | bytes 688136 | tf_op jit(solution)/shard_map/ppermute | solution.py:174
  38.0 1.8 %collective-permute-start.11 = (bf16[2,112,512]{2,1,0:T(8,128)(2,1)S(1)}, bf16[2,112,512]{2,1,0:T(8,128)(2,1)S(1)}, u32[]{:S(2)}, u32[]{:S(2)}) collective-permute-start(bf16[2,112,512]{2,1,0:T(8,128)(2,1)S(1)} %get-tuple-element.48.refs_1_), channel_id=1, source_target_pairs={{0,4},{4,0},{8,12},{12,8},{16,20},{20,16},{24,28},{28,24},{1,5},{5... | collective-permute-start | bytes 688136 | tf_op jit(solution)/shard_map/ppermute | solution.py:174
  41.2 30.2 %collective-permute-start.21 = (bf16[448,1024]{1,0:T(8,128)(2,1)S(1)}, bf16[448,1024]{1,0:T(8,128)(2,1)S(1)}, u32[]{:S(2)}, u32[]{:S(2)}) collective-permute-start(bf16[448,1024]{1,0:T(8,128)(2,1)S(1)} %relay.1.refs_3_.refs_0_), channel_id=1, source_target_pairs={{1,0},{2,3},{5,4},{6,7},{9,8},{10,11},{13,12},{14,15},{17,16},{18,... | collective-permute-start | bytes 2752520 | tf_op jit(solution)/shard_map/ppermute | solution.py:404
  51.6 12.3 %collective-permute-start.16 = (bf16[448,512]{1,0:T(8,128)(2,1)S(1)}, bf16[448,512]{1,0:T(8,128)(2,1)S(1)}, u32[]{:S(2)}, u32[]{:S(2)}) collective-permute-start(bf16[448,512]{1,0:T(8,128)(2,1)S(1)} %add.30.refs_2_.refs_0_), channel_id=1, source_target_pairs={{0,16},{4,20},{8,24},{12,28},{16,0},{20,4},{24,8},{28,12},{1,17},{... | collective-permute-start | bytes 1376264 | tf_op jit(solution)/shard_map/ppermute | solution.py:174
  53.2 1.5 %collective-permute-start.12 = (bf16[224,512]{1,0:T(8,128)(2,1)S(1)}, bf16[224,512]{1,0:T(8,128)(2,1)S(1)}, u32[]{:S(2)}, u32[]{:S(2)}) collective-permute-start(bf16[224,512]{1,0:T(8,128)(2,1)S(1)} %get-tuple-element.50.refs_1_), channel_id=1, source_target_pairs={{0,4},{4,0},{8,12},{12,8},{16,20},{20,16},{24,28},{28,24},{1,5},{5... | collective-permute-start | bytes 688136 | tf_op jit(solution)/shard_map/ppermute | solution.py:174
  53.2 1.8 %collective-permute-start.13 = (bf16[224,512]{1,0:T(8,128)(2,1)S(1)}, bf16[224,512]{1,0:T(8,128)(2,1)S(1)}, u32[]{:S(2)}, u32[]{:S(2)}) collective-permute-start(bf16[224,512]{1,0:T(8,128)(2,1)S(1)} %get-tuple-element.51), channel_id=1, source_target_pairs={{0,4},{4,0},{8,12},{12,8},{16,20},{20,16},{24,28},{28,24},{1,5},{5... | collective-permute-start | bytes 688136 | tf_op jit(solution)/shard_map/ppermute | solution.py:174
  53.7 8.0 %collective-permute-start.17 = (bf16[112,512]{1,0:T(8,128)(2,1)S(1)}, bf16[112,512]{1,0:T(8,128)(2,1)S(1)}, u32[]{:S(2)}, u32[]{:S(2)}) collective-permute-start(bf16[112,512]{1,0:T(8,128)(2,1)S(1)} %merge.4.refs_0_), channel_id=1, source_target_pairs={{0,2},{1,3},{2,0},{3,1},{4,6},{5,7},{6,4},{7,5},{8,10},{9,11},{10,... | collective-permute-start | bytes 344072 | tf_op jit(solution)/shard_map/ppermute | solution.py:174
  55.1 9.9 %collective-permute-start.15 = (bf16[224,512]{1,0:T(8,128)(2,1)S(1)}, bf16[224,512]{1,0:T(8,128)(2,1)S(1)}, u32[]{:S(2)}, u32[]{:S(2)}) collective-permute-start(bf16[224,512]{1,0:T(8,128)(2,1)S(1)} %get-tuple-element.52.refs_4_.mine), channel_id=1, source_target_pairs={{0,8},{4,12},{8,0},{12,4},{16,24},{20,28},{24,16},{28,20},{1,9},{5... | collective-permute-start | bytes 688136 | tf_op jit(solution)/shard_map/ppermute | solution.py:174
  56.7 10.1 %collective-permute-start.18 = (bf16[224,512]{1,0:T(8,128)(2,1)S(1)}, bf16[224,512]{1,0:T(8,128)(2,1)S(1)}, u32[]{:S(2)}, u32[]{:S(2)}) collective-permute-start(bf16[224,512]{1,0:T(8,128)(2,1)S(1)} %get-tuple-element.55.mine), channel_id=1, source_target_pairs={{0,16},{4,20},{8,24},{12,28},{16,0},{20,4},{24,8},{28,12},{1,17},{... | collective-permute-start | bytes 688136 | tf_op jit(solution)/shard_map/ppermute | solution.py:174
  64.5 3.9 %collective-permute-start.22 = (bf16[2,112,512]{2,1,0:T(8,128)(2,1)S(1)}, bf16[2,112,512]{2,1,0:T(8,128)(2,1)S(1)}, u32[]{:S(2)}, u32[]{:S(2)}) collective-permute-start(bf16[2,112,512]{2,1,0:T(8,128)(2,1)S(1)} %get-tuple-element.54.refs_1_.refs_0_), channel_id=1, source_target_pairs={{0,4},{4,0},{8,12},{12,8},{16,20},{20,16},{24,28},{28,24},{1,5},{5... | collective-permute-start | bytes 688136 | tf_op jit(solution)/shard_map/ppermute | solution.py:174
  64.5 3.9 %collective-permute-start.23 = (bf16[2,112,512]{2,1,0:T(8,128)(2,1)S(1)}, bf16[2,112,512]{2,1,0:T(8,128)(2,1)S(1)}, u32[]{:S(2)}, u32[]{:S(2)}) collective-permute-start(bf16[2,112,512]{2,1,0:T(8,128)(2,1)S(1)} %get-tuple-element.57.refs_1_), channel_id=1, source_target_pairs={{0,4},{4,0},{8,12},{12,8},{16,20},{20,16},{24,28},{28,24},{1,5},{5... | collective-permute-start | bytes 688136 | tf_op jit(solution)/shard_map/ppermute | solution.py:174
  65.1 9.1 %collective-permute-start.19 = (bf16[224,512]{1,0:T(8,128)(2,1)S(1)}, bf16[224,512]{1,0:T(8,128)(2,1)S(1)}, u32[]{:S(2)}, u32[]{:S(2)}) collective-permute-start(bf16[224,512]{1,0:T(8,128)(2,1)S(1)} %add.32.refs_1_.refs_0_), channel_id=1, source_target_pairs={{0,16},{4,20},{8,24},{12,28},{16,0},{20,4},{24,8},{28,12},{1,17},{... | collective-permute-start | bytes 688136 | tf_op jit(solution)/shard_map/ppermute | solution.py:174
  66.8 7.4 %collective-permute-start.20 = (bf16[224,512]{1,0:T(8,128)(2,1)S(1)}, bf16[224,512]{1,0:T(8,128)(2,1)S(1)}, u32[]{:S(2)}, u32[]{:S(2)}) collective-permute-start(bf16[224,512]{1,0:T(8,128)(2,1)S(1)} %add.33.refs_5_.refs_1_), channel_id=1, source_target_pairs={{0,8},{4,12},{8,0},{12,4},{16,24},{20,28},{24,16},{28,20},{1,9},{5... | collective-permute-start | bytes 688136 | tf_op jit(solution)/shard_map/ppermute | solution.py:174
  72.6 3.1 %collective-permute-start.27 = (bf16[224,512]{1,0:T(8,128)(2,1)S(1)}, bf16[224,512]{1,0:T(8,128)(2,1)S(1)}, u32[]{:S(2)}, u32[]{:S(2)}) collective-permute-start(bf16[224,512]{1,0:T(8,128)(2,1)S(1)} %get-tuple-element.58.refs_6_), channel_id=1, source_target_pairs={{0,4},{4,0},{8,12},{12,8},{16,20},{20,16},{24,28},{28,24},{1,5},{5... | collective-permute-start | bytes 688136 | tf_op jit(solution)/shard_map/ppermute | solution.py:174
  72.7 3.0 %collective-permute-start.28 = (bf16[224,512]{1,0:T(8,128)(2,1)S(1)}, bf16[224,512]{1,0:T(8,128)(2,1)S(1)}, u32[]{:S(2)}, u32[]{:S(2)}) collective-permute-start(bf16[224,512]{1,0:T(8,128)(2,1)S(1)} %get-tuple-element.61), channel_id=1, source_target_pairs={{0,4},{4,0},{8,12},{12,8},{16,20},{20,16},{24,28},{28,24},{1,5},{5... | collective-permute-start | bytes 688136 | tf_op jit(solution)/shard_map/ppermute | solution.py:174
  75.8 9.5 %collective-permute-start.30 = (bf16[224,512]{1,0:T(8,128)(2,1)S(1)}, bf16[224,512]{1,0:T(8,128)(2,1)S(1)}, u32[]{:S(2)}, u32[]{:S(2)}) collective-permute-start(bf16[224,512]{1,0:T(8,128)(2,1)S(1)} %get-tuple-element.63.mine.refs_1_), channel_id=1, source_target_pairs={{0,8},{4,12},{8,0},{12,4},{16,24},{20,28},{24,16},{28,20},{1,9},{5... | collective-permute-start | bytes 688136 | tf_op jit(solution)/shard_map/ppermute | solution.py:174
  77.4 8.0 %collective-permute-start.29 = (bf16[224,512]{1,0:T(8,128)(2,1)S(1)}, bf16[224,512]{1,0:T(8,128)(2,1)S(1)}, u32[]{:S(2)}, u32[]{:S(2)}) collective-permute-start(bf16[224,512]{1,0:T(8,128)(2,1)S(1)} %get-tuple-element.62.mine), channel_id=1, source_target_pairs={{0,16},{4,20},{8,24},{12,28},{16,0},{20,4},{24,8},{28,12},{1,17},{... | collective-permute-start | bytes 688136 | tf_op jit(solution)/shard_map/ppermute | solution.py:174
  77.9 7.4 %collective-permute-start.26 = (bf16[112,512]{1,0:T(8,128)(2,1)S(1)}, bf16[112,512]{1,0:T(8,128)(2,1)S(1)}, u32[]{:S(2)}, u32[]{:S(2)}) collective-permute-start(bf16[112,512]{1,0:T(8,128)(2,1)S(1)} %merge.5.refs_3_), channel_id=1, source_target_pairs={{0,2},{1,3},{2,0},{3,1},{4,6},{5,7},{6,4},{7,5},{8,10},{9,11},{10,... | collective-permute-start | bytes 344072 | tf_op jit(solution)/shard_map/ppermute | solution.py:174
  79.5 7.6 %collective-permute-start.24 = (bf16[2,112,512]{2,1,0:T(8,128)(2,1)S(1)}, bf16[2,112,512]{2,1,0:T(8,128)(2,1)S(1)}, u32[]{:S(2)}, u32[]{:S(2)}) collective-permute-start(bf16[2,112,512]{2,1,0:T(8,128)(2,1)S(1)} %get-tuple-element.59.refs_3_.refs_0_), channel_id=1, source_target_pairs={{0,4},{4,0},{8,12},{12,8},{16,20},{20,16},{24,28},{28,24},{1,5},{5... | collective-permute-start | bytes 688136 | tf_op jit(solution)/shard_map/ppermute | solution.py:174
  79.5 7.6 %collective-permute-start.25 = (bf16[2,112,512]{2,1,0:T(8,128)(2,1)S(1)}, bf16[2,112,512]{2,1,0:T(8,128)(2,1)S(1)}, u32[]{:S(2)}, u32[]{:S(2)}) collective-permute-start(bf16[2,112,512]{2,1,0:T(8,128)(2,1)S(1)} %get-tuple-element.60.refs_1_), channel_id=1, source_target_pairs={{0,4},{4,0},{8,12},{12,8},{16,20},{20,16},{24,28},{28,24},{1,5},{5... | collective-permute-start | bytes 688136 | tf_op jit(solution)/shard_map/ppermute | solution.py:174
  85.5 7.8 %collective-permute-start.33 = (bf16[224,512]{1,0:T(8,128)(2,1)S(1)}, bf16[224,512]{1,0:T(8,128)(2,1)S(1)}, u32[]{:S(2)}, u32[]{:S(2)}) collective-permute-start(bf16[224,512]{1,0:T(8,128)(2,1)S(1)} %add.36.refs_7_.refs_1_), channel_id=1, source_target_pairs={{0,8},{4,12},{8,0},{12,4},{16,24},{20,28},{24,16},{28,20},{1,9},{5... | collective-permute-start | bytes 688136 | tf_op jit(solution)/shard_map/ppermute | solution.py:174
  86.1 7.2 %collective-permute-start.32 = (bf16[224,512]{1,0:T(8,128)(2,1)S(1)}, bf16[224,512]{1,0:T(8,128)(2,1)S(1)}, u32[]{:S(2)}, u32[]{:S(2)}) collective-permute-start(bf16[224,512]{1,0:T(8,128)(2,1)S(1)} %add.35.refs_1_.refs_0_), channel_id=1, source_target_pairs={{0,16},{4,20},{8,24},{12,28},{16,0},{20,4},{24,8},{28,12},{1,17},{... | collective-permute-start | bytes 688136 | tf_op jit(solution)/shard_map/ppermute | solution.py:174
  88.4 4.9 %collective-permute-start.31 = (bf16[112,512]{1,0:T(8,128)(2,1)S(1)}, bf16[112,512]{1,0:T(8,128)(2,1)S(1)}, u32[]{:S(2)}, u32[]{:S(2)}) collective-permute-start(bf16[112,512]{1,0:T(8,128)(2,1)S(1)} %get-tuple-element.65.refs_6_), channel_id=1, source_target_pairs={{0,1},{1,0},{2,3},{3,2},{4,5},{5,4},{6,7},{7,6},{8,9},{9,8},{10,11... | collective-permute-start | bytes 344072 | tf_op jit(solution)/shard_map/ppermute | solution.py:174
  93.6 1.6 %collective-permute-start.34 = (bf16[2,112,512]{2,1,0:T(8,128)(2,1)S(1)}, bf16[2,112,512]{2,1,0:T(8,128)(2,1)S(1)}, u32[]{:S(2)}, u32[]{:S(2)}) collective-permute-start(bf16[2,112,512]{2,1,0:T(8,128)(2,1)S(1)} %get-tuple-element.67.refs_0_.refs_3_), channel_id=1, source_target_pairs={{0,4},{4,0},{8,12},{12,8},{16,20},{20,16},{24,28},{28,24},{1,5},{5... | collective-permute-start | bytes 688136 | tf_op jit(solution)/shard_map/ppermute | solution.py:174
  93.7 1.8 %collective-permute-start.35 = (bf16[2,112,512]{2,1,0:T(8,128)(2,1)S(1)}, bf16[2,112,512]{2,1,0:T(8,128)(2,1)S(1)}, u32[]{:S(2)}, u32[]{:S(2)}) collective-permute-start(bf16[2,112,512]{2,1,0:T(8,128)(2,1)S(1)} %get-tuple-element.68.refs_1_), channel_id=1, source_target_pairs={{0,4},{4,0},{8,12},{12,8},{16,20},{20,16},{24,28},{28,24},{1,5},{5... | collective-permute-start | bytes 688136 | tf_op jit(solution)/shard_map/ppermute | solution.py:174
  95.2 8.6 %copy-start.3 = (bf16[512,512]{1,0:T(8,128)(2,1)S(1)}, bf16[512,512]{1,0:T(8,128)(2,1)}, u32[]{:S(2)}) copy-start(bf16[512,512]{1,0:T(8,128)(2,1)} %refs_2_.7) | copy-start | bytes 1572868
  96.5 7.2 %collective-permute-start.36 = (bf16[112,512]{1,0:T(8,128)(2,1)S(1)}, bf16[112,512]{1,0:T(8,128)(2,1)S(1)}, u32[]{:S(2)}, u32[]{:S(2)}) collective-permute-start(bf16[112,512]{1,0:T(8,128)(2,1)S(1)} %get-tuple-element.69.refs_1_), channel_id=1, source_target_pairs={{0,1},{1,0},{2,3},{3,2},{4,5},{5,4},{6,7},{7,6},{8,9},{9,8},{10,11... | collective-permute-start | bytes 344072 | tf_op jit(solution)/shard_map/ppermute | solution.py:174
  96.6 8.7 %collective-permute-start.37 = (bf16[112,512]{1,0:T(8,128)(2,1)S(1)}, bf16[112,512]{1,0:T(8,128)(2,1)S(1)}, u32[]{:S(2)}, u32[]{:S(2)}) collective-permute-start(bf16[112,512]{1,0:T(8,128)(2,1)S(1)} %add.37.refs_1_.refs_0_), channel_id=1, source_target_pairs={{0,2},{1,3},{2,0},{3,1},{4,6},{5,7},{6,4},{7,5},{8,10},{9,11},{10,... | collective-permute-start | bytes 344072 | tf_op jit(solution)/shard_map/ppermute | solution.py:174
  103.7 6.9 %collective-permute-start.38 = (bf16[112,512]{1,0:T(8,128)(2,1)S(1)}, bf16[112,512]{1,0:T(8,128)(2,1)S(1)}, u32[]{:S(2)}, u32[]{:S(2)}) collective-permute-start(bf16[112,512]{1,0:T(8,128)(2,1)S(1)} %add.38.refs_1_.refs_3_), channel_id=1, source_target_pairs={{0,2},{1,3},{2,0},{3,1},{4,6},{5,7},{6,4},{7,5},{8,10},{9,11},{10,... | collective-permute-start | bytes 344072 | tf_op jit(solution)/shard_map/ppermute | solution.py:174
